TPU v7x, 32 devices: a whole 2x2x4 slice. The times are simulated.
32 devices in a mesh: win: 16 (over z, x, core), mlp: 2 (over y).
Axes of the slice: x: 2, y: 2, z: 4, core: 2. Of those that a mesh axis runs over, the one named last changes fastest.
Arguments:
- tokens: bfloat16 [32, 28, 28, 384], P(('win', 'mlp')), may hold values from -6 to 6
- crop_ids: int32 [32, 28, 28], P(('win', 'mlp')), may hold values from 0 to 3, as said below
- norm_gain: float32 [2, 2, 384], replicated, may hold values from 0.5 to 1.5
- norm_bias: float32 [2, 2, 384], replicated, may hold values from -2 to 2
- input_proj: bfloat16 [2, 384, 1152], replicated, may hold values from -0.3125 to 0.3125
- input_bias: float32 [2, 2, 384], replicated, may hold values from -3 to 3
- position_table: float32 [2, 169, 12], replicated, may hold values from -4 to 4
- output_proj: bfloat16 [2, 384, 384], replicated, may hold values from -1.25 to 1.25
- output_bias: float32 [2, 384], replicated, may hold values from -2 to 2
- expand_weight: bfloat16 [2, 384, 1536], P(None, None, 'mlp'), may hold values from -0.3125 to 0.3125
- expand_bias: bfloat16 [2, 1536], P(None, 'mlp'), may hold values from -3 to 3
- reduce_weight: bfloat16 [2, 1536, 384], P(None, 'mlp'), may hold values from -0.21875 to 0.21875
- reduce_bias: float32 [2, 384], replicated, may hold values from -2 to 2
- cotangent: bfloat16 [32, 28, 28, 384], P(('win', 'mlp')), may hold values from -6 to 6
Outputs:
- out: bfloat16 [32, 28, 28, 384], P(('win', 'mlp'))
- grad_tokens: bfloat16 [32, 28, 28, 384], P(('win', 'mlp'))
- grad_norm_gain: float32 [2, 2, 384], replicated
- grad_norm_bias: float32 [2, 2, 384], replicated
- grad_input_proj: float32 [2, 384, 1152], replicated
- grad_input_bias: float32 [2, 2, 384], replicated
- grad_position_table: float32 [2, 169, 12], replicated
- grad_output_proj: float32 [2, 384, 384], replicated
- grad_output_bias: float32 [2, 384], replicated
- grad_expand_weight: float32 [2, 384, 1536], P(None, None, 'mlp')
- grad_expand_bias: float32 [2, 1536], P(None, 'mlp')
- grad_reduce_weight: float32 [2, 1536, 384], P(None, 'mlp')
- grad_reduce_bias: float32 [2, 384], replicated
Inputs may be any that keep to these rules, and one draw needn't show every extreme that they name: `crop_ids`: in each canvas one row cut and one column cut split the slots into four rectangles, each non-empty, carrying the ids 0, 1, 2, 3 in a drawn order; 0 marks empty slots.
All inputs are finite; a program needn't handle non-finite values.
Results may differ from a plain program's by a relative error of at most 0.02.
Values may be sent and summed in bfloat16 or wider, within the bound.
A program may use at most 256 MiB of HBM per device.

v0:
```python
from functools import partial

import jax
import jax.numpy as jnp
from jax import lax
from jax.sharding import PartitionSpec as P

HEADS = 12
HEAD_DIM = 32
WIN = 7
SHIFT = 3


epsilon = 1e-05
masked_score = -1e30


def layer_norm(values, gain, offset):
    centre = jnp.mean(values, axis=-1, keepdims=True)
    centred = values - centre
    variance = jnp.mean(centred * centred, axis=-1, keepdims=True)
    return centred * lax.rsqrt(variance + epsilon) * gain + offset


def norm_backward(values, gain, offset, upstream):
    result, pullback = jax.vjp(layer_norm, values, gain, offset)
    return pullback(upstream)


def relative_index():
    coords = jnp.arange(WIN * WIN, dtype=jnp.int32)
    row_pos = coords // WIN
    col_pos = coords % WIN
    delta_row = row_pos[:, None] - row_pos[None, :] + WIN - 1
    delta_col = col_pos[:, None] - col_pos[None, :] + WIN - 1
    return delta_row * (2 * WIN - 1) + delta_col


def to_windows(grid_vals):
    canvas_count, side_len = (grid_vals.shape[0], grid_vals.shape[1])
    per_side = side_len // WIN
    tail_shape = grid_vals.shape[3:]
    shaped = grid_vals.reshape((canvas_count, per_side, WIN, per_side, WIN) + tail_shape)
    shaped = jnp.swapaxes(shaped, 2, 3)
    return shaped.reshape((canvas_count, per_side * per_side, WIN * WIN) + tail_shape)


def from_windows(windows, side_len):
    per_side = side_len // WIN
    tail_shape = windows.shape[3:]
    shaped = windows.reshape((windows.shape[0], per_side, per_side, WIN, WIN) + tail_shape)
    shaped = jnp.swapaxes(shaped, 2, 3)
    return shaped.reshape((windows.shape[0], side_len, side_len) + tail_shape)


def window_keys(crop_ids, shifted):
    if shifted:
        side_len = crop_ids.shape[1]
        places = jnp.arange(side_len, dtype=jnp.int32)
        labels = (places >= side_len - WIN).astype(jnp.int32) + (places >= side_len - SHIFT).astype(
            jnp.int32
        )
        region = labels[:, None] * 3 + labels[None, :]
        rolled = jnp.roll(crop_ids, (-SHIFT, -SHIFT), axis=(1, 2))
        return to_windows(rolled * 9 + region[None])
    return to_windows(crop_ids * 9)


def rows_to_windows(rows_in, side_len, shifted):
    grid_vals = rows_in.reshape((-1, side_len, side_len, rows_in.shape[-1]))
    if shifted:
        grid_vals = jnp.roll(grid_vals, (-SHIFT, -SHIFT), axis=(1, 2))
    return to_windows(grid_vals)


def windows_to_rows(windows, side_len, shifted):
    grid_vals = from_windows(windows, side_len)
    if shifted:
        grid_vals = jnp.roll(grid_vals, (SHIFT, SHIFT), axis=(1, 2))
    return grid_vals.reshape((-1, grid_vals.shape[-1]))


def head_bias(onehot, table_vals):
    flat_bias = jnp.dot(onehot, table_vals, precision=lax.Precision.HIGHEST)
    return jnp.transpose(flat_bias.reshape(WIN * WIN, WIN * WIN, -1), (2, 0, 1))


def make_qkv(normed, weight, bias_pair, side_len, shifted):
    bias_full = jnp.concatenate([bias_pair[0], jnp.zeros_like(bias_pair[0]), bias_pair[1]])
    qkv_rows = (jnp.dot(normed, weight, preferred_element_type=jnp.float32) + bias_full).astype(
        jnp.bfloat16
    )
    return rows_to_windows(qkv_rows, side_len, shifted)


def masked_scores(qkv_win, key_win, bias_heads):
    win_count = qkv_win.shape[0]
    heads_split = qkv_win.reshape(win_count, WIN * WIN, 3, HEADS, HEAD_DIM)
    queries = heads_split[:, :, 0]
    key_rows = heads_split[:, :, 1]
    value_rows = heads_split[:, :, 2]
    scores = (
        jnp.einsum("wqhd,wkhd->whqk", queries, key_rows, preferred_element_type=jnp.float32)
        * HEAD_DIM ** (-0.5)
        + bias_heads[None]
    )
    allowed = key_win[:, None, :, None] == key_win[:, None, None, :]
    return (jnp.where(allowed, scores, masked_score), queries, key_rows, value_rows)


def attend_forward(qkv_win, key_win, bias_heads):
    win_count = qkv_win.shape[0]
    scores, queries, key_rows, value_rows = masked_scores(qkv_win, key_win, bias_heads)
    row_top = jnp.max(scores, axis=-1, keepdims=True)
    expd_vals = jnp.exp(scores - row_top)
    row_total = jnp.sum(expd_vals, axis=-1, keepdims=True)
    attn_probs = (expd_vals / row_total).astype(jnp.bfloat16)
    attended = jnp.einsum(
        "whqk,wkhd->wqhd", attn_probs, value_rows, preferred_element_type=jnp.float32
    )
    log_norm = row_top + jnp.log(row_total)
    return (attended.reshape(win_count, WIN * WIN, HEADS * HEAD_DIM), log_norm)


def attend_backward(qkv_win, key_win, bias_heads, log_norm, grad_win):
    win_count = qkv_win.shape[0]
    scores, queries, key_rows, value_rows = masked_scores(qkv_win, key_win, bias_heads)
    prob_full = jnp.exp(scores - log_norm)
    grad_rows = grad_win.reshape(win_count, WIN * WIN, HEADS, HEAD_DIM)
    grad_probs = jnp.einsum(
        "wqhd,wkhd->whqk", grad_rows, value_rows, preferred_element_type=jnp.float32
    )
    grad_scores = prob_full * (grad_probs - jnp.sum(prob_full * grad_probs, axis=-1, keepdims=True))
    grad_low = grad_scores.astype(jnp.bfloat16)
    scale_factor = HEAD_DIM ** (-0.5)
    grad_query = (
        jnp.einsum("whqk,wkhd->wqhd", grad_low, key_rows, preferred_element_type=jnp.float32)
        * scale_factor
    )
    grad_key = (
        jnp.einsum("whqk,wqhd->wkhd", grad_low, queries, preferred_element_type=jnp.float32)
        * scale_factor
    )
    grad_value = jnp.einsum(
        "whqk,wqhd->wkhd",
        prob_full.astype(jnp.bfloat16),
        grad_rows,
        preferred_element_type=jnp.float32,
    )
    stacked = jnp.stack([grad_query, grad_key, grad_value], axis=2).reshape(
        win_count, WIN * WIN, 3 * HEADS * HEAD_DIM
    )
    bias_grad = jnp.sum(grad_low.astype(jnp.float32), axis=0)
    return (stacked, bias_grad)


def on_device(
    tokens,
    crop_ids,
    norm_gain,
    norm_bias,
    input_proj,
    input_bias,
    position_table,
    output_proj,
    output_bias,
    expand_weight,
    expand_bias,
    reduce_weight,
    reduce_bias,
    cotangent,
):
    canvas_count, side_len, width = (tokens.shape[0], tokens.shape[1], tokens.shape[3])
    row_count = canvas_count * side_len * side_len
    span_count = position_table.shape[1]
    onehot = (
        relative_index().reshape(-1)[:, None] == jnp.arange(span_count, dtype=jnp.int32)[None, :]
    ).astype(jnp.float32)
    expand_all, expand_bias_all, reduce_all = (expand_weight, expand_bias, reduce_weight)
    field_now = tokens.astype(jnp.float32).reshape(row_count, width)
    saved = []
    for layer_idx in range(2):
        shifted = layer_idx == 1
        key_win = window_keys(crop_ids, shifted)
        bias_heads = head_bias(onehot, position_table[layer_idx])
        normed = layer_norm(field_now, norm_gain[layer_idx, 0], norm_bias[layer_idx, 0]).astype(
            jnp.bfloat16
        )
        qkv_win = make_qkv(normed, input_proj[layer_idx], input_bias[layer_idx], side_len, shifted)
        mixed_win, log_norm = lax.map(
            lambda bundle: attend_forward(bundle[0], bundle[1], bias_heads), (qkv_win, key_win)
        )
        mixed_rows = windows_to_rows(mixed_win, side_len, shifted).astype(jnp.bfloat16)
        middle = (
            field_now
            + jnp.dot(mixed_rows, output_proj[layer_idx], preferred_element_type=jnp.float32)
            + output_bias[layer_idx]
        )
        second = layer_norm(middle, norm_gain[layer_idx, 1], norm_bias[layer_idx, 1]).astype(
            jnp.bfloat16
        )
        gathered = lax.all_gather(second, "mlp", axis=0, tiled=True)
        before = jnp.dot(
            gathered, expand_all[layer_idx], preferred_element_type=jnp.float32
        ) + expand_bias_all[layer_idx].astype(jnp.float32)
        hidden = jax.nn.gelu(before, approximate=False).astype(jnp.bfloat16)
        reduce_now = reduce_all[layer_idx]
        reduced = lax.psum_scatter(
            jnp.dot(hidden, reduce_now, preferred_element_type=jnp.float32).astype(jnp.bfloat16),
            "mlp",
            scatter_dimension=0,
            tiled=True,
        ).astype(jnp.float32)
        saved.append((field_now, log_norm, mixed_rows, middle, gathered, before))
        field_now = middle + reduced + reduce_bias[layer_idx]
    grad_now = cotangent.astype(jnp.float32).reshape(row_count, width)
    layer_results = [None, None]
    mlp_results = [None, None]
    for layer_idx in (1, 0):
        shifted = layer_idx == 1
        field_in, log_norm, mixed_rows, middle, gathered, before = saved[layer_idx]
        grad_reduce_bias = jnp.sum(grad_now, axis=0)
        grad_out_low = grad_now.astype(jnp.bfloat16)
        hidden_vals, gelu_back = jax.vjp(partial(jax.nn.gelu, approximate=False), before)
        hidden = hidden_vals.astype(jnp.bfloat16)
        grad_gathered = lax.all_gather(grad_out_low, "mlp", axis=0, tiled=True)
        grad_reduce = jnp.einsum(
            "rf,rc->fc", hidden, grad_gathered, preferred_element_type=jnp.float32
        )
        grad_hidden = jnp.einsum(
            "rc,fc->rf", grad_gathered, reduce_all[layer_idx], preferred_element_type=jnp.float32
        )
        grad_before = gelu_back(grad_hidden)[0]
        grad_expand_bias = jnp.sum(grad_before, axis=0)
        grad_before_low = grad_before.astype(jnp.bfloat16)
        grad_expand = jnp.einsum(
            "rc,rf->cf", gathered, grad_before_low, preferred_element_type=jnp.float32
        )
        expand_now = expand_all[layer_idx]
        grad_second = lax.psum_scatter(
            jnp.einsum(
                "rf,cf->rc", grad_before_low, expand_now, preferred_element_type=jnp.float32
            ).astype(jnp.bfloat16),
            "mlp",
            scatter_dimension=0,
            tiled=True,
        ).astype(jnp.float32)
        grad_mid_part, gain_two, offset_two = norm_backward(
            middle, norm_gain[layer_idx, 1], norm_bias[layer_idx, 1], grad_second
        )
        grad_middle = grad_now + grad_mid_part
        grad_output_bias = jnp.sum(grad_middle, axis=0)
        grad_mid_low = grad_middle.astype(jnp.bfloat16)
        grad_output_proj = jnp.einsum(
            "rc,rd->cd", mixed_rows, grad_mid_low, preferred_element_type=jnp.float32
        )
        grad_mixed = jnp.einsum(
            "rd,cd->rc", grad_mid_low, output_proj[layer_idx], preferred_element_type=jnp.float32
        ).astype(jnp.bfloat16)
        key_win = window_keys(crop_ids, shifted)
        bias_heads = head_bias(onehot, position_table[layer_idx])
        normed = layer_norm(field_in, norm_gain[layer_idx, 0], norm_bias[layer_idx, 0]).astype(
            jnp.bfloat16
        )
        qkv_win = make_qkv(normed, input_proj[layer_idx], input_bias[layer_idx], side_len, shifted)
        grad_win = rows_to_windows(grad_mixed, side_len, shifted)
        grad_qkv_win, bias_parts = lax.map(
            lambda bundle: attend_backward(bundle[0], bundle[1], bias_heads, bundle[2], bundle[3]),
            (qkv_win, key_win, log_norm, grad_win),
        )
        grad_qkv = windows_to_rows(grad_qkv_win, side_len, shifted)
        grad_input_bias = jnp.stack(
            [jnp.sum(grad_qkv[:, :width], axis=0), jnp.sum(grad_qkv[:, 2 * width :], axis=0)]
        )
        grad_qkv_low = grad_qkv.astype(jnp.bfloat16)
        grad_input_proj = jnp.einsum(
            "rc,rk->ck", normed, grad_qkv_low, preferred_element_type=jnp.float32
        )
        grad_normed = jnp.einsum(
            "rk,ck->rc", grad_qkv_low, input_proj[layer_idx], preferred_element_type=jnp.float32
        )
        grad_in_part, gain_one, offset_one = norm_backward(
            field_in, norm_gain[layer_idx, 0], norm_bias[layer_idx, 0], grad_normed
        )
        bias_total = jnp.sum(bias_parts, axis=0).reshape(HEADS, -1)
        grad_table = jnp.einsum("pt,hp->th", onehot, bias_total, precision=lax.Precision.HIGHEST)
        grad_now = grad_middle + grad_in_part
        gain_pair = jnp.stack([gain_one, gain_two])
        offset_pair = jnp.stack([offset_one, offset_two])
        layer_results[layer_idx] = lax.psum(
            (
                gain_pair,
                offset_pair,
                grad_input_proj,
                grad_input_bias,
                grad_table,
                grad_output_proj,
                grad_output_bias,
                grad_reduce_bias,
            ),
            ("win", "mlp"),
        )
        mlp_results[layer_idx] = (grad_expand, grad_expand_bias, grad_reduce)
    stacked = tuple(
        (
            jnp.stack([layer_results[0][member_idx], layer_results[1][member_idx]])
            for member_idx in range(8)
        )
    )
    expand_grads = jnp.stack([mlp_results[0][0], mlp_results[1][0]])
    expand_bias_grads = jnp.stack([mlp_results[0][1], mlp_results[1][1]])
    reduce_grads = jnp.stack([mlp_results[0][2], mlp_results[1][2]])
    expand_grads, expand_bias_grads, reduce_grads = (
        lax.psum(expand_grads.astype(jnp.bfloat16), "win").astype(jnp.float32),
        lax.psum(expand_bias_grads.astype(jnp.bfloat16), "win").astype(jnp.float32),
        lax.psum(reduce_grads.astype(jnp.bfloat16), "win").astype(jnp.float32),
    )
    out = field_now.astype(jnp.bfloat16).reshape(tokens.shape)
    grad_tokens = grad_now.astype(jnp.bfloat16).reshape(tokens.shape)
    return (
        out,
        grad_tokens,
        stacked[0],
        stacked[1],
        stacked[2],
        stacked[3],
        stacked[4],
        stacked[5],
        stacked[6],
        expand_grads,
        expand_bias_grads,
        reduce_grads,
        stacked[7],
    )


def solution(mesh):
    placed = (
        P(("win", "mlp"), None, None, None),
        P(("win", "mlp"), None, None),
        P(),
        P(),
        P(),
        P(),
        P(),
        P(),
        P(),
        P(None, None, "mlp"),
        P(None, "mlp"),
        P(None, "mlp", None),
        P(),
        P(("win", "mlp"), None, None, None),
    )
    return jax.shard_map(
        on_device,
        mesh=mesh,
        in_specs=placed,
        out_specs=(
            P(("win", "mlp"), None, None, None),
            P(("win", "mlp"), None, None, None),
            P(),
            P(),
            P(),
            P(),
            P(),
            P(),
            P(),
            P(None, None, "mlp"),
            P(None, "mlp"),
            P(None, "mlp", None),
            P(),
        ),
        check_vma=False,
    )
```

profile of v0, /device:TPU:0, one launch (start us, length us, event | category | flops | bytes accessed | tf_op | source)
XLA Modules:
  0.0 873.7 jit_solution(9327689435185476410)
XLA Ops:
  25.6 11.7 %reshape.668 = bf16[16,49,3,12,32]{4,3,2,0,1:T(8,128)(2,1)} reshape(bf16[1,4,4,7,7,1152]{5,2,1,4,3,0:T(4,128)(2,1)} %copy.156) | data formatting | bytes 3612672 | tf_op jit(solution)/shard_map/while/body/eval_jaxpr/reshape | solution.py:98
  37.3 7.4 fusion.158
  44.7 3.8 copy.207
  48.5 4.5 copy.208
  53.1 5.3 copy.209
  66.7 6.8 copy.164
  73.5 2.9 convert_element_type.239
  81.5 25.8 %all-gather.5.cloned.1.call-done = bf16[1568,384]{1,0:T(8,128)(2,1)} async-done(((bf16[784,384]{1,0:T(8,128)(2,1)}), bf16[1568,384]{1,0:T(8,128)(2,1)}) %all-gather.5.cloned.1.call-update) | async-done | bytes 1204240 | tf_op jit(solution)/shard_map/all_gather | solution.py:202
  107.3 14.6 %multiply_convert_fusion.3 = (bf16[1568,768]{1,0:T(8,128)(2,1)S(1)}, f32[1568,768]{1,0:T(8,128)}, f32[1568,768]{1,0:T(8,128)}) fusion(f32[768]{0:T(1024)S(1)} %get-tuple-element.195, bf16[1568,384]{1,0:T(8,128)(2,1)} %all-gather.5.cloned.1.call-done, bf16[2,384,768]{2,1,0:T(8,128)(2,1)} %param.23), kind=kOutput, calls=%fused_computation.37 | convolution fusion | flops 1004322816 | bytes 13839360 | tf_op jit(solution)/shard_map/dot_general | solution.py:203
  128.9 19.1 %reduce-scatter.5.cloned.1.call-done = bf16[784,384]{1,0:T(8,128)(2,1)} async-done(((bf16[1568,384]{1,0:T(8,128)(2,1)}), bf16[784,384]{1,0:T(8,128)(2,1)}) %reduce-scatter.5.cloned.1.call-update) | async-done | bytes 602128 | tf_op jit(solution)/shard_map/reduce_scatter | solution.py:208
  153.6 3.9 reshape.670
  162.3 3.9 reshape.671
  166.1 3.5 copy.166
  169.6 11.7 %reshape.672 = bf16[16,49,3,12,32]{4,3,2,0,1:T(8,128)(2,1)} reshape(bf16[1,4,4,7,7,1152]{5,2,1,4,3,0:T(4,128)(2,1)} %copy.166) | data formatting | bytes 3612672 | tf_op jit(solution)/shard_map/while/body/eval_jaxpr/reshape | solution.py:98
  181.4 8.4 fusion.157
  189.8 5.4 copy.211
  195.2 5.4 copy.212
  200.5 5.4 copy.213
  205.9 3.7 fusion.162
  214.6 7.3 copy.174
  221.9 4.3 reshape.673
  228.4 4.1 fusion.91
  240.5 18.8 %all-gather.7.cloned.1.call-done = bf16[1568,384]{1,0:T(8,128)(2,1)} async-done(((bf16[784,384]{1,0:T(8,128)(2,1)}), bf16[1568,384]{1,0:T(8,128)(2,1)}) %all-gather.7.cloned.1.call-update) | async-done | bytes 1204240 | tf_op jit(solution)/shard_map/all_gather | solution.py:202
  259.2 14.9 %multiply_convert_fusion.2 = (bf16[1568,768]{1,0:T(8,128)(2,1)}, f32[1568,768]{1,0:T(8,128)}, f32[1568,768]{1,0:T(8,128)}) fusion(f32[768]{0:T(1024)S(1)} %get-tuple-element.194, bf16[1568,384]{1,0:T(8,128)(2,1)} %all-gather.7.cloned.1.call-done, bf16[2,384,768]{2,1,0:T(8,128)(2,1)} %param.23), kind=kOutput, calls=%fused_computation.24 | convolution fusion | flops 1004322816 | bytes 13839360 | tf_op jit(solution)/shard_map/dot_general | solution.py:203
  274.2 10.1 %all-gather.9.cloned.1.call-done = bf16[1568,384]{1,0:T(8,128)(2,1)} async-done(((bf16[784,384]{1,0:T(8,128)(2,1)}), bf16[1568,384]{1,0:T(8,128)(2,1)}) %all-gather.9.cloned.1.call-update) | async-done | bytes 1204240 | tf_op jit(solution)/shard_map/all_gather | solution.py:226
  284.3 7.1 fusion.164
  295.5 4.3 convolution_convert_fusion.2
  299.8 17.7 %reduce-scatter.9.cloned.1.call-done = bf16[784,384]{1,0:T(8,128)(2,1)} async-done(((bf16[1568,384]{1,0:T(8,128)(2,1)}), bf16[784,384]{1,0:T(8,128)(2,1)}) %reduce-scatter.9.cloned.1.call-update) | async-done | bytes 602128 | tf_op jit(solution)/shard_map/reduce_scatter | solution.py:240
  320.9 20.8 %reduce-scatter.7.cloned.1.call-done = bf16[784,384]{1,0:T(8,128)(2,1)} async-done(((bf16[1568,384]{1,0:T(8,128)(2,1)}), bf16[784,384]{1,0:T(8,128)(2,1)}) %reduce-scatter.7.cloned.1.call-update) | async-done | bytes 602128 | tf_op jit(solution)/shard_map/reduce_scatter | solution.py:208
  347.0 3.4 reshape.679
  350.4 5.6 copy.177
  356.1 6.4 fusion.36
  370.5 4.9 pad_maximum_fusion
  375.4 19.6 %copy.182 = f32[16,49,3,12,32]{4,3,2,0,1:T(8,128)} copy(f32[16,49,3,12,32]{1,4,3,0,2:T(8,128)} %pad_maximum_fusion) | data formatting | bytes 7225344 | tf_op jit(solution)/shard_map/while/body/eval_jaxpr/stack | solution.py:150
  395.0 14.3 %reshape.680 = f32[1,4,4,7,7,1152]{5,2,1,4,3,0:T(4,128)} reshape(f32[16,49,3,12,32]{4,3,2,0,1:T(8,128)} %copy.182) | data formatting | bytes 7225344 | tf_op jit(solution)/shard_map/reshape | solution.py:51
  409.2 5.7 copy.183
  417.3 23.7 %fusion.150 = (f32[28,28,1152]{2,1,0:T(8,128)}, bf16[1,28,28,1152]{3,0,2,1:T(2,128)(2,1)S(1)}) fusion(f32[1,25,28,1152]{3,0,2,1:T(1,128)S(1)} %slice.333, f32[1,3,28,1152]{3,0,2,1:T(1,128)S(1)} %slice.332), kind=kLoop, calls=%fused_computation.316 | loop fusion | flops 3612672 | bytes 9031680 | tf_op jit(solution)/shard_map/jit(_roll_static)/concatenate | solution.py:79
  441.0 11.7 %convert_reduce_fusion.2 = bf16[28,28,1152]{2,1,0:T(8,128)(2,1)} fusion(bf16[1,28,28,1152]{3,0,2,1:T(2,128)(2,1)S(1)} %get-tuple-element.227), kind=kLoop, calls=%fused_computation.59 | loop fusion | bytes 3612672 | tf_op jit(solution)/shard_map/convert_element_type | solution.py:275
  452.7 4.1 convert_element_type.268
  456.8 3.2 multiply_reduce_fusion.3
  463.6 4.3 fusion.70
  469.5 17.2 %all-gather.11.cloned.1.call-done = bf16[1568,384]{1,0:T(8,128)(2,1)} async-done(((bf16[784,384]{1,0:T(8,128)(2,1)}), bf16[1568,384]{1,0:T(8,128)(2,1)}) %all-gather.11.cloned.1.call-update) | async-done | bytes 1204240 | tf_op jit(solution)/shard_map/all_gather | solution.py:226
  486.7 7.1 fusion.165
  500.3 4.3 convolution_convert_fusion
  508.9 4.8 reshape.693
  520.8 33.6 %psum.148 = bf16[2,768]{1,0:T(2,128)(2,1)S(1)} all-reduce(bf16[2,768]{1,0:T(2,128)(2,1)S(1)} %pad_maximum_fusion.19), channel_id=1, replica_groups=mesh['win'=16,'mlp'=2] {'win'}, use_global_device_ids=true, to_apply=%region_59.60 | all-reduce | flops 1536 | bytes 6144 | tf_op jit(solution)/shard_map/psum | solution.py:315
  555.0 44.5 %all-reduce.8.cloned.1.call-done = (bf16[2,384,768]{2,1,0:T(8,128)(2,1)}, bf16[2,768,384]{2,1,0:T(8,128)(2,1)}) async-done(((bf16[2,384,768]{2,1,0:T(8,128)(2,1)}, bf16[2,768,384]{2,1,0:T(8,128)(2,1)}), (bf16[2,384,768]{2,1,0:T(8,128)(2,1)}, bf16[2,768,384]{2,1,0:T(8,128)(2,1)})) %all-reduce.8.cloned.1.call-update) | async-done | bytes 2359312 | tf_op jit(solution)/shard_map/psum | solution.py:314
  599.5 2.9 convert_element_type.283
  604.0 19.2 %reduce-scatter.11.cloned.1.call-done = bf16[784,384]{1,0:T(8,128)(2,1)} async-done(((bf16[1568,384]{1,0:T(8,128)(2,1)}), bf16[784,384]{1,0:T(8,128)(2,1)}) %reduce-scatter.11.cloned.1.call-update) | async-done | bytes 602128 | tf_op jit(solution)/shard_map/reduce_scatter | solution.py:240
  630.3 3.4 reshape.682
  633.6 5.7 copy.185
  639.4 6.4 fusion.39
  649.8 3.2 multiply_bitcast_fusion
  656.0 9.5 %pad_maximum_fusion.1 = f32[16,49,3,12,32]{1,4,3,0,2:T(8,128)} fusion(f32[16,49,1,12,32]{1,4,3,0,2:T(8,128)} %fusion.39, f32[16,49,1,12,32]{1,4,3,0,2:T(8,128)} %multiply_bitcast_fusion, f32[16,49,1,12,32]{1,4,3,0,2:T(8,128)} %multiply_bitcast_fusion.1), kind=kLoop, calls=%fused_computation.1 | loop fusion | flops 1806336 | bytes 7225344 | tf_op jit(solution)/shard_map/while/body/eval_jaxpr/stack | solution.py:150
  665.5 19.6 %copy.190 = f32[16,49,3,12,32]{4,3,2,0,1:T(8,128)} copy(f32[16,49,3,12,32]{1,4,3,0,2:T(8,128)} %pad_maximum_fusion.1) | data formatting | bytes 7225344 | tf_op jit(solution)/shard_map/while/body/eval_jaxpr/stack | solution.py:150
  685.1 14.1 %reshape.683 = f32[1,4,4,7,7,1152]{5,2,1,4,3,0:T(4,128)} reshape(f32[16,49,3,12,32]{4,3,2,0,1:T(8,128)} %copy.190) | data formatting | bytes 7225344 | tf_op jit(solution)/shard_map/reshape | solution.py:51
  703.5 4.1 convert_element_type.278
  707.6 4.0 convolution_bitcast_fusion.1
  711.6 4.1 multiply_reduce_fusion.4
  718.7 5.3 copy.192
  724.0 4.8 reshape_reshape.13
  731.6 40.3 %all-reduce = (f32[1,2,384]{2,1,0:T(2,128)S(1)}, f32[1,2,384]{2,1,0:T(2,128)S(1)}, f32[1,2,384]{2,1,0:T(2,128)S(1)}, f32[1,2,384]{2,1,0:T(2,128)S(1)}, f32[1,2,3...) all-reduce(f32[1,2,384]{2,1,0:T(2,128)S(1)} %maximum_bitcast_fusion, ...), channel_id=1, replica_groups=mesh['win'=16,'mlp'=2] {'win','mlp'}, use_global_device_ids=true, to_apply=%region_31.32 | all-reduce | flops 10200 | bytes 81600 | tf_op jit(solution)/shard_map/psum | solution.py:290
  775.6 85.6 %all-reduce.6.cloned.1.call-done = (f32[1,384,1152]{2,1,0:T(8,128)}, f32[1,384,1152]{2,1,0:T(8,128)}, f32[1,384,384]{2,1,0:T(8,128)}, f32[1,384,384]{2,1,0:T(8,128)}) async-done(((f32[1,384,1152]{2,1,0:T(8,128)}, f32[1,384,1152]{2,1,0:T(8,128)}, f32[1,384,384]{2,1,0:T(8,128)}, f32[1,384,384]{2,1,0:T(8,128)}), (f32[1,384,1152]{2,1,0:T(8,128)}, f32[1,384,1152]{2,1,0:T(8,128)}, f32[1,384,384]{2,1,0:T(8,128)}, ...) | async-done | bytes 4718608 | tf_op jit(solution)/shard_map/psum | solution.py:290
  861.2 4.1 pad_maximum_fusion.4
  (408 shorter events, 140.1 us)
Async XLA Ops:
  7.2 4.4 copy-start.16
  7.2 4.3 copy-start.83
  7.2 4.3 copy-start.58
  7.2 5.5 copy-start.69
  7.2 100.1 %all-gather.5.cloned.1.call-start = ((), (), s32[]{:S(2)}) async-start(), calls=%async_computation.4 | async-start | bytes 1806336 | tf_op jit(solution)/shard_map/all_gather | solution.py:202
  8.7 7.9 copy-start.84
  8.7 7.9 copy-start.85
  11.6 6.2 copy-start.46
  13.3 5.3 copy-start.90
  53.1 8.2 copy-start.7
  73.5 4.4 copy-start.82
  79.9 68.2 %copy-start.2 = (f32[784,384]{1,0:T(8,128)}, f32[784,384]{1,0:T(8,128)S(1)}, u32[]{:S(2)}) copy-start(f32[784,384]{1,0:T(8,128)S(1)} %get-tuple-element.254) | copy-start | bytes 3612676
  79.9 42.0 %copy-start.48 = (f32[784]{0:T(1024)}, f32[784]{0:T(1024)S(1)}, u32[]{:S(2)}) copy-start(f32[784]{0:T(1024)S(1)} %broadcast_multiply_fusion.3) | copy-start | bytes 9412
  80.2 41.7 %copy-start.63 = (f32[784]{0:T(1024)}, f32[784]{0:T(1024)S(1)}, u32[]{:S(2)}) copy-start(f32[784]{0:T(1024)S(1)} %multiply_reduce_fusion.9) | copy-start | bytes 9412
  80.3 41.7 %copy-start.54 = (f32[784]{0:T(1024)}, f32[784]{0:T(1024)S(1)}, u32[]{:S(2)}) copy-start(f32[784]{0:T(1024)S(1)} %fusion.139) | copy-start | bytes 9412
  81.4 66.6 %reduce-scatter.5.cloned.1.call-start = ((), (), s32[]{:S(2)}) async-start(), calls=%async_computation.5 | async-start | bytes 1806336 | tf_op jit(solution)/shard_map/reduce_scatter | solution.py:208
  81.5 40.4 %copy-start.86 = (f32[768]{0:T(1024)}, f32[768]{0:T(1024)S(1)}, u32[]{:S(2)}) copy-start(f32[768]{0:T(1024)S(1)} %get-tuple-element.195) | copy-start | bytes 9220
  107.3 16.0 %copy-start.95 = (bf16[2,768,384]{2,1,0:T(8,128)(2,1)S(1)}, bf16[2,768,384]{2,1,0:T(8,128)(2,1)}, u32[]{:S(2)}) copy-start(bf16[2,768,384]{2,1,0:T(8,128)(2,1)} %param.25) | copy-start | bytes 3538948
  125.9 133.4 %all-gather.7.cloned.1.call-start = ((), (), s32[]{:S(2)}) async-start(), calls=%async_computation.6 | async-start | bytes 1806336 | tf_op jit(solution)/shard_map/all_gather | solution.py:202
  128.5 22.6 %copy-start.72 = (f32[384]{0:T(512)S(1)}, f32[384]{0:T(512)}, u32[]{:S(2)}) copy-start(f32[384]{0:T(512)} %get-tuple-element.273) | copy-start | bytes 4612
  128.5 22.6 %copy-start.76 = (f32[384]{0:T(512)S(1)}, f32[384]{0:T(512)}, u32[]{:S(2)}) copy-start(f32[384]{0:T(512)} %get-tuple-element.187) | copy-start | bytes 4612
  128.5 22.6 %copy-start.80 = (f32[1152]{0:T(1024)S(1)}, f32[1152]{0:T(1024)}, u32[]{:S(2)}) copy-start(f32[1152]{0:T(1024)} %get-tuple-element.249) | copy-start | bytes 13828
  227.3 5.4 copy-start.81
  236.0 48.3 %all-gather.9.cloned.1.call-start = ((), (), s32[]{:S(2)}) async-start(), calls=%async_computation.8 | async-start | bytes 1806336 | tf_op jit(solution)/shard_map/all_gather | solution.py:226
  240.4 77.1 %reduce-scatter.9.cloned.1.call-start = ((), (), s32[]{:S(2)}) async-start(), calls=%async_computation.9 | async-start | bytes 1806336 | tf_op jit(solution)/shard_map/reduce_scatter | solution.py:240
  284.3 8.6 copy-start.96
  295.4 46.3 %reduce-scatter.7.cloned.1.call-start = ((), (), s32[]{:S(2)}) async-start(), calls=%async_computation.7 | async-start | bytes 1806336 | tf_op jit(solution)/shard_map/reduce_scatter | solution.py:208
  295.4 4.3 copy-start.45
  299.7 187.0 %all-gather.11.cloned.1.call-start = ((), (), s32[]{:S(2)}) async-start(), calls=%async_computation.10 | async-start | bytes 1806336 | tf_op jit(solution)/shard_map/all_gather | solution.py:226
  317.6 24.2 %copy-start.26 = (bf16[784,384]{1,0:T(8,128)(2,1)S(1)}, bf16[784,384]{1,0:T(8,128)(2,1)}, u32[]{:S(2)}) copy-start(bf16[784,384]{1,0:T(8,128)(2,1)} %reduce-scatter.9.cloned.1.call-done) | copy-start | bytes 1806340
  350.4 12.1 %slice-start.2 = ((s8[5505024]{0:T(1024)(128)(4,1)}), s8[1310720]{0:T(1024)(128)(4,1)S(1)}, s32[]{:S(2)}) async-start(s8[5505024]{0:T(1024)(128)(4,1)} %bitcast.249), calls=%async_computation.16 | async-start | bytes 2621440
  356.1 6.4 slice-start.3
  356.1 6.4 copy-start.13
  356.1 6.4 copy-start.24
  452.6 4.1 copy-start.57
  452.6 4.1 copy-start.68
  452.7 4.1 copy-start.73
  463.5 136.0 %all-reduce.8.cloned.1.call-start = ((), (), s32[]{:S(2)}) async-start(), calls=%async_computation.13 | async-start | bytes 4718592 | tf_op jit(solution)/shard_map/psum | solution.py:314
  463.6 4.3 copy-start.93
  463.6 4.3 copy-start.99
  467.9 18.9 %copy-start.87 = (f32[768]{0:T(1024)S(1)}, f32[768]{0:T(1024)}, u32[]{:S(2)}) copy-start(f32[768]{0:T(1024)} %copy-done.86) | copy-start | bytes 9220
  486.7 7.1 copy-start.92
  500.2 4.5 copy-start.47
  500.2 4.6 copy-start.52
  500.2 4.7 copy-start.31
  500.2 4.9 copy-start.53
  500.2 5.0 copy-start.35
  500.2 5.0 copy-start.43
  500.2 123.1 %reduce-scatter.11.cloned.1.call-start = ((), (), s32[]{:S(2)}) async-start(), calls=%async_computation.11 | async-start | bytes 1806336 | tf_op jit(solution)/shard_map/reduce_scatter | solution.py:240
  504.6 356.6 %all-reduce.6.cloned.1.call-start = ((), (), s32[]{:S(2)}) async-start(), calls=%async_computation.12 | async-start | bytes 9437184 | tf_op jit(solution)/shard_map/psum | solution.py:290
  508.9 7.9 copy-start.30
  513.7 4.5 copy-start.4
  513.7 4.5 copy-start.77
  602.5 20.8 %copy-start.3 = (f32[784,384]{1,0:T(8,128)S(1)}, f32[784,384]{1,0:T(8,128)}, u32[]{:S(2)}) copy-start(f32[784,384]{1,0:T(8,128)} %copy-done.2) | copy-start | bytes 3612676
  602.5 20.8 %copy-start.49 = (f32[784]{0:T(1024)S(1)}, f32[784]{0:T(1024)}, u32[]{:S(2)}) copy-start(f32[784]{0:T(1024)} %copy-done.48) | copy-start | bytes 9412
  602.5 20.8 %copy-start.62 = (f32[384]{0:T(512)S(1)}, f32[384]{0:T(512)}, u32[]{:S(2)}) copy-start(f32[384]{0:T(512)} %get-tuple-element.275) | copy-start | bytes 4612
  602.5 22.5 %copy-start.64 = (f32[784]{0:T(1024)S(1)}, f32[784]{0:T(1024)}, u32[]{:S(2)}) copy-start(f32[784]{0:T(1024)} %copy-done.63) | copy-start | bytes 9412
  602.5 22.5 %copy-start.55 = (f32[784]{0:T(1024)S(1)}, f32[784]{0:T(1024)}, u32[]{:S(2)}) copy-start(f32[784]{0:T(1024)} %copy-done.54) | copy-start | bytes 9412
  633.6 12.1 %slice-start = ((s8[5505024]{0:T(1024)(128)(4,1)}), s8[1310720]{0:T(1024)(128)(4,1)S(1)}, s32[]{:S(2)}) async-start(s8[5505024]{0:T(1024)(128)(4,1)} %bitcast.247), calls=%async_computation.14 | async-start | bytes 2621440
  639.3 6.4 slice-start.1
  639.4 6.4 copy-start.14
  639.4 6.4 copy-start.22
  861.2 4.1 copy-start.39
  861.2 4.1 copy-start.40
  (52 other events, 122.3 us)
Sparse Core Ops, SparseCore 0:
  81.6 25.7 all-gather.4
  126.0 22.0 reduce-scatter.4
  236.1 23.0 all-gather.6
  261.2 23.0 all-gather.8
  295.5 22.0 reduce-scatter.8
  319.7 22.0 reduce-scatter.6
  463.6 23.0 all-gather.10
  500.3 99.1 all-reduce.7
  601.8 21.4 reduce-scatter.10
  715.8 145.3 all-reduce.5
where the time goes:
time: 885 us; the launch traced here: 874 us
  waiting for transfers between devices  279 us (32%)
  local copies, waits for them, and re-layouts  269 us (30%)
  matrix products  135 us (15%)
  other arithmetic  101 us (11%)
  blocking collectives  73.9 us (8%)
  between operations  16.3 us (2%)
    psum x1, waiting for transfers between devices, on_device(): lax.psum((gain_pair, offset_pair, grad_input_proj, grad_input_bias, grad_...  85.6 us
    all_gather x2, waiting for transfers between devices, on_device(): gathered = lax.all_gather(second, 'mlp', axis=0, tiled=True)  44.6 us
    psum x1, waiting for transfers between devices, on_device(): lax.psum(expand_grads.astype(jnp.bfloat16), 'win').astype(jnp.float32)  44.5 us
    unnamed x219, local copies, waits for them, and re-layouts  42.6 us
    psum x1, blocking collectives, on_device(): lax.psum((gain_pair, offset_pair, grad_input_proj, grad_input_bias, grad_...  40.3 us
    reduce_scatter x2, waiting for transfers between devices, on_device(): lax.psum_scatter(jnp.dot(hidden, reduce_now, preferred_element_type=jnp.f...  39.9 us
    another operation x2, local copies, waits for them, and re-layouts, attend_backward(): jnp.stack([grad_query, grad_key, grad_value], axis=2)  39.1 us
    reduce_scatter x2, waiting for transfers between devices, on_device(): lax.psum_scatter(jnp.einsum('rf,cf->rc', grad_before_low, expand_now, pre...  37 us
  transfers between devices with their start and end apart: 10, of which 10 were waited for; matrix products, arithmetic and copies ran while one was open for 9% of the time, Pallas kernels for 0%

commit v1 on v0

v1 whole, which is shorter than its diff:
```python
import functools

import jax
import jax.numpy as jnp
from jax import lax
from jax.experimental import pallas as pl
from jax.experimental.pallas import tpu as pltpu
from jax.sharding import PartitionSpec as P

HEADS = 12
HEAD_DIM = 32
WIN = 7
SHIFT = 3
SPAN_SIDE = 2 * WIN - 1

EPS = 1e-05
MASKED = -1e30

PITCH = 8
SLOTS = WIN * PITCH
GROUP = 4
GROUPS = HEADS // GROUP
GLANES = GROUP * HEAD_DIM
GQ = GROUP * SLOTS

F32 = jnp.float32
BF16 = jnp.bfloat16

ERF_P = 0.39
ERF_C = (
    0.22003399505358215,
    0.22002241291251284,
    0.20367769093249805,
    0.16514655576456758,
    0.15214218925854978,
    -0.024768996902218943,
    0.20836931643666226,
    -0.19248882577712367,
    0.04786540601145673,
)


def dot(a, b):
    return lax.dot_general(a, b, (((1,), (0,)), ((), ())), preferred_element_type=F32)


def dot_nt(a, b):
    return lax.dot_general(a, b, (((1,), (1,)), ((), ())), preferred_element_type=F32)


def dot_tn(a, b):
    return lax.dot_general(a, b, (((0,), (0,)), ((), ())), preferred_element_type=F32)


def gelu_pair(u):
    bell = jnp.exp(-0.5 * u * u)
    t = 1.0 / (1.0 + (ERF_P * 0.5**0.5) * jnp.abs(u))
    poly = jnp.full_like(u, ERF_C[-1])
    for coef in ERF_C[-2::-1]:
        poly = poly * t + coef
    tail = 0.5 * bell * t * poly
    phi = jnp.where(u < 0, tail, 1.0 - tail)
    return u * phi, phi + u * bell * (0.5 * 2**0.5 * 0.5641895835477563)


def norm_stats(v):
    centred = v - jnp.mean(v, axis=-1, keepdims=True)
    rstd = lax.rsqrt(jnp.mean(centred * centred, axis=-1, keepdims=True) + EPS)
    return centred * rstd, rstd


def norm_back(v, gain, upstream):
    xhat, rstd = norm_stats(v)
    scaled = upstream * gain
    inner = (
        scaled
        - jnp.mean(scaled, axis=-1, keepdims=True)
        - xhat * jnp.mean(scaled * xhat, axis=-1, keepdims=True)
    )
    return rstd * inner, jnp.sum(upstream * xhat, axis=0, keepdims=True), jnp.sum(upstream, axis=0, keepdims=True)


def iota(shape, dim):
    return lax.broadcasted_iota(jnp.int32, shape, dim)


def expand_heads(rows):
    head = iota(rows.shape, 1) // HEAD_DIM
    return jnp.concatenate([jnp.where(head == j, rows, 0.0) for j in range(GROUP)], axis=0).astype(BF16)


def fold_heads(rows):
    head = iota((SLOTS, GLANES), 1) // HEAD_DIM
    out = rows[:SLOTS]
    for j in range(1, GROUP):
        out = jnp.where(head == j, rows[j * SLOTS : (j + 1) * SLOTS], out)
    return out


def window_row(per_side, wr, wc, r):
    return pl.multiple_of((wr * per_side + wc) * SLOTS + r * PITCH, PITCH)


def grid_to_windows(src, side, shifted, emit):
    per_side = side // WIN

    def step(wr, carry):
        for r in range(WIN):
            row = lax.rem(wr * WIN + r + (SHIFT if shifted else 0), side)
            line = src[row].astype(F32)
            width = line.shape[1]
            line = jnp.concatenate([line, jnp.zeros((32 - side, width), F32)], axis=0)
            if shifted:
                i = iota(line.shape, 0)
                line = jnp.where(i < side - SHIFT, pltpu.roll(line, 32 - SHIFT, 0), pltpu.roll(line, side - SHIFT, 0))
            for wc in range(per_side):
                part = line if wc == 0 else pltpu.roll(line, 32 - WIN * wc, 0)
                part = part[:PITCH]
                part = jnp.where(iota(part.shape, 0) < WIN, part, 0.0)
                emit(wr, wc, r, part)
        return carry

    lax.fori_loop(0, per_side, step, 0)


def windows_to_grid(src, dst, side, shifted):
    per_side = side // WIN

    def step(wr, carry):
        for r in range(WIN):
            row = lax.rem(wr * WIN + r + (SHIFT if shifted else 0), side)
            width = src.shape[1]
            line = jnp.zeros((32, width), F32)
            i = iota(line.shape, 0)
            for wc in range(per_side):
                tile = src[pl.ds(window_row(per_side, wr, wc, r), PITCH), :]
                tile = jnp.concatenate([tile, jnp.zeros((32 - PITCH, width), F32)], axis=0)
                if wc:
                    tile = pltpu.roll(tile, WIN * wc, 0)
                line = jnp.where((i >= WIN * wc) & (i < WIN * (wc + 1)), tile, line)
            if shifted:
                line = jnp.where(i < SHIFT, pltpu.roll(line, 32 - side + SHIFT, 0), pltpu.roll(line, SHIFT, 0))
            dst[row] = line[:side].astype(dst.dtype)
        return carry

    lax.fori_loop(0, per_side, step, 0)


def regular_to_shifted(src, dst, side):
    per_side = side // WIN

    def step(wr, carry):
        below = lax.rem(wr + 1, per_side)
        for r in range(WIN):
            sr, srr = (wr, r + SHIFT) if r + SHIFT < WIN else (below, r + SHIFT - WIN)
            for wc in range(per_side):
                here = src[pl.ds(window_row(per_side, sr, wc, srr), PITCH), :]
                right = src[pl.ds(window_row(per_side, sr, (wc + 1) % per_side, srr), PITCH), :]
                i = iota(here.shape, 0)
                tile = jnp.where(
                    i < WIN - SHIFT,
                    pltpu.roll(here, PITCH - SHIFT, 0),
                    jnp.where(i < WIN, pltpu.roll(right, WIN - SHIFT, 0), 0.0),
                )
                dst[pl.ds(window_row(per_side, wr, wc, r), PITCH), :] = tile
        return carry

    lax.fori_loop(0, per_side, step, 0)


def shifted_to_regular(src, dst, side):
    per_side = side // WIN

    def step(wr, carry):
        above = lax.rem(wr + per_side - 1, per_side)
        for r in range(WIN):
            sr, srr = (wr, r - SHIFT) if r >= SHIFT else (above, r - SHIFT + WIN)
            for wc in range(per_side):
                here = src[pl.ds(window_row(per_side, sr, wc, srr), PITCH), :]
                left = src[pl.ds(window_row(per_side, sr, (wc + per_side - 1) % per_side, srr), PITCH), :]
                i = iota(here.shape, 0)
                tile = jnp.where(
                    i < SHIFT,
                    pltpu.roll(left, PITCH - (WIN - SHIFT), 0),
                    jnp.where(i < WIN, pltpu.roll(here, SHIFT, 0), 0.0),
                )
                dst[pl.ds(window_row(per_side, wr, wc, r), PITCH), :] = tile
        return carry

    lax.fori_loop(0, per_side, step, 0)


ROWS_BLOCK = 4 * SLOTS
SMALL = {"gain1": 0, "gain2": 1, "bias1": 2, "bias2": 3, "query": 4, "value": 5, "output": 6, "reduce": 7}
TABLE_ROW = 8


def kernel(
    side,
    tokens,
    ids,
    gain,
    offset,
    w_in,
    b_in,
    table,
    w_out,
    b_out,
    w_exp,
    b_exp,
    w_red,
    b_red,
    cot,
    out,
    grad_tokens,
    d_in,
    d_out,
    d_exp,
    d_red,
    small,
    d_table,
    d_bexp,
    x,
    normed,
    qkv,
    probs,
    mixed,
    mid,
    second,
    hidden,
    slope,
    keys,
    bias,
    bias_sum,
    g,
    gs,
    gz,
    gb_low,
    dqkv,
    go,
):
    per_side = side // WIN
    windows = per_side * per_side
    rows = windows * SLOTS
    blocks = rows // ROWS_BLOCK
    shards, _, width, ff = w_exp.shape
    chunk = 256 if ff % 256 == 0 else ff

    def over_blocks(body):
        def step(i, carry):
            body(pl.ds(pl.multiple_of(i * ROWS_BLOCK, ROWS_BLOCK), ROWS_BLOCK))
            return carry

        lax.fori_loop(0, blocks, step, 0)

    def over_shards(body):
        def step(i, carry):
            body(i)
            return carry

        lax.fori_loop(0, shards, step, 0)

    def put_tokens(wr, wc, r, tile):
        x[0, pl.ds(window_row(per_side, wr, wc, r), PITCH), :] = tile

    grid_to_windows(tokens, side, False, put_tokens)

    for l in range(2):
        shifted = l == 1

        def put_keys(wr, wc, r, tile, shifted=shifted):
            lane = iota(tile.shape, 1).astype(F32)
            slot = iota(tile.shape, 0)
            label = tile
            if shifted:
                row_at = wr * WIN + r
                row_label = jnp.where(row_at >= side - WIN, 1, 0) + jnp.where(row_at >= side - SHIFT, 1, 0)
                col_at = wc * WIN + slot
                col_label = jnp.where(col_at >= side - WIN, 1, 0) + jnp.where(col_at >= side - SHIFT, 1, 0)
                label = label + (12 * row_label + 4 * col_label).astype(F32)
            hot = jnp.where((lane == label) & (slot < WIN), 1.0, 0.0)
            keys[pl.ds(window_row(per_side, wr, wc, r), PITCH), :] = hot

        grid_to_windows(ids, side, shifted, put_keys)

        krow = iota((SLOTS, 128), 0)
        qlane = iota((SLOTS, 128), 1)
        ahead = (qlane & (PITCH - 1)) >= (krow & (PITCH - 1))
        for grp in range(GROUPS):
            low = jnp.zeros((SLOTS, 128), F32)
            high = jnp.zeros((SLOTS, 128), F32)
            for j in range(GROUP):
                h = grp * GROUP + j
                both = [
                    pltpu.roll(
                        jnp.broadcast_to(table[l, 2 * h + s : 2 * h + s + 1, :], (SLOTS, 128)),
                        0,
                        1,
                        stride=1,
                        stride_axis=0,
                    )
                    for s in range(2)
                ]
                one = jnp.where(ahead, both[0], both[1])
                at = j * SLOTS
                if at < 128:
                    moved = pltpu.roll(one, at, 1) if at else one
                    low = jnp.where((qlane >= at) & (qlane < at + SLOTS), moved, low)
                if at + SLOTS > 128:
                    moved = pltpu.roll(one, (at - 128) % 128, 1)
                    high = jnp.where((qlane >= at - 128) & (qlane < at - 128 + SLOTS), moved, high)
            bias[grp, :, :128] = low
            bias[grp, :, 128:] = high[:, : GQ - 128]

        bias_row = jnp.concatenate(
            [b_in[l, 0:1, :], jnp.zeros((1, width), F32), b_in[l, 1:2, :]], axis=1
        )

        def project(at, l=l, bias_row=bias_row):
            xhat, _ = norm_stats(x[l, at, :])
            a = (xhat * gain[l, 0:1, :] + offset[l, 0:1, :]).astype(BF16)
            normed[l, at, :] = a
            for c in range(3):
                cols = slice(c * width, (c + 1) * width)
                qkv[l, at, cols] = (dot(a, w_in[l, :, cols]) + bias_row[:, cols]).astype(BF16)

        over_blocks(project)

        def attend(i, carry, l=l):
            at = pl.ds(pl.multiple_of(i * 2 * SLOTS, 2 * SLOTS), 2 * SLOTS)
            q = qkv[l, at, :width].astype(F32)
            k = qkv[l, at, width : 2 * width].astype(F32)
            v = qkv[l, at, 2 * width :].astype(F32)
            hot = keys[at, :]
            parts = []
            for w in range(2):
                here = slice(w * SLOTS, (w + 1) * SLOTS)
                hot_w = hot[here]
                allowed = dot_nt(hot_w.astype(BF16), jnp.concatenate([hot_w] * GROUP, axis=0).astype(BF16)) > 0.5
                outs = []
                for grp in range(GROUPS):
                    lanes = slice(grp * GLANES, (grp + 1) * GLANES)
                    q_all = expand_heads(q[here, lanes])
                    s = dot_nt(k[here, lanes].astype(BF16), q_all) * HEAD_DIM**-0.5 + bias[grp]
                    s = jnp.where(allowed, s, MASKED)
                    e = jnp.exp(s - jnp.max(s, axis=0, keepdims=True))
                    p = e / jnp.sum(e, axis=0, keepdims=True)
                    probs[l, 2 * i + w, grp] = p
                    outs.append(fold_heads(dot_tn(p.astype(BF16), v[here, lanes].astype(BF16))))
                parts.append(jnp.concatenate(outs, axis=1))
            mixed[l, at, :] = jnp.concatenate(parts, axis=0).astype(BF16)
            return carry

        lax.fori_loop(0, windows // 2, attend, 0)

        def middle(at, l=l):
            m = x[l, at, :] + dot(mixed[l, at, :], w_out[l]) + b_out[l : l + 1, :]
            mid[l, at, :] = m
            xhat, _ = norm_stats(m)
            second[l, at, :] = (xhat * gain[l, 1:2, :] + offset[l, 1:2, :]).astype(BF16)
            gs[at, :] = m + b_red[l : l + 1, :]

        over_blocks(middle)

        def feed(at, l=l):
            s = second[l, at, :]

            def one(i):
                for c in range(0, ff, chunk):
                    cols = slice(c, c + chunk)
                    before = dot(s, w_exp[i, l, :, cols]) + b_exp[i, l : l + 1, cols]
                    value, slope_now = gelu_pair(before)
                    hidden[l, i, at, cols] = value.astype(BF16)
                    slope[l, i, at, cols] = slope_now.astype(BF16)
                gs[at, :] += dot(hidden[l, i, at, :], w_red[i, l])

            over_shards(one)

        over_blocks(feed)

        if l == 0:
            regular_to_shifted(gs, x.at[1], side)
        else:
            windows_to_grid(gs, out, side, True)

    def put_cot(wr, wc, r, tile):
        g[pl.ds(window_row(per_side, wr, wc, r), PITCH), :] = tile

    grid_to_windows(cot, side, True, put_cot)
    small[...] = jnp.zeros(small.shape, F32)
    d_bexp[...] = jnp.zeros(d_bexp.shape, F32)

    for l in (1, 0):

        def add_small(name, value, l=l):
            at = SMALL[name]
            small[l, at : at + 1, :] += value

        def feed_back(at, l=l):
            g_now = g[at, :]
            add_small("reduce", jnp.sum(g_now, axis=0, keepdims=True))
            g_low = g_now.astype(BF16)
            gz[at, :] = g_low
            gs[at, :] = jnp.zeros(g_now.shape, F32)

            def one(i):
                for c in range(0, ff, chunk):
                    cols = slice(c, c + chunk)
                    gh = dot_nt(g_low, w_red[i, l, cols, :])
                    gb = gh * slope[l, i, at, cols].astype(F32)
                    d_bexp[i, l : l + 1, cols] += jnp.sum(gb, axis=0, keepdims=True)
                    gb_low[i, at, cols] = gb.astype(BF16)
                gs[at, :] += dot_nt(gb_low[i, at, :], w_exp[i, l])

            over_shards(one)

        over_blocks(feed_back)

        def feed_weights(i, l=l):
            for c in range(0, ff, chunk):
                cols = slice(c, c + chunk)
                d_red[i, l, cols, :] = dot_tn(hidden[l, i, :, cols], gz[...]).astype(BF16)
                d_exp[i, l, :, cols] = dot_tn(second[l], gb_low[i, :, cols]).astype(BF16)

        over_shards(feed_weights)

        def middle_back(at, l=l):
            dmid, dgain, doffset = norm_back(mid[l, at, :], gain[l, 1:2, :], gs[at, :])
            add_small("gain2", dgain)
            add_small("bias2", doffset)
            gm = g[at, :] + dmid
            g[at, :] = gm
            add_small("output", jnp.sum(gm, axis=0, keepdims=True))
            low = gm.astype(BF16)
            gz[at, :] = low
            go[at, :] = dot_nt(low, w_out[l]).astype(BF16)

        over_blocks(middle_back)
        d_out[l] = dot_tn(mixed[l], gz[...]).astype(BF16)
        bias_sum[...] = jnp.zeros(bias_sum.shape, F32)

        def attend_back(i, carry, l=l):
            at = pl.ds(pl.multiple_of(i * 2 * SLOTS, 2 * SLOTS), 2 * SLOTS)
            q = qkv[l, at, :width].astype(F32)
            k = qkv[l, at, width : 2 * width].astype(F32)
            v = qkv[l, at, 2 * width :].astype(F32)
            go_now = go[at, :].astype(F32)
            made = ([], [], [])
            for w in range(2):
                here = slice(w * SLOTS, (w + 1) * SLOTS)
                for grp in range(GROUPS):
                    lanes = slice(grp * GLANES, (grp + 1) * GLANES)
                    q_all = expand_heads(q[here, lanes])
                    go_all = expand_heads(go_now[here, lanes])
                    k_low = k[here, lanes].astype(BF16)
                    dp = dot_nt(v[here, lanes].astype(BF16), go_all)
                    p = probs[l, 2 * i + w, grp]
                    ds = (p * (dp - jnp.sum(p * dp, axis=0, keepdims=True))).astype(BF16)
                    bias_sum[grp] += ds.astype(F32)
                    made[0].append(fold_heads(dot_tn(ds, k_low)) * HEAD_DIM**-0.5)
                    made[1].append(dot(ds, q_all) * HEAD_DIM**-0.5)
                    made[2].append(dot(p.astype(BF16), go_all))
            for part in range(3):
                whole = jnp.concatenate(
                    [
                        jnp.concatenate(made[part][w * GROUPS : (w + 1) * GROUPS], axis=1)
                        for w in range(2)
                    ],
                    axis=0,
                )
                if part == 0:
                    add_small("query", jnp.sum(whole, axis=0, keepdims=True))
                if part == 2:
                    add_small("value", jnp.sum(whole, axis=0, keepdims=True))
                dqkv[at, part * width : (part + 1) * width] = whole.astype(BF16)
            return carry

        lax.fori_loop(0, windows // 2, attend_back, 0)

        for c in range(3):
            cols = slice(c * width, (c + 1) * width)
            d_in[l, :, cols] = dot_tn(normed[l], dqkv[:, cols]).astype(BF16)

        krow = iota((SLOTS, 128), 0)
        qlane = iota((SLOTS, 128), 1)
        ahead = (qlane & (PITCH - 1)) >= (krow & (PITCH - 1))
        for grp in range(GROUPS):
            low = bias_sum[grp, :, :128]
            high = jnp.concatenate([bias_sum[grp, :, 128:], jnp.zeros((SLOTS, 256 - GQ), F32)], axis=1)
            for j in range(GROUP):
                h = grp * GROUP + j
                at = j * SLOTS
                if at + SLOTS <= 128:
                    one = pltpu.roll(low, 128 - at, 1) if at else low
                elif at < 128:
                    one = jnp.where(qlane < 128 - at, pltpu.roll(low, 128 - at, 1), pltpu.roll(high, 128 - at, 1))
                else:
                    one = pltpu.roll(high, (256 - at) % 128, 1)
                one = jnp.where(qlane < SLOTS, one, 0.0)
                for s in range(2):
                    picked = jnp.where(ahead if s == 0 else jnp.logical_not(ahead), one, 0.0)
                    tile = picked[:PITCH]
                    for r in range(1, WIN):
                        tile = tile + pltpu.roll(picked[r * PITCH : (r + 1) * PITCH], 128 - r * PITCH, 1)
                    for step in (1, 2, 4):
                        tile = jnp.where((iota(tile.shape, 0) & step) > 0, pltpu.roll(tile, 128 - step, 1), tile)
                    d_table[l, 2 * h + s : 2 * h + s + 1, :] = jnp.sum(tile, axis=0, keepdims=True)

        def input_back(at, l=l):
            ga = dot_nt(dqkv[at, :], w_in[l])
            dx, dgain, doffset = norm_back(x[l, at, :], gain[l, 0:1, :], ga)
            add_small("gain1", dgain)
            add_small("bias1", doffset)
            gs[at, :] = g[at, :] + dx

        over_blocks(input_back)
        if l == 1:
            shifted_to_regular(gs, g, side)
        else:
            windows_to_grid(gs, grad_tokens, side, False)


def table_lanes(table):
    layers, _, heads = table.shape
    square = table.reshape(layers, SPAN_SIDE, SPAN_SIDE, heads).transpose(0, 3, 1, 2)
    right = jnp.pad(square[..., WIN - 1 :], ((0, 0),) * 3 + ((0, PITCH - WIN),))
    left = jnp.pad(square[..., : WIN - 1], ((0, 0),) * 3 + ((PITCH - WIN + 1, 0),))
    span = SPAN_SIDE * PITCH

    def lanes(part, back):
        flat = jnp.pad(part.reshape(layers, heads, span), ((0, 0), (0, 0), (0, 128 - span)))
        return jnp.roll(flat, -back, axis=-1)

    both = jnp.stack([lanes(right, (WIN - 1) * PITCH), lanes(left, WIN * PITCH)], axis=2)
    return both.reshape(layers, 2 * heads, 128)


def lanes_table(lanes):
    layers, heads = lanes.shape[0], lanes.shape[1] // 2
    both = lanes.reshape(layers, heads, 2, 128)
    span = SPAN_SIDE * PITCH

    def square(part, back):
        return jnp.roll(part, back, axis=-1)[..., :span].reshape(layers, heads, SPAN_SIDE, PITCH)

    right = square(both[:, :, 0], (WIN - 1) * PITCH)[..., :WIN]
    left = square(both[:, :, 1], WIN * PITCH)[..., PITCH - WIN + 1 :]
    whole = jnp.concatenate([left, right], axis=-1)
    return whole.reshape(layers, heads, SPAN_SIDE * SPAN_SIDE).transpose(0, 2, 1)


def on_device(
    tokens,
    crop_ids,
    norm_gain,
    norm_bias,
    input_proj,
    input_bias,
    position_table,
    output_proj,
    output_bias,
    expand_weight,
    expand_bias,
    reduce_weight,
    reduce_bias,
    cotangent,
):
    _, side, _, width = tokens.shape
    layers, _, ff = expand_weight.shape
    w_exp = lax.all_gather(expand_weight, "mlp", axis=0)
    w_red = lax.all_gather(reduce_weight, "mlp", axis=0)
    b_exp = lax.all_gather(expand_bias, "mlp", axis=0).astype(F32)
    shards = w_exp.shape[0]
    ids = jnp.broadcast_to(crop_ids[0, :, :, None].astype(F32), (side, side, 128))
    windows = (side // WIN) ** 2
    rows = windows * SLOTS
    vmem = pl.BlockSpec(memory_space=pltpu.VMEM)
    outs = pl.pallas_call(
        functools.partial(kernel, side),
        out_shape=(
            jax.ShapeDtypeStruct(tokens.shape[1:], BF16),
            jax.ShapeDtypeStruct(tokens.shape[1:], BF16),
            jax.ShapeDtypeStruct(input_proj.shape, BF16),
            jax.ShapeDtypeStruct(output_proj.shape, BF16),
            jax.ShapeDtypeStruct(w_exp.shape, BF16),
            jax.ShapeDtypeStruct(w_red.shape, BF16),
            jax.ShapeDtypeStruct((layers, 8, width), F32),
            jax.ShapeDtypeStruct((layers, 2 * HEADS, 128), F32),
            jax.ShapeDtypeStruct(b_exp.shape, F32),
        ),
        in_specs=[vmem] * 14,
        out_specs=[vmem] * 9,
        scratch_shapes=[
            pltpu.VMEM((layers, rows, width), F32),
            pltpu.VMEM((layers, rows, width), BF16),
            pltpu.VMEM((layers, rows, 3 * width), BF16),
            pltpu.VMEM((layers, windows, GROUPS, SLOTS, GQ), F32),
            pltpu.VMEM((layers, rows, width), BF16),
            pltpu.VMEM((layers, rows, width), F32),
            pltpu.VMEM((layers, rows, width), BF16),
            pltpu.VMEM((layers, shards, rows, ff), BF16),
            pltpu.VMEM((layers, shards, rows, ff), BF16),
            pltpu.VMEM((rows, 128), F32),
            pltpu.VMEM((GROUPS, SLOTS, GQ), F32),
            pltpu.VMEM((GROUPS, SLOTS, GQ), F32),
            pltpu.VMEM((rows, width), F32),
            pltpu.VMEM((rows, width), F32),
            pltpu.VMEM((rows, width), BF16),
            pltpu.VMEM((shards, rows, ff), BF16),
            pltpu.VMEM((rows, 3 * width), BF16),
            pltpu.VMEM((rows, width), BF16),
        ],
        compiler_params=pltpu.CompilerParams(vmem_limit_bytes=64 * 1024 * 1024),
    )(
        tokens[0],
        ids,
        norm_gain,
        norm_bias,
        input_proj,
        input_bias,
        table_lanes(position_table),
        output_proj,
        output_bias,
        w_exp,
        b_exp,
        w_red,
        reduce_bias,
        cotangent[0],
    )
    out, grad_tokens, d_in, d_out, d_exp, d_red, small, d_table, d_bexp = outs
    d_in, d_out = lax.psum((d_in, d_out), ("win", "mlp"))
    small, d_table = lax.psum((small, d_table), ("win", "mlp"))
    d_exp = lax.psum(lax.psum_scatter(d_exp, "mlp", scatter_dimension=0, tiled=False), "win")
    d_red = lax.psum(lax.psum_scatter(d_red, "mlp", scatter_dimension=0, tiled=False), "win")
    d_bexp = lax.psum(lax.psum_scatter(d_bexp, "mlp", scatter_dimension=0, tiled=False), "win")
    return (
        out[None],
        grad_tokens[None],
        small[:, 0:2],
        small[:, 2:4],
        d_in.astype(F32),
        small[:, 4:6],
        lanes_table(d_table),
        d_out.astype(F32),
        small[:, 6],
        d_exp.astype(F32),
        d_bexp,
        d_red.astype(F32),
        small[:, 7],
    )


def solution(mesh):
    tokens = P(("win", "mlp"), None, None, None)
    placed = (
        tokens,
        P(("win", "mlp"), None, None),
        P(),
        P(),
        P(),
        P(),
        P(),
        P(),
        P(),
        P(None, None, "mlp"),
        P(None, "mlp"),
        P(None, "mlp", None),
        P(),
        tokens,
    )
    return jax.shard_map(
        on_device,
        mesh=mesh,
        in_specs=placed,
        out_specs=(
            tokens,
            tokens,
            P(),
            P(),
            P(),
            P(),
            P(),
            P(),
            P(),
            P(None, None, "mlp"),
            P(None, "mlp"),
            P(None, "mlp", None),
            P(),
        ),
        check_vma=False,
    )
```

time: 885 us -> 542 us (0.61); the launches traced: 874 us -> 542 us
  local copies, waits for them, and re-layouts: 269 us -> 6.95 us
  matrix products: 135 us -> 0 us
  Pallas kernels: 0 us -> 127 us
  other arithmetic: 101 us -> 10.1 us
  waiting for transfers between devices: 279 us -> 298 us
  blocking collectives: 73.9 us -> 85 us
    dot_general x40 -> x0, matrix products: 135 us -> none  [the longest x2 29.5 us: on_device(): jnp.dot(gathered, expand_all[layer_idx], preferred_element_type=jnp.float32)]
    pallas_call x0 -> x1, Pallas kernels: none -> 127 us  [on_device(): pl.pallas_call(functools.partial(kernel, side), out_shape=(jax.ShapeDtype...]
    reshape x30 -> x6, local copies, waits for them, and re-layouts: 95 us -> 0.92 us  [the longest x2 0.74 us: lanes_table(): whole.reshape(layers, heads, SPAN_SIDE * SPAN_SIDE).transpose(0, 2, 1)]
    another operation x16 -> x1, local copies, waits for them, and re-layouts: 46.8 us -> 0.62 us  [table_lanes(): jnp.stack([lanes(right, (WIN - 1) * PITCH), lanes(left, WIN * PITCH)], ax...]
    unnamed x219 -> x24, local copies, waits for them, and re-layouts: 42.6 us -> 2.35 us
    convert_element_type x10 -> x0, local copies, waits for them, and re-layouts: 33 us -> none  [the longest x4 21.6 us: on_device(): grad_qkv_low = grad_qkv.astype(jnp.bfloat16)]
    reduce_sum x22 -> x0, other arithmetic: 28.7 us -> none  [the longest x4 6.67 us: layer_norm(): return centred * lax.rsqrt(variance + epsilon) * gain + offset]
    concatenate x8 -> x3, other arithmetic: 27.1 us -> 0.21 us  [the longest x2 0.17 us: square(): jnp.roll(part, back, axis=-1)[..., :span]]
  transfers between devices with their start and end apart: 10 -> 6, of which waited for: 10 -> 6; matrix products, arithmetic and copies ran while one was open for 9% -> 2% of each run, Pallas kernels for 0% -> 0%
where the time goes in v1:
time: 542 us
  waiting for transfers between devices  298 us (55%)
  Pallas kernels  127 us (23%)
  blocking collectives  85 us (16%)
  between operations  14.4 us (3%)
  other arithmetic  10.1 us (2%)
  local copies, waits for them, and re-layouts  6.95 us (1%)
    pallas_call x1, Pallas kernels, on_device(): pl.pallas_call(functools.partial(kernel, side), out_shape=(jax.ShapeDtype...  127 us
    psum x1, waiting for transfers between devices, on_device(): lax.psum(lax.psum_scatter(d_exp, 'mlp', scatter_dimension=0, tiled=False)...  97.4 us
    psum x1, waiting for transfers between devices, on_device(): d_in, d_out = lax.psum((d_in, d_out), ('win', 'mlp'))  57.4 us
    psum x1, blocking collectives, on_device(): small, d_table = lax.psum((small, d_table), ('win', 'mlp'))  40.2 us
    all_gather x1, waiting for transfers between devices, on_device(): w_red = lax.all_gather(reduce_weight, 'mlp', axis=0)  37.6 us
    reduce_scatter x1, waiting for transfers between devices, on_device(): lax.psum_scatter(d_red, 'mlp', scatter_dimension=0, tiled=False)  37.5 us
    reduce_scatter x1, waiting for transfers between devices, on_device(): lax.psum_scatter(d_exp, 'mlp', scatter_dimension=0, tiled=False)  33.6 us
    all_gather x1, waiting for transfers between devices, on_device(): w_exp = lax.all_gather(expand_weight, 'mlp', axis=0)  31.7 us
  transfers between devices with their start and end apart: 6, of which 6 were waited for; matrix products, arithmetic and copies ran while one was open for 2% of the time, Pallas kernels for 0%

profile of v1, /device:TPU:0, one launch (start us, length us, event | category | flops | bytes accessed | tf_op | source)
XLA Modules:
  0.0 541.7 jit_solution(3476537010642626421)
XLA Ops:
  7.2 0.0 copy-start.2
  7.2 0.0 all-gather.7.cloned.1.call-start
  7.2 0.7 all-gather.7.cloned.1.call-update
  7.9 0.0 copy-start.5
  7.9 0.0 copy-start.7
  7.9 0.0 all-gather.9.cloned.1.call-start
  8.0 0.7 all-gather.9.cloned.1.call-update
  8.7 0.0 reduce-scatter.3.cloned.1.call-start
  8.7 0.0 copy-done.2
  8.7 0.1 reshape.58
  8.9 0.1 slice.94
  9.0 0.3 copy.55
  9.3 0.1 copy.41
  9.4 0.1 copy.42
  9.5 0.3 copy.56
  9.8 0.1 copy.44
  9.9 0.1 copy.45
  10.0 0.1 maximum_bitcast_fusion
  10.1 0.6 copy.46
  10.8 0.0 copy-done.5
  10.8 0.0 copy-done.7
  10.8 5.3 all-gather.3
  16.1 0.6 convert_element_type.41.b_exp
  16.7 31.7 %all-gather.7.cloned.1.call-done = bf16[4,384,768]{2,1,0:T(8,128)(2,1)} async-done(((bf16[2,384,768]{2,1,0:T(8,128)(2,1)}), bf16[4,384,768]{2,1,0:T(8,128)(2,1)}) %all-gather.7.cloned.1.call-update) | async-done | bytes 2359312 | tf_op jit(solution)/shard_map/all_gather | solution.py:570
  48.4 37.6 %all-gather.9.cloned.1.call-done = bf16[4,768,384]{2,1,0:T(8,128)(2,1)} async-done(((bf16[2,768,384]{2,1,0:T(8,128)(2,1)}), bf16[4,768,384]{2,1,0:T(8,128)(2,1)}) %all-gather.9.cloned.1.call-update) | async-done | bytes 2359312 | tf_op jit(solution)/shard_map/all_gather | solution.py:571
  86.0 0.9 broadcast_in_dim.11.ids
  87.0 127.3 %shard_map.237 = (bf16[28,28,384]{2,1,0:T(8,128)(2,1)}, bf16[28,28,384]{2,1,0:T(8,128)(2,1)}, bf16[2,384,1152]{2,1,0:T(8,128)(2,1)}, bf16[2,384,384]{2,1,0:T(8,1...) custom-call(bf16[28,28,384]{2,1,0:T(8,128)(2,1)} %bitcast.53, ...), custom_call_target="tpu_custom_call" | custom-call | tf_op jit(solution)/shard_map/pallas_call | solution.py:578
  214.3 0.0 reduce-scatter.3.cloned.1.call-update
  214.3 0.0 reduce-scatter.5.cloned.1.call-start
  214.3 0.5 reduce-scatter.5.cloned.1.call-update
  214.9 0.0 all-reduce.11.cloned.1.call-start
  214.9 0.5 all-reduce.11.cloned.1.call-update
  215.5 0.0 copy-start.8
  215.5 0.0 copy-start.4
  215.5 0.0 copy-start.3
  215.5 0.0 all-reduce.13.cloned.1.call-start
  215.5 33.6 %reduce-scatter.3.cloned.1.call-done = bf16[1,2,384,768]{3,2,1,0:T(8,128)(2,1)} async-done(((bf16[2,2,384,768]{3,2,1,0:T(8,128)(2,1)}), bf16[1,2,384,768]{3,2,1,0:T(8,128)(2,1)}) %reduce-scatter.3.cloned.1.call-update) | async-done | bytes 1179664 | tf_op jit(solution)/shard_map/reduce_scatter | solution.py:633
  249.2 37.5 %reduce-scatter.5.cloned.1.call-done = bf16[1,2,768,384]{3,2,1,0:T(8,128)(2,1)} async-done(((bf16[2,2,768,384]{3,2,1,0:T(8,128)(2,1)}), bf16[1,2,768,384]{3,2,1,0:T(8,128)(2,1)}) %reduce-scatter.5.cloned.1.call-update) | async-done | bytes 1179664 | tf_op jit(solution)/shard_map/reduce_scatter | solution.py:634
  286.7 0.0 all-reduce.13.cloned.1.call-update
  286.7 0.0 copy-done.8
  286.7 0.6 dynamic-slice
  287.3 0.0 copy-done.4
  287.3 0.0 copy-done.3
  287.3 40.2 %all-reduce.5 = (f32[2,8,384]{2,1,0:T(8,128)S(1)}, f32[2,12,2,128]{3,0,1,2:T(2,128)S(1)}) all-reduce(f32[2,8,384]{2,1,0:T(8,128)S(1)} %copy-done.3, f32[2,12,2,128]{3,0,1,2:T(2,128)S(1)} %copy.47), channel_id=1, replica_groups=mesh['win'=16,'mlp'=2] {'win','mlp'}, use_global_device_ids=true, to_apply=%region_0.1 | all-reduce | flops 12288 | bytes 98304 | tf_op jit(solution)/shard_map/psum | solution.py:632
  327.6 0.1 slice.102
  327.7 0.1 pad_maximum_fusion.3
  327.8 0.1 copy.48
  327.9 0.1 slice.106
  328.0 0.1 pad_maximum_fusion.2
  328.1 0.1 copy.49
  328.2 0.7 copy.51
  329.0 0.6 copy.61
  329.6 0.6 copy.62
  330.1 8.8 %all-reduce.4 = f32[2,2,768]{2,1,0:T(2,128)S(1)} all-reduce(f32[2,2,768]{2,1,0:T(2,128)S(1)} %copy-done.6), channel_id=6, replica_groups=mesh['win'=16,'mlp'=2] {'mlp'}, use_global_device_ids=true, to_apply=%region_6.7.clone | all-reduce | flops 3072 | bytes 24576
  339.0 0.6 dynamic-slice_bitcast_fusion
  339.6 30.6 %psum.54 = f32[2,768]{1,0:T(2,128)} all-reduce(f32[2,768]{1,0:T(2,128)S(1)} %dynamic-slice_bitcast_fusion), channel_id=1, replica_groups=mesh['win'=16,'mlp'=2] {'win'}, use_global_device_ids=true, to_apply=%region_7.8 | all-reduce | flops 1536 | bytes 12288 | tf_op jit(solution)/shard_map/psum | solution.py:635
  370.3 0.6 fusion.1
  370.9 57.4 %all-reduce.11.cloned.1.call-done = (bf16[2,384,1152]{2,1,0:T(8,128)(2,1)}, bf16[2,384,384]{2,1,0:T(8,128)(2,1)}) async-done(((bf16[2,384,1152]{2,1,0:T(8,128)(2,1)}, bf16[2,384,384]{2,1,0:T(8,128)(2,1)}), (bf16[2,384,1152]{2,1,0:T(8,128)(2,1)}, bf16[2,384,384]{2,1,0:T(8,128)(2,1)})) %all-reduce.11.cloned.1.call-update) | async-done | bytes 2359312 | tf_op jit(solution)/shard_map/psum | solution.py:631
  428.3 3.6 convert_element_type.36
  431.9 0.0 copy-done.1
  431.9 1.1 convert_element_type.37
  433.0 97.4 %all-reduce.13.cloned.1.call-done = (bf16[2,384,768]{2,1,0:T(8,128)(2,1)}, bf16[2,768,384]{2,1,0:T(8,128)(2,1)}) async-done(((bf16[2,384,768]{2,1,0:T(8,128)(2,1)}, bf16[2,768,384]{2,1,0:T(8,128)(2,1)}), (bf16[2,384,768]{2,1,0:T(8,128)(2,1)}, bf16[2,768,384]{2,1,0:T(8,128)(2,1)})) %all-reduce.13.cloned.1.call-update) | async-done | bytes 2359312 | tf_op jit(solution)/shard_map/psum | solution.py:633
  530.4 2.9 convert_element_type.38
  533.3 1.6 convert_element_type.39
  (20 shorter events, 0.2 us)
Async XLA Ops:
  7.2 1.6 copy-start.2
  7.2 41.2 %all-gather.7.cloned.1.call-start = ((), (), s32[]{:S(2)}) async-start(), calls=%async_computation.4 | async-start | bytes 3538944 | tf_op jit(solution)/shard_map/all_gather | solution.py:570
  7.9 2.8 copy-start.5
  7.9 2.9 copy-start.7
  7.9 78.1 %all-gather.9.cloned.1.call-start = ((), (), s32[]{:S(2)}) async-start(), calls=%async_computation.5 | async-start | bytes 3538944 | tf_op jit(solution)/shard_map/all_gather | solution.py:571
  8.7 240.5 %reduce-scatter.3.cloned.1.call-start = ((), (), s32[]{:S(2)}) async-start(), calls=%async_computation.2 | async-start | bytes 3538944 | tf_op jit(solution)/shard_map/reduce_scatter | solution.py:633
  214.3 72.4 %reduce-scatter.5.cloned.1.call-start = ((), (), s32[]{:S(2)}) async-start(), calls=%async_computation.3 | async-start | bytes 3538944 | tf_op jit(solution)/shard_map/reduce_scatter | solution.py:634
  214.9 213.4 %all-reduce.11.cloned.1.call-start = ((), (), s32[]{:S(2)}) async-start(), calls=%async_computation.6 | async-start | bytes 4718592 | tf_op jit(solution)/shard_map/psum | solution.py:631
  215.5 71.2 %copy-start.8 = (u32[32]{0:T(128)S(1)}, u32[32]{0:T(128)}, u32[]{:S(2)}) copy-start(u32[32]{0:T(128)} %constant.16) | copy-start | bytes 388
  215.5 71.8 %copy-start.4 = (f32[2,24,128]{2,1,0:T(8,128)S(1)}, f32[2,24,128]{2,1,0:T(8,128)}, u32[]{:S(2)}) copy-start(f32[2,24,128]{2,1,0:T(8,128)} %get-tuple-element.26) | copy-start | bytes 73732
  215.5 71.8 %copy-start.3 = (f32[2,8,384]{2,1,0:T(8,128)S(1)}, f32[2,8,384]{2,1,0:T(8,128)}, u32[]{:S(2)}) copy-start(f32[2,8,384]{2,1,0:T(8,128)} %get-tuple-element.24) | copy-start | bytes 73732
  215.5 314.9 %all-reduce.13.cloned.1.call-start = ((), (), s32[]{:S(2)}) async-start(), calls=%async_computation.7 | async-start | bytes 4718592 | tf_op jit(solution)/shard_map/psum | solution.py:633
  286.7 43.5 %copy-start.6 = (f32[2,2,768]{2,1,0:T(2,128)S(1)}, f32[2,2,768]{2,1,0:T(2,128)}, u32[]{:S(2)}) copy-start(f32[2,2,768]{2,1,0:T(2,128)} %get-tuple-element.29) | copy-start | bytes 36868
  428.3 3.6 copy-start.1
  530.4 2.9 copy-start
Sparse Core Ops, SparseCore 0:
  9.6 38.7 all-gather.6
  49.9 36.0 all-gather.8
  214.4 34.7 reduce-scatter.2
  251.9 34.6 reduce-scatter.4
  292.8 135.4 all-reduce.10
  432.2 98.1 all-reduce.12

commit v2 on v1

--- a/solution.py
+++ b/solution.py
@@ -192,59 +192,346 @@
 
 ROWS_BLOCK = 4 * SLOTS
 SMALL = {"gain1": 0, "gain2": 1, "bias1": 2, "bias2": 3, "query": 4, "value": 5, "output": 6, "reduce": 7}
-TABLE_ROW = 8
-
-
-def kernel(
-    side,
-    tokens,
-    ids,
-    gain,
-    offset,
-    w_in,
-    b_in,
-    table,
-    w_out,
-    b_out,
-    w_exp,
-    b_exp,
-    w_red,
-    b_red,
-    cot,
-    out,
-    grad_tokens,
-    d_in,
-    d_out,
-    d_exp,
-    d_red,
-    small,
-    d_table,
-    d_bexp,
-    x,
-    normed,
-    qkv,
-    probs,
-    mixed,
-    mid,
-    second,
-    hidden,
-    slope,
-    keys,
-    bias,
-    bias_sum,
-    g,
-    gs,
-    gz,
-    gb_low,
-    dqkv,
-    go,
-):
+SMALL_TABLE = 8
+SMALL_EXPAND = 16
+SMALL_ROWS = 24
+ADD_ROWS = 96
+
+
+def rounded(value, step):
+    return -(-value // step) * step
+
+
+def feed_layout(width, ff):
+    blocked = ff % width == 0
+    return 2 * ff, blocked
+
+
+class Links:
+    def __init__(self, mesh_shape, send_sem, recv_sem):
+        self.win, self.mlp = mesh_shape
+        self.send_sem, self.recv_sem = send_sem, recv_sem
+        self.used = 0
+        w, m = lax.axis_index("win"), lax.axis_index("mlp")
+        self.core, self.x, self.z, self.m = lax.rem(w, 2), lax.rem(lax.div(w, 2), 2), lax.div(w, 4), m
+        self.depth = self.win // 4
+        self.groups = {
+            "core": (2, self.core, lambda q: self.at(core=q)),
+            "x": (2, self.x, lambda q: self.at(x=q)),
+            "z": (self.depth, self.z, lambda q: self.at(z=q)),
+            "mlp": (self.mlp, m, lambda q: self.at(m=q)),
+            "plane": (
+                2 * self.mlp,
+                self.x * self.mlp + m,
+                lambda q: self.at(x=lax.div(q, self.mlp), m=lax.rem(q, self.mlp)),
+            ),
+        }
+
+    def at(self, core=None, x=None, z=None, m=None):
+        core = self.core if core is None else core
+        x = self.x if x is None else x
+        z = self.z if z is None else z
+        m = self.m if m is None else m
+        return ((z * 2 + x) * 2 + core, m)
+
+    def peers(self, group):
+        size, me, _ = self.groups[group]
+        return [(d, lax.rem(me + d, size), lax.rem(me + size - d, size)) for d in range(1, size)]
+
+    def me(self, group):
+        return self.groups[group][1]
+
+    def size(self, group):
+        return self.groups[group][0]
+
+    def barrier(self):
+        sem = pltpu.get_barrier_semaphore()
+        count = 0
+        for group in ("core", "plane", "z"):
+            for _, q, _ in self.peers(group):
+                pl.semaphore_signal(
+                    sem, inc=1, device_id=self.groups[group][2](q), device_id_type=pl.DeviceIdType.MESH
+                )
+                count += 1
+        pl.semaphore_wait(sem, count)
+
+    def copy(self, group, q, src, dst):
+        n = self.used
+        self.used += 1
+        made = pltpu.make_async_remote_copy(
+            src_ref=src,
+            dst_ref=dst,
+            send_sem=self.send_sem.at[n],
+            recv_sem=self.recv_sem.at[n],
+            device_id=self.groups[group][2](q),
+            device_id_type=pl.DeviceIdType.MESH,
+        )
+        made.start()
+        return made
+
+
+def add_rows(dst, sources, start, count):
+    step = next(n for n in (ADD_ROWS, 48, 32, 16) if count % n == 0)
+
+    def one(i, carry):
+        at = pl.multiple_of(start + i * step, 16)
+        total = dst[pl.ds(at, step), :].astype(F32)
+        for source, first in sources:
+            total = total + source[pl.ds(pl.multiple_of(first + i * step, 16), step), :].astype(F32)
+        dst[pl.ds(at, step), :] = total.astype(dst.dtype)
+        return carry
+
+    lax.fori_loop(0, count // step, one, 0)
+
+
+class Reduction:
+    def __init__(self, links, staged, out, stages, buffers, local_sem):
+        self.links, self.staged, self.out = links, staged, out
+        self.stages, self.buffers, self.local_sem = stages, buffers, local_sem
+        self.level = 0
+        self.base, self.rows = 0, staged.shape[0]
+        self.waiting = None
+        self.trail = []
+
+    def send(self):
+        group = self.stages[self.level]
+        links, block = self.links, self.rows // self.links.size(group)
+        self.waiting = [
+            links.copy(
+                group,
+                q,
+                self.staged.at[pl.ds(pl.multiple_of(self.base + q * block, 16), block)],
+                self.buffers[self.level].at[d - 1],
+            )
+            for d, q, _ in links.peers(group)
+        ]
+
+    def take(self):
+        group = self.stages[self.level]
+        links, block = self.links, self.rows // self.links.size(group)
+        for copy in self.waiting:
+            copy.wait()
+        self.trail.append((group, self.base, block))
+        self.base = self.base + links.me(group) * block
+        self.rows = block
+        buffer = self.buffers[self.level]
+        add_rows(
+            self.staged,
+            [(buffer.at[d - 1], 0) for d, _, _ in links.peers(group)],
+            self.base,
+            block,
+        )
+        self.level += 1
+
+    def turn(self):
+        mine = pl.ds(pl.multiple_of(self.base, 16), self.rows)
+        self.local = pltpu.make_async_copy(self.staged.at[mine], self.out.at[mine], self.local_sem)
+        self.local.start()
+        self.spread(self.staged)
+
+    def spread(self, source):
+        group, base, block = self.trail[-1]
+        links = self.links
+        mine = pl.ds(pl.multiple_of(self.base, 16), self.rows)
+        self.waiting = [links.copy(group, q, source.at[mine], self.out.at[mine]) for _, q, _ in links.peers(group)]
+
+    def collect(self):
+        group, base, block = self.trail.pop()
+        for copy in self.waiting:
+            copy.wait()
+        if self.local is not None:
+            self.local.wait()
+            self.local = None
+        self.base, self.rows = base, block * self.links.size(group)
+
+    def widen(self):
+        self.collect()
+        if self.trail:
+            self.spread(self.out)
+
+
+class FeedReduction(Reduction):
+    def __init__(self, links, staged, out, buffers, local_sem):
+        shards, rows, width = staged.shape
+        self.all = staged
+        self.first = buffers[0]
+        self.second = buffers[1]
+        super().__init__(links, staged.at[links.m], out, ("core", "mlp", "x", "z"), (None, None) + tuple(buffers[2:]), local_sem)
+
+    def send(self):
+        if self.level > 1:
+            return super().send()
+        links = self.links
+        half = self.staged.shape[0] // 2
+        if self.level == 0:
+            (_, q, _), = links.peers("core")
+            self.waiting = [
+                links.copy("core", q, self.all.at[:, pl.ds(pl.multiple_of(q * half, 16), half)], self.first)
+            ]
+        else:
+            mine = pl.ds(pl.multiple_of(self.base, 16), half)
+            self.waiting = [
+                links.copy("mlp", q, self.all.at[q, mine], self.second.at[d - 1])
+                for d, q, _ in links.peers("mlp")
+            ]
+
+    def take(self):
+        if self.level > 1:
+            return super().take()
+        links = self.links
+        for copy in self.waiting:
+            copy.wait()
+        half = self.staged.shape[0] // 2
+        if self.level == 0:
+            self.trail.append(("core", 0, half))
+            self.base = links.core * half
+            self.rows = half
+            for i in range(self.all.shape[0]):
+                add_rows(self.all.at[i], [(self.first.at[i], 0)], self.base, half)
+        else:
+            add_rows(
+                self.staged,
+                [(self.second.at[d - 1], 0) for d, _, _ in links.peers("mlp")],
+                self.base,
+                half,
+            )
+        self.level += 1
+
+
+class SmallSum:
+    def __init__(self, links, value, buffers, out):
+        self.links, self.value, self.buffers, self.out = links, value, buffers, out
+        self.level = 0
+        self.stages = ("core", "plane", "z")
+
+    def send(self):
+        group = self.stages[self.level]
+        links, buffer = self.links, self.buffers[self.level]
+        me = links.me(group)
+        buffer[me] = self.value[...]
+        self.waiting = [links.copy(group, q, buffer.at[me], buffer.at[me]) for _, q, _ in links.peers(group)]
+
+    def take(self):
+        for copy in self.waiting:
+            copy.wait()
+        buffer = self.buffers[self.level]
+        total = buffer[0]
+        for j in range(1, buffer.shape[0]):
+            total = total + buffer[j]
+        self.level += 1
+        if self.level == len(self.stages):
+            self.out[...] = total
+        else:
+            self.value[...] = total
+
+    def step(self):
+        self.take()
+        if self.level < len(self.stages):
+            self.send()
+
+
+class Idle:
+    def skip(self):
+        pass
+
+    send = take = turn = widen = step = skip
+
+
+def kernel(side, mesh_shape, *refs):
+    refs = list(refs)
+
+    def take(n):
+        got = refs[:n]
+        del refs[:n]
+        return got
+
+    tokens, ids, gain, offset, w_in, b_in, table, w_out, b_out, w_exp, b_exp, w_red, b_red, cot = take(14)
+    fused = mesh_shape is not None
+    out, grad_tokens, d_attn, d_feed, small = take(5)
+    (x, normed, qkv, probs, mixed, mid, second, hidden, slope) = take(9)
+    (keys, bias, bias_sum, g, gs, gz, gb_low, dqkv, go, d_bexp) = take(10)
+    if fused:
+        out_attn, out_feed, out_small = d_attn, d_feed, small
+        d_attn, d_feed, small = take(3)
+        local_exp, local_bexp, local_red = w_exp, b_exp, w_red
+        w_exp, b_exp, w_red = take(3)
+        feed_buffers, attn_buffers, small_buffers = take(4), take(3), take(3)
+        local_sems, send_sem, recv_sem = take(3)
+        links = Links(mesh_shape, send_sem, recv_sem)
+        feeds = [
+            FeedReduction(links, d_feed.at[l], out_feed.at[l], [b.at[l] for b in feed_buffers], local_sems.at[2 * l])
+            for l in range(2)
+        ]
+        attns = [
+            Reduction(
+                links, d_attn.at[l], out_attn.at[l], ("core", "plane", "z"), [b.at[l] for b in attn_buffers], local_sems.at[2 * l + 1]
+            )
+            for l in range(2)
+        ]
+        smalls = [SmallSum(links, small.at[l], [b.at[l] for b in small_buffers], out_small.at[l]) for l in range(2)]
+
+    def hook(*actions):
+        for action in actions:
+            action()
+
+    if not fused:
+        idle = Idle()
+        feeds = attns = smalls = (idle, idle)
+
     per_side = side // WIN
     windows = per_side * per_side
     rows = windows * SLOTS
     blocks = rows // ROWS_BLOCK
     shards, _, width, ff = w_exp.shape
     chunk = 256 if ff % 256 == 0 else ff
+    _, blocked = feed_layout(width, ff)
+
+    if fused:
+        locals_ = [
+            pltpu.make_async_copy(local_exp, w_exp.at[links.m], local_sems.at[4]),
+            pltpu.make_async_copy(local_red, w_red.at[links.m], local_sems.at[5]),
+            pltpu.make_async_copy(local_bexp, b_exp.at[links.m], local_sems.at[6]),
+        ]
+        for copy in locals_:
+            copy.start()
+        links.barrier()
+        halves = (
+            pl.ds(pl.multiple_of(links.core * (width // 2), 16), width // 2),
+            pl.ds(pl.multiple_of(links.core * (ff // 2), 16), ff // 2),
+        )
+        fetched = [
+            [
+                copy
+                for _, q, _ in links.peers("mlp")
+                for copy in (
+                    links.copy("mlp", q, local_exp.at[l, halves[0]], w_exp.at[links.m, l, halves[0]]),
+                    links.copy("mlp", q, local_red.at[l, halves[1]], w_red.at[links.m, l, halves[1]]),
+                )
+            ]
+            for l in range(2)
+        ]
+        fetched_bias = [links.copy("mlp", q, local_bexp, b_exp.at[links.m]) for _, q, _ in links.peers("mlp")]
+        passed = [None, None]
+
+        def pass_weights(l):
+            for copy in fetched[l]:
+                copy.wait()
+            (_, sibling, _), = links.peers("core")
+            passed[l] = [
+                copy
+                for _, _, q in links.peers("mlp")
+                for copy in (
+                    links.copy("core", sibling, w_exp.at[q, l, halves[0]], w_exp.at[q, l, halves[0]]),
+                    links.copy("core", sibling, w_red.at[q, l, halves[1]], w_red.at[q, l, halves[1]]),
+                )
+            ]
+
+        def have_weights(l):
+            for copy in passed[l]:
+                copy.wait()
+            if l == 0:
+                for copy in locals_ + fetched_bias:
+                    copy.wait()
 
     def over_blocks(body):
         def step(i, carry):
@@ -352,6 +639,8 @@
             return carry
 
         lax.fori_loop(0, windows // 2, attend, 0)
+        if fused:
+            pass_weights(l)
 
         def middle(at, l=l):
             m = x[l, at, :] + dot(mixed[l, at, :], w_out[l]) + b_out[l : l + 1, :]
@@ -361,6 +650,8 @@
             gs[at, :] = m + b_red[l : l + 1, :]
 
         over_blocks(middle)
+        if fused:
+            have_weights(l)
 
         def feed(at, l=l):
             s = second[l, at, :]
@@ -388,7 +679,6 @@
 
     grid_to_windows(cot, side, True, put_cot)
     small[...] = jnp.zeros(small.shape, F32)
-    d_bexp[...] = jnp.zeros(d_bexp.shape, F32)
 
     for l in (1, 0):
 
@@ -408,21 +698,36 @@
                     cols = slice(c, c + chunk)
                     gh = dot_nt(g_low, w_red[i, l, cols, :])
                     gb = gh * slope[l, i, at, cols].astype(F32)
-                    d_bexp[i, l : l + 1, cols] += jnp.sum(gb, axis=0, keepdims=True)
+                    summed = jnp.sum(gb, axis=0, keepdims=True)
+                    d_bexp[i, 0:1, cols] += summed
                     gb_low[i, at, cols] = gb.astype(BF16)
                 gs[at, :] += dot_nt(gb_low[i, at, :], w_exp[i, l])
 
             over_shards(one)
 
+        d_bexp[...] = jnp.zeros(d_bexp.shape, F32)
         over_blocks(feed_back)
+        span = min(width, ff)
+        for n in range(shards * (ff // span)):
+            i, c = n // (ff // span), n % (ff // span) * span
+            small[l, SMALL_EXPAND + n : SMALL_EXPAND + n + 1, :span] = d_bexp[i, 0:1, c : c + span]
+        if l == 0:
+            hook(smalls[1].step, feeds[1].take, feeds[1].turn)
 
         def feed_weights(i, l=l):
             for c in range(0, ff, chunk):
                 cols = slice(c, c + chunk)
-                d_red[i, l, cols, :] = dot_tn(hidden[l, i, :, cols], gz[...]).astype(BF16)
-                d_exp[i, l, :, cols] = dot_tn(second[l], gb_low[i, :, cols]).astype(BF16)
+                d_feed[l, i, ff + c : ff + c + chunk, :] = dot_tn(hidden[l, i, :, cols], gz[...]).astype(BF16)
+            if blocked:
+                for c in range(0, ff, width):
+                    d_feed[l, i, c : c + width, :] = dot_tn(second[l], gb_low[i, :, c : c + width]).astype(BF16)
+            else:
+                d_feed[l, i, :ff, :] = dot_tn(gb_low[i], second[l]).astype(BF16)
 
         over_shards(feed_weights)
+        hook(feeds[l].send)
+        if l == 0:
+            hook(attns[1].take, attns[1].send, smalls[1].step)
 
         def middle_back(at, l=l):
             dmid, dgain, doffset = norm_back(mid[l, at, :], gain[l, 1:2, :], gs[at, :])
@@ -436,7 +741,10 @@
             go[at, :] = dot_nt(low, w_out[l]).astype(BF16)
 
         over_blocks(middle_back)
-        d_out[l] = dot_tn(mixed[l], gz[...]).astype(BF16)
+        hook(feeds[l].take, feeds[l].send)
+        if l == 0:
+            hook(feeds[1].widen, attns[1].take, attns[1].turn, smalls[1].step)
+        d_attn[l, 3 * width :, :] = dot_tn(mixed[l], gz[...]).astype(BF16)
         bias_sum[...] = jnp.zeros(bias_sum.shape, F32)
 
         def attend_back(i, carry, l=l):
@@ -475,11 +783,20 @@
                 dqkv[at, part * width : (part + 1) * width] = whole.astype(BF16)
             return carry
 
-        lax.fori_loop(0, windows // 2, attend_back, 0)
+        lax.fori_loop(0, windows // 4, attend_back, 0)
+        hook(feeds[l].take, feeds[l].send)
+        if l == 0:
+            hook(feeds[1].widen, attns[1].widen)
+        lax.fori_loop(windows // 4, windows // 2, attend_back, 0)
+        if l == 0:
+            hook(feeds[0].take, feeds[0].send)
 
         for c in range(3):
             cols = slice(c * width, (c + 1) * width)
-            d_in[l, :, cols] = dot_tn(normed[l], dqkv[:, cols]).astype(BF16)
+            d_attn[l, cols, :] = dot_tn(normed[l], dqkv[:, cols]).astype(BF16)
+        hook(attns[l].send)
+        if l == 0:
+            hook(feeds[1].widen, attns[1].widen)
 
         krow = iota((SLOTS, 128), 0)
         qlane = iota((SLOTS, 128), 1)
@@ -504,7 +821,13 @@
                         tile = tile + pltpu.roll(picked[r * PITCH : (r + 1) * PITCH], 128 - r * PITCH, 1)
                     for step in (1, 2, 4):
                         tile = jnp.where((iota(tile.shape, 0) & step) > 0, pltpu.roll(tile, 128 - step, 1), tile)
-                    d_table[l, 2 * h + s : 2 * h + s + 1, :] = jnp.sum(tile, axis=0, keepdims=True)
+                    n = 2 * h + s
+                    small[l, SMALL_TABLE + n // 3 : SMALL_TABLE + n // 3 + 1, n % 3 * 128 : (n % 3 + 1) * 128] = jnp.sum(
+                        tile, axis=0, keepdims=True
+                    )
+
+        if l == 0:
+            hook(attns[0].take, attns[0].send, feeds[0].take, feeds[0].turn)
 
         def input_back(at, l=l):
             ga = dot_nt(dqkv[at, :], w_in[l])
@@ -514,10 +837,16 @@
             gs[at, :] = g[at, :] + dx
 
         over_blocks(input_back)
+        hook(smalls[l].send)
         if l == 1:
+            hook(feeds[1].take, feeds[1].send, attns[1].take, attns[1].send)
             shifted_to_regular(gs, g, side)
         else:
+            hook(attns[0].take, attns[0].send, feeds[0].widen)
             windows_to_grid(gs, grad_tokens, side, False)
+            hook(smalls[0].step, attns[0].take, attns[0].turn, feeds[0].widen)
+            hook(smalls[0].step, attns[0].widen, smalls[0].step, feeds[0].widen, attns[1].widen)
+            hook(attns[0].widen, attns[0].widen)
 
 
 def table_lanes(table):
@@ -550,6 +879,7 @@
 
 
 def on_device(
+    mesh_shape,
     tokens,
     crop_ids,
     norm_gain,
@@ -567,50 +897,83 @@
 ):
     _, side, _, width = tokens.shape
     layers, _, ff = expand_weight.shape
-    w_exp = lax.all_gather(expand_weight, "mlp", axis=0)
-    w_red = lax.all_gather(reduce_weight, "mlp", axis=0)
-    b_exp = lax.all_gather(expand_bias, "mlp", axis=0).astype(F32)
-    shards = w_exp.shape[0]
+    win, shards = mesh_shape
     ids = jnp.broadcast_to(crop_ids[0, :, :, None].astype(F32), (side, side, 128))
     windows = (side // WIN) ** 2
     rows = windows * SLOTS
+    attn_rows, feed_rows = 4 * width, 2 * ff
+    fused = win % 4 == 0 and attn_rows % (16 * win * shards) == 0 and feed_rows % (16 * win) == 0
     vmem = pl.BlockSpec(memory_space=pltpu.VMEM)
+    hbm = pl.BlockSpec(memory_space=pl.ANY)
+    if fused:
+        w_exp, w_red = expand_weight, reduce_weight
+        b_exp = jnp.pad(expand_bias.astype(F32), ((0, 8 - layers), (0, 0)))
+    else:
+        w_exp = lax.all_gather(expand_weight, "mlp", axis=0)
+        w_red = lax.all_gather(reduce_weight, "mlp", axis=0)
+        b_exp = lax.all_gather(expand_bias, "mlp", axis=0).astype(F32)
+    scratch = [
+        pltpu.VMEM((layers, rows, width), F32),
+        pltpu.VMEM((layers, rows, width), BF16),
+        pltpu.VMEM((layers, rows, 3 * width), BF16),
+        pltpu.VMEM((layers, windows, GROUPS, SLOTS, GQ), F32),
+        pltpu.VMEM((layers, rows, width), BF16),
+        pltpu.VMEM((layers, rows, width), F32),
+        pltpu.VMEM((layers, rows, width), BF16),
+        pltpu.VMEM((layers, shards, rows, ff), BF16),
+        pltpu.VMEM((layers, shards, rows, ff), BF16),
+        pltpu.VMEM((rows, 128), F32),
+        pltpu.VMEM((GROUPS, SLOTS, GQ), F32),
+        pltpu.VMEM((GROUPS, SLOTS, GQ), F32),
+        pltpu.VMEM((rows, width), F32),
+        pltpu.VMEM((rows, width), F32),
+        pltpu.VMEM((rows, width), BF16),
+        pltpu.VMEM((shards, rows, ff), BF16),
+        pltpu.VMEM((rows, 3 * width), BF16),
+        pltpu.VMEM((rows, width), BF16),
+        pltpu.VMEM((shards, 8, ff), F32),
+    ]
+    small_shape = (layers, SMALL_ROWS, width)
+    if fused:
+        plane, depth = 2 * shards, win // 4
+        half = feed_rows // 2
+        scratch += [
+            pltpu.VMEM((layers, attn_rows, width), BF16),
+            pltpu.VMEM((layers, shards, feed_rows, width), BF16),
+            pltpu.VMEM(small_shape, F32),
+            pltpu.VMEM((shards, layers, width, ff), BF16),
+            pltpu.VMEM((shards, 8, ff), F32),
+            pltpu.VMEM((shards, layers, ff, width), BF16),
+            pltpu.VMEM((layers, shards, half, width), BF16),
+            pltpu.VMEM((layers, shards - 1, half, width), BF16),
+            pltpu.VMEM((layers, 1, half // 2, width), BF16),
+            pltpu.VMEM((layers, depth - 1, half // 2 // depth, width), BF16),
+            pltpu.VMEM((layers, 1, attn_rows // 2, width), BF16),
+            pltpu.VMEM((layers, plane - 1, attn_rows // 2 // plane, width), BF16),
+            pltpu.VMEM((layers, depth - 1, attn_rows // 2 // plane // depth, width), BF16),
+            pltpu.VMEM((layers, 2) + small_shape[1:], F32),
+            pltpu.VMEM((layers, plane) + small_shape[1:], F32),
+            pltpu.VMEM((layers, depth) + small_shape[1:], F32),
+            pltpu.SemaphoreType.DMA((7,)),
+            pltpu.SemaphoreType.DMA((96,)),
+            pltpu.SemaphoreType.DMA((96,)),
+        ]
     outs = pl.pallas_call(
-        functools.partial(kernel, side),
+        functools.partial(kernel, side, mesh_shape if fused else None),
         out_shape=(
             jax.ShapeDtypeStruct(tokens.shape[1:], BF16),
             jax.ShapeDtypeStruct(tokens.shape[1:], BF16),
-            jax.ShapeDtypeStruct(input_proj.shape, BF16),
-            jax.ShapeDtypeStruct(output_proj.shape, BF16),
-            jax.ShapeDtypeStruct(w_exp.shape, BF16),
-            jax.ShapeDtypeStruct(w_red.shape, BF16),
-            jax.ShapeDtypeStruct((layers, 8, width), F32),
-            jax.ShapeDtypeStruct((layers, 2 * HEADS, 128), F32),
-            jax.ShapeDtypeStruct(b_exp.shape, F32),
+            jax.ShapeDtypeStruct((layers, attn_rows, width), BF16),
+            jax.ShapeDtypeStruct((layers, feed_rows, width) if fused else (layers, shards, feed_rows, width), BF16),
+            jax.ShapeDtypeStruct(small_shape, F32),
         ),
-        in_specs=[vmem] * 14,
-        out_specs=[vmem] * 9,
-        scratch_shapes=[
-            pltpu.VMEM((layers, rows, width), F32),
-            pltpu.VMEM((layers, rows, width), BF16),
-            pltpu.VMEM((layers, rows, 3 * width), BF16),
-            pltpu.VMEM((layers, windows, GROUPS, SLOTS, GQ), F32),
-            pltpu.VMEM((layers, rows, width), BF16),
-            pltpu.VMEM((layers, rows, width), F32),
-            pltpu.VMEM((layers, rows, width), BF16),
-            pltpu.VMEM((layers, shards, rows, ff), BF16),
-            pltpu.VMEM((layers, shards, rows, ff), BF16),
-            pltpu.VMEM((rows, 128), F32),
-            pltpu.VMEM((GROUPS, SLOTS, GQ), F32),
-            pltpu.VMEM((GROUPS, SLOTS, GQ), F32),
-            pltpu.VMEM((rows, width), F32),
-            pltpu.VMEM((rows, width), F32),
-            pltpu.VMEM((rows, width), BF16),
-            pltpu.VMEM((shards, rows, ff), BF16),
-            pltpu.VMEM((rows, 3 * width), BF16),
-            pltpu.VMEM((rows, width), BF16),
-        ],
-        compiler_params=pltpu.CompilerParams(vmem_limit_bytes=64 * 1024 * 1024),
+        in_specs=[vmem] * 9 + ([hbm, vmem, hbm] if fused else [vmem] * 3) + [vmem] * 2,
+        out_specs=[vmem] * 2 + ([hbm] * 2 if fused else [vmem] * 2) + [vmem],
+        scratch_shapes=scratch,
+        compiler_params=pltpu.CompilerParams(
+            vmem_limit_bytes=64 * 1024 * 1024,
+            **(dict(collective_id=0, has_side_effects=True) if fused else {}),
+        ),
     )(
         tokens[0],
         ids,
@@ -627,12 +990,19 @@
         reduce_bias,
         cotangent[0],
     )
-    out, grad_tokens, d_in, d_out, d_exp, d_red, small, d_table, d_bexp = outs
-    d_in, d_out = lax.psum((d_in, d_out), ("win", "mlp"))
-    small, d_table = lax.psum((small, d_table), ("win", "mlp"))
-    d_exp = lax.psum(lax.psum_scatter(d_exp, "mlp", scatter_dimension=0, tiled=False), "win")
-    d_red = lax.psum(lax.psum_scatter(d_red, "mlp", scatter_dimension=0, tiled=False), "win")
-    d_bexp = lax.psum(lax.psum_scatter(d_bexp, "mlp", scatter_dimension=0, tiled=False), "win")
+    out, grad_tokens, d_attn, d_feed, small = outs
+    if not fused:
+        d_attn, small = lax.psum((d_attn, small), ("win", "mlp"))
+        d_feed = lax.psum(lax.psum_scatter(d_feed, "mlp", scatter_dimension=1, tiled=False), "win")
+    d_in = jnp.concatenate([d_attn[:, c * width : (c + 1) * width] for c in range(3)], axis=2)
+    if ff % width == 0:
+        d_exp = jnp.concatenate([d_feed[:, c : c + width] for c in range(0, ff, width)], axis=2)
+    else:
+        d_exp = d_feed[:, :ff].swapaxes(1, 2)
+    span = min(width, ff)
+    d_bexp = small[:, SMALL_EXPAND : SMALL_EXPAND + shards * (ff // span), :span].reshape(layers, shards, ff)
+    d_bexp = lax.dynamic_index_in_dim(d_bexp, lax.axis_index("mlp"), 1, keepdims=False)
+    d_table = small[:, SMALL_TABLE : SMALL_TABLE + 8].reshape(layers, 2 * HEADS, 128)
     return (
         out[None],
         grad_tokens[None],
@@ -641,11 +1011,11 @@
         d_in.astype(F32),
         small[:, 4:6],
         lanes_table(d_table),
-        d_out.astype(F32),
+        d_attn[:, 3 * width :].astype(F32),
         small[:, 6],
         d_exp.astype(F32),
         d_bexp,
-        d_red.astype(F32),
+        d_feed[:, ff:].astype(F32),
         small[:, 7],
     )
 
@@ -669,7 +1039,7 @@
         tokens,
     )
     return jax.shard_map(
-        on_device,
+        functools.partial(on_device, (mesh.shape["win"], mesh.shape["mlp"])),
         mesh=mesh,
         in_specs=placed,
         out_specs=(

time: 542 us -> 212 us (0.39)
  waiting for transfers between devices: 298 us -> 0 us
  blocking collectives: 85 us -> 0 us
  Pallas kernels: 127 us -> 187 us
  between operations: 14.4 us -> 0.83 us
  local copies, waits for them, and re-layouts: 6.95 us -> 14.3 us
    psum x2 -> x0, waiting for transfers between devices: 155 us -> none  [the longest x1 97.4 us: on_device(): lax.psum(lax.psum_scatter(d_exp, 'mlp', scatter_dimension=0, tiled=False)...]
    reduce_scatter x2 -> x0, waiting for transfers between devices: 71.1 us -> none  [the longest x1 37.5 us: on_device(): lax.psum_scatter(d_red, 'mlp', scatter_dimension=0, tiled=False)]
    psum x2 -> x0, blocking collectives: 70.9 us -> none  [the longest x1 40.2 us: on_device(): small, d_table = lax.psum((small, d_table), ('win', 'mlp'))]
    all_gather x2 -> x0, waiting for transfers between devices: 69.4 us -> none  [the longest x1 37.6 us: on_device(): w_red = lax.all_gather(reduce_weight, 'mlp', axis=0)]
    pallas_call x1, Pallas kernels: 127 us -> 187 us  [on_device(): pl.pallas_call(functools.partial(kernel, side, mesh_shape if fused else N...]
    unnamed x1 -> x0, blocking collectives: 8.84 us -> none
  transfers between devices with their start and end apart: 6 -> 0, of which waited for: 6 -> 0; matrix products, arithmetic and copies ran while one was open for 2% -> 0% of each run, Pallas kernels for 0% -> 0%
where the time goes in v2:
time: 212 us; the launch traced here: 211 us
  Pallas kernels  187 us (88%)
  local copies, waits for them, and re-layouts  14.3 us (7%)
  other arithmetic  8.78 us (4%)
    pallas_call x1, Pallas kernels, on_device(): pl.pallas_call(functools.partial(kernel, side, mesh_shape if fused else N...  187 us
    unnamed x18, local copies, waits for them, and re-layouts  4.98 us

profile of v2, /device:TPU:0, one launch (start us, length us, event | category | flops | bytes accessed | tf_op | source)
XLA Modules:
  0.0 211.0 jit_solution(4400439698046821659)
XLA Ops:
  0.6 0.7 convert_element_type.33
  1.4 1.3 pad_convert_fusion.refs_10_
  2.7 0.9 reshape.58
  3.6 0.3 copy.61
  3.9 0.1 copy.46
  4.0 0.1 copy.45
  4.0 0.1 slice.130
  4.2 0.3 copy.60
  4.5 0.1 copy.43
  4.6 0.1 copy.42
  4.7 0.1 maximum_bitcast_fusion
  4.8 0.6 copy.47
  5.4 1.0 broadcast_in_dim.11.refs_1_
  6.4 187.1 %shard_map.237 = (bf16[28,28,384]{2,1,0:T(8,128)(2,1)}, bf16[28,28,384]{2,1,0:T(8,128)(2,1)}, bf16[2,1536,384]{2,1,0:T(8,128)(2,1)}, bf16[2,1536,384]{2,1,0:T(8,128)(2,1)}, f32[2,24,384]{2,1,0:T(8,128)}) custom-call(bf16[28,28,384]{2,1,0:T(8,128)(2,1)} %bitcast.45, f32[28,28,128]{2,1,0:T(8,128)} %broadcast_in_dim.11.refs_1_, f32[2,2,384]{2,1,0:T(2,128)} %refs_2_.1, ...), custom_call_target="tpu_custom_call" | custom-call | tf_op jit(solution)/shard_map/pallas_call | solution.py:961
  193.5 0.0 copy-start
  193.5 0.9 fusion.1
  194.4 0.6 copy.72
  195.0 0.6 copy.73
  195.6 0.7 slice.127
  196.3 0.6 copy.71
  196.9 1.5 fusion.2
  198.4 0.7 slice.112
  199.2 0.1 slice.135
  199.3 0.1 pad_maximum_fusion.3
  199.4 0.1 slice.139
  199.5 0.1 pad_maximum_fusion.2
  199.5 0.1 copy.51
  199.7 0.1 copy.49
  199.9 0.7 copy.53
  200.6 1.4 fusion
  201.9 0.0 copy-done
  202.0 1.6 slice_convert_fusion
  203.5 0.0 copy-start.1
  203.5 1.6 maximum_convert_fusion.1
  205.1 0.9 copy-done.1
  206.0 1.3 slice_convert_fusion.1
  207.3 0.0 copy-start.3
  207.3 0.0 copy-start.2
  207.3 2.0 maximum_convert_fusion
  209.3 0.0 copy-done.3
  209.3 0.8 copy.76
  210.2 0.0 copy-done.2
  210.2 0.8 copy.77
  (17 shorter events, 0.2 us)
Async XLA Ops:
  193.5 8.5 %copy-start = (bf16[2,1536,384]{2,1,0:T(8,128)(2,1)S(1)}, bf16[2,1536,384]{2,1,0:T(8,128)(2,1)}, u32[]{:S(2)}) copy-start(bf16[2,1536,384]{2,1,0:T(8,128)(2,1)} %get-tuple-element.22) | copy-start | bytes 7077892
  203.5 2.5 %copy-start.1 = (bf16[2,1536,384]{2,1,0:T(8,128)(2,1)S(1)}, bf16[2,1536,384]{2,1,0:T(8,128)(2,1)}, u32[]{:S(2)}) copy-start(bf16[2,1536,384]{2,1,0:T(8,128)(2,1)} %get-tuple-element.21) | copy-start | bytes 7077892
  207.3 2.0 copy-start.3
  207.3 2.9 %copy-start.2 = (bf16[28,28,384]{2,1,0:T(8,128)(2,1)S(1)}, bf16[28,28,384]{2,1,0:T(8,128)(2,1)}, u32[]{:S(2)}) copy-start(bf16[28,28,384]{2,1,0:T(8,128)(2,1)} %get-tuple-element.19) | copy-start | bytes 1806340

commit v3 on v1

v3 whole, which is shorter than its diff:
```python
import functools

import jax
import jax.numpy as jnp
from jax import lax
from jax.experimental import pallas as pl
from jax.experimental.pallas import tpu as pltpu
from jax.sharding import PartitionSpec as P

HEADS = 12
HEAD_DIM = 32
WIN = 7
SHIFT = 3
SPAN_SIDE = 2 * WIN - 1

EPS = 1e-05
MASKED = -1e30

PITCH = 8
SLOTS = WIN * PITCH
GROUP = 4
GROUPS = HEADS // GROUP
GLANES = GROUP * HEAD_DIM
GQ = GROUP * SLOTS

F32 = jnp.float32
BF16 = jnp.bfloat16

ERF_P = 0.39
ERF_C = (
    0.22003399505358215,
    0.22002241291251284,
    0.20367769093249805,
    0.16514655576456758,
    0.15214218925854978,
    -0.024768996902218943,
    0.20836931643666226,
    -0.19248882577712367,
    0.04786540601145673,
)


LOG2E = 1.4426950408889634
BELL = 0.3989422804014327


def dot(a, b):
    return lax.dot_general(a, b, (((1,), (0,)), ((), ())), preferred_element_type=F32)


def dot_nt(a, b):
    return lax.dot_general(a, b, (((1,), (1,)), ((), ())), preferred_element_type=F32)


def dot_tn(a, b):
    return lax.dot_general(a, b, (((0,), (0,)), ((), ())), preferred_element_type=F32)


def gelu_pair(u):
    bell = jnp.exp2(u * u * (-0.5 * LOG2E))
    size = jnp.abs(u)
    t = 1.0 / (1.0 + (ERF_P * 0.5**0.5) * size)
    poly = 0.5 * ERF_C[-1] * t + 0.5 * ERF_C[-2]
    for coef in ERF_C[-3::-1]:
        poly = poly * t + 0.5 * coef
    tail = bell * (t * poly)
    phi = jnp.where(u < 0, tail, 1.0 - tail)
    return jnp.maximum(u, 0.0) - size * tail, phi + u * (bell * BELL)


def norm_stats(v):
    centred = v - jnp.mean(v, axis=-1, keepdims=True)
    rstd = lax.rsqrt(jnp.mean(centred * centred, axis=-1, keepdims=True) + EPS)
    return centred * rstd, rstd


def norm_back(v, gain, upstream):
    xhat, rstd = norm_stats(v)
    scaled = upstream * gain
    inner = (
        scaled
        - jnp.mean(scaled, axis=-1, keepdims=True)
        - xhat * jnp.mean(scaled * xhat, axis=-1, keepdims=True)
    )
    return rstd * inner, jnp.sum(upstream * xhat, axis=0, keepdims=True), jnp.sum(upstream, axis=0, keepdims=True)


def iota(shape, dim):
    return lax.broadcasted_iota(jnp.int32, shape, dim)


def expand_heads(rows):
    head = iota(rows.shape, 1) // HEAD_DIM
    return jnp.concatenate([jnp.where(head == j, rows, 0.0) for j in range(GROUP)], axis=0).astype(BF16)


def fold_heads(rows):
    head = iota((SLOTS, GLANES), 1) // HEAD_DIM
    out = rows[:SLOTS]
    for j in range(1, GROUP):
        out = jnp.where(head == j, rows[j * SLOTS : (j + 1) * SLOTS], out)
    return out


def by_window(parts):
    return jnp.concatenate(
        [jnp.concatenate(parts[w * GROUPS : (w + 1) * GROUPS], axis=1) for w in range(BLOCK_WINDOWS)], axis=0
    )


def window_row(per_side, wr, wc, r):
    return pl.multiple_of((wr * per_side + wc) * SLOTS + r * PITCH, PITCH)


def grid_to_windows(src, side, shifted, emit):
    per_side = side // WIN

    def step(wr, carry):
        for r in range(WIN):
            row = lax.rem(wr * WIN + r + (SHIFT if shifted else 0), side)
            line = src[row].astype(F32)
            width = line.shape[1]
            line = jnp.concatenate([line, jnp.zeros((32 - side, width), F32)], axis=0)
            if shifted:
                i = iota(line.shape, 0)
                line = jnp.where(i < side - SHIFT, pltpu.roll(line, 32 - SHIFT, 0), pltpu.roll(line, side - SHIFT, 0))
            for wc in range(per_side):
                part = line if wc == 0 else pltpu.roll(line, 32 - WIN * wc, 0)
                part = part[:PITCH]
                part = jnp.where(iota(part.shape, 0) < WIN, part, 0.0)
                emit(wr, wc, r, part)
        return carry

    lax.fori_loop(0, per_side, step, 0)


def windows_to_grid(src, dst, side, shifted):
    per_side = side // WIN

    def step(wr, carry):
        for r in range(WIN):
            row = lax.rem(wr * WIN + r + (SHIFT if shifted else 0), side)
            width = src.shape[1]
            line = jnp.zeros((32, width), F32)
            i = iota(line.shape, 0)
            for wc in range(per_side):
                tile = src[pl.ds(window_row(per_side, wr, wc, r), PITCH), :]
                tile = jnp.concatenate([tile, jnp.zeros((32 - PITCH, width), F32)], axis=0)
                if wc:
                    tile = pltpu.roll(tile, WIN * wc, 0)
                line = jnp.where((i >= WIN * wc) & (i < WIN * (wc + 1)), tile, line)
            if shifted:
                line = jnp.where(i < SHIFT, pltpu.roll(line, 32 - side + SHIFT, 0), pltpu.roll(line, SHIFT, 0))
            dst[row] = line[:side].astype(dst.dtype)
        return carry

    lax.fori_loop(0, per_side, step, 0)


def regular_to_shifted(src, dst, side):
    per_side = side // WIN

    def step(wr, carry):
        below = lax.rem(wr + 1, per_side)
        for r in range(WIN):
            sr, srr = (wr, r + SHIFT) if r + SHIFT < WIN else (below, r + SHIFT - WIN)
            for wc in range(per_side):
                here = src[pl.ds(window_row(per_side, sr, wc, srr), PITCH), :]
                right = src[pl.ds(window_row(per_side, sr, (wc + 1) % per_side, srr), PITCH), :]
                i = iota(here.shape, 0)
                tile = jnp.where(
                    i < WIN - SHIFT,
                    pltpu.roll(here, PITCH - SHIFT, 0),
                    jnp.where(i < WIN, pltpu.roll(right, WIN - SHIFT, 0), 0.0),
                )
                dst[pl.ds(window_row(per_side, wr, wc, r), PITCH), :] = tile
        return carry

    lax.fori_loop(0, per_side, step, 0)


def shifted_to_regular(src, dst, side):
    per_side = side // WIN

    def step(wr, carry):
        above = lax.rem(wr + per_side - 1, per_side)
        for r in range(WIN):
            sr, srr = (wr, r - SHIFT) if r >= SHIFT else (above, r - SHIFT + WIN)
            for wc in range(per_side):
                here = src[pl.ds(window_row(per_side, sr, wc, srr), PITCH), :]
                left = src[pl.ds(window_row(per_side, sr, (wc + per_side - 1) % per_side, srr), PITCH), :]
                i = iota(here.shape, 0)
                tile = jnp.where(
                    i < SHIFT,
                    pltpu.roll(left, PITCH - (WIN - SHIFT), 0),
                    jnp.where(i < WIN, pltpu.roll(here, SHIFT, 0), 0.0),
                )
                dst[pl.ds(window_row(per_side, wr, wc, r), PITCH), :] = tile
        return carry

    lax.fori_loop(0, per_side, step, 0)


BLOCK_WINDOWS = 4
ROWS_BLOCK = BLOCK_WINDOWS * SLOTS
JOBS = [
    (w, grp, slice(w * SLOTS, (w + 1) * SLOTS), slice(grp * GLANES, (grp + 1) * GLANES))
    for w in range(BLOCK_WINDOWS)
    for grp in range(GROUPS)
]
SMALL = {"gain1": 0, "gain2": 1, "bias1": 2, "bias2": 3, "query": 4, "value": 5, "output": 6, "reduce": 7}
SMALL_TABLE = 8
SMALL_EXPAND = 16
SMALL_ROWS = 24
ADD_ROWS = 96
PART = 3
ATTN_PARTS = (((0, 2), (2, 1)), ((0, 3),))


def table_spans():
    spans = []
    for dr in range(SPAN_SIDE):
        at = PITCH * (dr - WIN + 1)
        spans.append((at % 128, dr * SPAN_SIDE + WIN - 1, WIN, 0))
        spans.append(((at - PITCH) % 128 + PITCH - WIN + 1, dr * SPAN_SIDE, WIN - 1, 1))
    return spans


class Links:
    def __init__(self, mesh_shape, send_sem, recv_sem):
        self.win, self.mlp = mesh_shape
        self.send_sem, self.recv_sem = send_sem, recv_sem
        w, m = lax.axis_index("win"), lax.axis_index("mlp")
        self.core, self.x, self.z, self.m = lax.rem(w, 2), lax.rem(lax.div(w, 2), 2), lax.div(w, 4), m
        self.depth = self.win // 4
        self.groups = {
            "core": (2, self.core, lambda q: self.at(core=q)),
            "x": (2, self.x, lambda q: self.at(x=q)),
            "z": (self.depth, self.z, lambda q: self.at(z=q)),
            "mlp": (self.mlp, m, lambda q: self.at(m=q)),
            "plane": (
                2 * self.mlp,
                self.x * self.mlp + m,
                lambda q: self.at(x=lax.div(q, self.mlp), m=lax.rem(q, self.mlp)),
            ),
        }
        self.used = 0

    def at(self, core=None, x=None, z=None, m=None):
        core = self.core if core is None else core
        x = self.x if x is None else x
        z = self.z if z is None else z
        m = self.m if m is None else m
        return ((z * 2 + x) * 2 + core, m)

    def peers(self, group):
        size, me, _ = self.groups[group]
        return [(d, lax.rem(me + d, size)) for d in range(1, size)]

    def me(self, group):
        return self.groups[group][1]

    def size(self, group):
        return self.groups[group][0]

    def greet(self):
        sem = pltpu.get_barrier_semaphore()
        for group in ("core", "plane", "z"):
            for _, q in self.peers(group):
                pl.semaphore_signal(
                    sem, inc=1, device_id=self.groups[group][2](q), device_id_type=pl.DeviceIdType.MESH
                )

    def meet(self):
        pl.semaphore_wait(pltpu.get_barrier_semaphore(), sum(self.size(g) - 1 for g in ("core", "plane", "z")))

    def reserve(self, count):
        first = self.used
        self.used += count
        return first

    def copy(self, group, q, src, dst, n):
        return pltpu.make_async_remote_copy(
            src_ref=src,
            dst_ref=dst,
            send_sem=self.send_sem.at[n],
            recv_sem=self.recv_sem.at[n],
            device_id=self.groups[group][2](q),
            device_id_type=pl.DeviceIdType.MESH,
        )


def add_rows(dst, sources, start, count):
    step = next(n for n in (ADD_ROWS, 64, 48, 32, 16) if count % n == 0)

    def one(i, carry):
        at = pl.multiple_of(start + i * step, 16)
        total = dst[pl.ds(at, step), :].astype(F32)
        for source in sources:
            total = total + source[pl.ds(pl.multiple_of(i * step, 16), step), :].astype(F32)
        dst[pl.ds(at, step), :] = total.astype(dst.dtype)
        return carry

    lax.fori_loop(0, count // step, one, 0)


def flow_table(mesh_shape, width, ff):
    part = 4 * width // PART
    flows = {}
    for l in (1, 0):
        flows[f"R{l}"] = (l, ff, ff, ("core", "mlp", "x", "z"))
        flows[f"E{l}"] = (l, 0, ff, ("core", "mlp", "x", "z"))
        for first, count in ATTN_PARTS[l]:
            flows[f"A{first + count - 1}{l}"] = (l, first * part, count * part, ("core", "plane", "z"))
    win, mlp = mesh_shape
    sizes = {"core": 2, "x": 2, "z": win // 4, "mlp": mlp, "plane": 2 * mlp}
    shapes = {}
    for name, (_, _, rows, stages) in flows.items():
        slots = mlp if "mlp" in stages else 1
        shapes[name] = []
        for stage in stages:
            if stage == "mlp":
                slots = 1
            else:
                rows //= sizes[stage]
            shapes[name].append((sizes[stage] - 1, slots, rows, width))
    return flows, shapes


class Flow:
    def __init__(self, links, staged, out, first, rows, stages, buffers, local_sem):
        self.links, self.staged, self.out, self.local_sem = links, staged, out, local_sem
        self.stages, self.buffers = stages, buffers
        self.spans = [(first, rows)]
        for stage in stages:
            first, rows = self.spans[-1]
            if stage != "mlp":
                rows = rows // links.size(stage)
                first = first + links.me(stage) * rows
            self.spans.append((first, rows))
        self.down = [n for n in reversed(range(len(stages))) if stages[n] != "mlp"]
        self.steps = len(stages) + len(self.down)
        self.sems = [
            links.reserve(links.size(stages[n]) - 1) for n in list(range(len(stages))) + self.down
        ]
        self.at = 0
        self.done = False

    def slots(self, n):
        return self.staged.shape[0] if "mlp" in self.stages[n:] else 1

    def copies(self, k):
        links = self.links
        made = []
        if k < len(self.stages):
            stage = self.stages[k]
            for d, q in links.peers(stage):
                first, rows = self.spans[k]
                if stage == "mlp":
                    src = self.staged.at[pl.ds(d, 1), pl.ds(pl.multiple_of(first, 16), rows)]
                else:
                    rows = self.spans[k + 1][1]
                    src = self.staged.at[pl.ds(0, self.slots(k)), pl.ds(pl.multiple_of(first + q * rows, 16), rows)]
                made.append(links.copy(stage, q, src, self.buffers[k].at[d - 1], self.sems[k] + d - 1))
            return made
        n = self.down[k - len(self.stages)]
        first, rows = self.spans[n + 1]
        mine = pl.ds(pl.multiple_of(first, 16), rows)
        src = self.staged.at[0, mine] if k == len(self.stages) else self.out.at[mine]
        for d, q in links.peers(self.stages[n]):
            made.append(links.copy(self.stages[n], q, src, self.out.at[mine], self.sems[k] + d - 1))
        return made

    def local(self):
        first, rows = self.spans[-1]
        mine = pl.ds(pl.multiple_of(first, 16), rows)
        return pltpu.make_async_copy(self.staged.at[0, mine], self.out.at[mine], self.local_sem)

    def advance(self):
        k = self.at
        if k:
            for copy in self.copies(k - 1):
                copy.wait()
            if k - 1 < len(self.stages):
                first, rows = self.spans[k]
                for slot in range(self.slots(k)):
                    add_rows(
                        self.staged.at[slot],
                        [self.buffers[k - 1].at[d - 1, slot] for d, _ in self.links.peers(self.stages[k - 1])],
                        first,
                        rows,
                    )
            elif k - 1 == len(self.stages):
                self.local().wait()
        if k < self.steps:
            if k == len(self.stages):
                self.local().start()
            for copy in self.copies(k):
                copy.start()
        else:
            self.done = True
        self.at += 1


class SmallFlow:
    def __init__(self, links, value, buffers, out):
        self.links, self.value, self.buffers, self.out = links, value, buffers, out
        self.stages = ("core", "plane", "z")
        self.sems = [links.reserve(links.size(stage) - 1) for stage in self.stages]
        self.at = 0
        self.done = False

    def copies(self, k):
        stage, buffer = self.stages[k], self.buffers[k]
        me = self.links.me(stage)
        return [
            self.links.copy(stage, q, buffer.at[me], buffer.at[me], self.sems[k] + d - 1)
            for d, q in self.links.peers(stage)
        ]

    def advance(self):
        k = self.at
        total = self.value[...] if k == 0 else None
        if k:
            for copy in self.copies(k - 1):
                copy.wait()
            buffer = self.buffers[k - 1]
            total = buffer[0]
            for j in range(1, buffer.shape[0]):
                total = total + buffer[j]
        if k < len(self.stages):
            self.buffers[k][self.links.me(self.stages[k])] = total
            for copy in self.copies(k):
                copy.start()
        else:
            self.out[...] = total
            self.done = True
        self.at += 1


PLAN = {
    (1, "feed_back"): {1: ("R1",)},
    (1, "middle_back"): {3: ("E1",)},
    (1, "attend_back0"): {0: ("R1",)},
    (1, "attend_back2"): {1: ("R1", "E1")},
    (1, "input_back"): {2: ("A21",)},
    (1, "placed"): {None: ("E1", "R1", "S1")},
    (0, "feed_back"): {2: ("R0", "E1", "A21"), 3: ("S1", "R1")},
    (0, "middle_back"): {3: ("E0", "E1", "R1", "R0")},
    (0, "attend_back0"): {0: ("A21", "R1")},
    (0, "group0"): {None: ("S1",)},
    (0, "attend_back1"): {1: ("E1",)},
    (0, "attend_back2"): {1: ("E0", "R0", "E1", "A10", "A21")},
    (0, "input_back"): {0: ("A20",), 3: ("E0",)},
    (0, "placed"): {None: ("R0",)},
}
LAST = ("S0", "A10", "E0", "A21", "R0", "A20", "A21", "A10", "S0", "E0", "R0", "A20", "R0", "A10", "E0", "S0", "A20", "E0", "A10", "A20", "A10", "A20")


def kernel(side, mesh_shape, *refs):
    refs = list(refs)

    def take(n):
        got = refs[:n]
        del refs[:n]
        return got

    tokens, ids, gain, offset, w_in, b_in, table, w_out, b_out, w_exp, b_exp, w_red, b_red, cot = take(14)
    fused = mesh_shape is not None
    out, grad_tokens, d_attn, d_feed, small = take(5)
    (x, normed, qkv, probs, mixed, mid, second, hidden, slope) = take(9)
    (keys, bias, bias_sum, g, gs, gz, gb_low, dqkv, go, d_bexp, turn, spread) = take(12)
    flows = {}
    if fused:
        out_attn, out_feed, out_small = d_attn, d_feed, small
        d_attn, d_feed, small = take(3)
        local_exp, local_bexp, local_red = w_exp, b_exp, w_red
        w_exp, b_exp, w_red = take(3)
        small_buffers = take(3)
        flow_rows, shapes = flow_table(mesh_shape, x.shape[2], local_exp.shape[2])
        landing = {name: take(len(shapes[name])) for name in flow_rows}
        local_sems, send_sem, recv_sem = take(3)
        links = Links(mesh_shape, send_sem, recv_sem)
        for n, (name, (l, first, count, stages)) in enumerate(flow_rows.items()):
            feed_flow = "mlp" in stages
            flows[name] = Flow(
                links,
                d_feed.at[l] if feed_flow else d_attn.at[pl.ds(l, 1)],
                out_feed.at[l] if feed_flow else out_attn.at[l],
                first,
                count,
                stages,
                landing[name],
                local_sems.at[3 + n],
            )
        for l in (1, 0):
            flows[f"S{l}"] = SmallFlow(links, small.at[l], [b.at[l] for b in small_buffers], out_small.at[l])

    def advance(*names):
        if fused:
            for name in names:
                flows[name].advance()

    def ticks(l, phase, i=None):
        for iteration, names in PLAN.get((l, phase), {}).items():
            if i is None:
                advance(*names)
            elif fused:
                pl.when(i == iteration)(functools.partial(advance, *names))

    per_side = side // WIN
    windows = per_side * per_side
    rows = windows * SLOTS
    blocks = rows // ROWS_BLOCK
    shards, _, width, ff = w_exp.shape
    chunk = 256 if ff % 256 == 0 else ff
    blocked = ff % width == 0
    part_rows = 4 * width // PART

    if fused:
        links.greet()
        own = [
            pltpu.make_async_copy(local_exp, w_exp.at[0], local_sems.at[0]),
            pltpu.make_async_copy(local_red, w_red.at[0], local_sems.at[1]),
        ]
        for copy in own:
            copy.start()
        b_exp[0, 0:2, :] = local_bexp[...].astype(F32)
        halves = (
            pl.ds(pl.multiple_of(links.core * (width // 2), 16), width // 2),
            pl.ds(pl.multiple_of(links.core * (ff // 2), 16), ff // 2),
        )
        weights = ((local_exp, w_exp, halves[0]), (local_red, w_red, halves[1]))
        fetch_sems = links.reserve(4 * (shards - 1))
        pass_sems = links.reserve(4 * (shards - 1))
        bias_sems = links.reserve(shards - 1)

        def fetches(l, n):
            source, dest, half = weights[n]
            return [
                links.copy("mlp", q, source.at[l, half], dest.at[shards - d, l, half], fetch_sems + (2 * l + n) * (shards - 1) + d - 1)
                for d, q in links.peers("mlp")
            ]

        def passes(l, n):
            _, dest, half = weights[n]
            ((_, sibling),) = links.peers("core")
            return [
                links.copy("core", sibling, dest.at[d, l, half], dest.at[d, l, half], pass_sems + (2 * l + n) * (shards - 1) + d - 1)
                for d, _ in links.peers("mlp")
            ]

        def bias_fetches():
            return [links.copy("mlp", q, b_exp.at[0], b_exp.at[shards - d], bias_sems + d - 1) for d, q in links.peers("mlp")]

        def fetch_all():
            for copy in bias_fetches():
                copy.start()
            for l in range(2):
                for n in range(2):
                    for copy in fetches(l, n):
                        copy.start()

        def pass_on(l, n):
            for copy in fetches(l, n):
                copy.wait()
            for copy in passes(l, n):
                copy.start()

        def passed(l, n):
            for copy in passes(l, n):
                copy.wait()

    def over_blocks(body, tick=None):
        def step(i, carry):
            body(pl.ds(pl.multiple_of(i * ROWS_BLOCK, ROWS_BLOCK), ROWS_BLOCK))
            if tick:
                ticks(*tick, i)
            return carry

        lax.fori_loop(0, blocks, step, 0)

    def put_tokens(wr, wc, r, tile):
        x[0, pl.ds(window_row(per_side, wr, wc, r), PITCH), :] = tile

    grid_to_windows(tokens, side, False, put_tokens)
    if fused:
        links.meet()
        fetch_all()

    for l in range(2):
        shifted = l == 1

        def put_keys(wr, wc, r, tile, shifted=shifted):
            lane = iota(tile.shape, 1).astype(F32)
            slot = iota(tile.shape, 0)
            label = tile
            if shifted:
                row_at = wr * WIN + r
                row_label = jnp.where(row_at >= side - WIN, 1, 0) + jnp.where(row_at >= side - SHIFT, 1, 0)
                col_at = wc * WIN + slot
                col_label = jnp.where(col_at >= side - WIN, 1, 0) + jnp.where(col_at >= side - SHIFT, 1, 0)
                label = label + (12 * row_label + 4 * col_label).astype(F32)
            hot = jnp.where((lane == label) & (slot < WIN), 1.0, 0.0)
            keys[pl.ds(window_row(per_side, wr, wc, r), PITCH), :] = hot

        grid_to_windows(ids, side, shifted, put_keys)

        krow = iota((SLOTS, 128), 0)
        qlane = iota((SLOTS, 128), 1)
        ahead = (qlane & (PITCH - 1)) >= (krow & (PITCH - 1))
        turn[...] = jnp.zeros(turn.shape, F32)
        for lane, entry, count, s in table_spans():
            turn[s, lane : lane + count, :HEADS] = table[l, entry : entry + count, :]
        for s in range(2):
            spread[s] = turn[s].T[: spread.shape[1]]
        for grp in range(GROUPS):
            low = jnp.zeros((SLOTS, 128), F32)
            high = jnp.zeros((SLOTS, 128), F32)
            for j in range(GROUP):
                h = grp * GROUP + j
                both = [
                    pltpu.roll(
                        jnp.broadcast_to(spread[s, h : h + 1, :], (SLOTS, 128)),
                        0,
                        1,
                        stride=1,
                        stride_axis=0,
                    )
                    for s in range(2)
                ]
                one = jnp.where(ahead, both[0], both[1])
                at = j * SLOTS
                if at < 128:
                    moved = pltpu.roll(one, at, 1) if at else one
                    low = jnp.where((qlane >= at) & (qlane < at + SLOTS), moved, low)
                if at + SLOTS > 128:
                    moved = pltpu.roll(one, (at - 128) % 128, 1)
                    high = jnp.where((qlane >= at - 128) & (qlane < at - 128 + SLOTS), moved, high)
            bias[grp, :, :128] = low
            bias[grp, :, 128:] = high[:, : GQ - 128]

        bias_row = jnp.concatenate(
            [b_in[l, 0:1, :], jnp.zeros((1, width), F32), b_in[l, 1:2, :]], axis=1
        )

        def project(at, l=l, bias_row=bias_row):
            xhat, _ = norm_stats(x[l, at, :])
            a = (xhat * gain[l, 0:1, :] + offset[l, 0:1, :]).astype(BF16)
            normed[l, at, :] = a
            for c in range(3):
                cols = slice(c * width, (c + 1) * width)
                qkv[l, at, cols] = (dot(a, w_in[l, :, cols]) + bias_row[:, cols]).astype(BF16)

        over_blocks(project)
        if fused and l == 1:
            pass_on(1, 0)
            pass_on(1, 1)

        def attend(i, carry, l=l):
            at = pl.ds(pl.multiple_of(i * ROWS_BLOCK, ROWS_BLOCK), ROWS_BLOCK)
            q = qkv[l, at, :width].astype(F32)
            k = qkv[l, at, width : 2 * width].astype(F32)
            v = qkv[l, at, 2 * width :].astype(F32)
            hot = keys[at, :]
            allowed = []
            for w in range(BLOCK_WINDOWS):
                hot_w = hot[w * SLOTS : (w + 1) * SLOTS]
                same = dot_nt(hot_w.astype(BF16), jnp.concatenate([hot_w] * GROUP, axis=0).astype(BF16))
                allowed.append(same > 0.5)
            scores = [
                dot_nt(k[here, lanes].astype(BF16), expand_heads(q[here, lanes])) for _, _, here, lanes in JOBS
            ]
            scores = [
                jnp.where(allowed[w], s * HEAD_DIM**-0.5 + bias[grp], MASKED)
                for s, (w, grp, _, _) in zip(scores, JOBS)
            ]
            tops = [jnp.max(s, axis=0, keepdims=True) for s in scores]
            raised = [jnp.exp(s - top) for s, top in zip(scores, tops)]
            shares = [1.0 / jnp.sum(e, axis=0, keepdims=True) for e in raised]
            ps = [(e * share).astype(BF16) for e, share in zip(raised, shares)]
            for p, (w, grp, _, _) in zip(ps, JOBS):
                probs[l, BLOCK_WINDOWS * i + w, grp] = p
            outs = [
                fold_heads(dot_tn(p, v[here, lanes].astype(BF16)))
                for p, (_, _, here, lanes) in zip(ps, JOBS)
            ]
            mixed[l, at, :] = by_window(outs).astype(BF16)
            return carry

        lax.fori_loop(0, blocks, attend, 0)

        def middle(at, l=l):
            m = x[l, at, :] + dot(mixed[l, at, :], w_out[l]) + b_out[l : l + 1, :]
            mid[l, at, :] = m
            xhat, _ = norm_stats(m)
            second[l, at, :] = (xhat * gain[l, 1:2, :] + offset[l, 1:2, :]).astype(BF16)
            gs[at, :] = m + b_red[l : l + 1, :]

        over_blocks(middle)
        if fused and l == 0:
            pass_on(0, 0)
            for copy in own:
                copy.wait()

        def feed(at, i, l=l):
            s = second[l, at, :]
            total = gs[at, :]
            jobs = [slice(c, c + chunk) for c in range(0, ff, chunk)]
            before = dot(s, w_exp[i, l, :, jobs[0]])
            held = None
            for n, cols in enumerate(jobs):
                after = dot(s, w_exp[i, l, :, jobs[n + 1]]) if n + 1 < len(jobs) else None
                if held is not None:
                    total = total + dot(*held)
                value, slope_now = gelu_pair(before + b_exp[i, l : l + 1, cols])
                value = value.astype(BF16)
                hidden[l, i, at, cols] = value
                slope[l, i, at, cols] = slope_now.astype(BF16)
                held = (value, w_red[i, l, cols, :])
                before = after
            gs[at, :] = total + dot(*held)

        over_blocks(functools.partial(feed, i=0))
        if fused:
            if l == 0:
                pass_on(0, 1)
                for copy in bias_fetches():
                    copy.wait()
            passed(l, 0)
            passed(l, 1)

        def feed_rest(i, carry, feed=feed):
            over_blocks(functools.partial(feed, i=i))
            return carry

        lax.fori_loop(1, shards, feed_rest, 0)

        if l == 0:
            regular_to_shifted(gs, x.at[1], side)

    def put_cot(wr, wc, r, tile):
        g[pl.ds(window_row(per_side, wr, wc, r), PITCH), :] = tile

    grid_to_windows(cot, side, True, put_cot)
    small[...] = jnp.zeros(small.shape, F32)

    for l in (1, 0):

        def add_small(name, value, l=l):
            at = SMALL[name]
            small[l, at : at + 1, :] += value

        def lower(at, l=l):
            g_now = g[at, :]
            add_small("reduce", jnp.sum(g_now, axis=0, keepdims=True))
            gz[at, :] = g_now.astype(BF16)

        over_blocks(lower)

        def reduce_weights(i, carry, l=l):
            for c in range(0, ff, chunk):
                d_feed[l, i, ff + c : ff + c + chunk, :] = dot_tn(hidden[l, i, :, c : c + chunk], gz[...]).astype(BF16)
            return carry

        lax.fori_loop(0, shards, reduce_weights, 0)
        advance(f"R{l}")
        ticks(l, "reduce_weights")
        if l == 1:
            windows_to_grid(gs, out, side, True)
        d_bexp[...] = jnp.zeros(d_bexp.shape, F32)

        def feed_back(at, l=l):
            g_low = gz[at, :]

            def one(i, total):
                jobs = [slice(c, c + chunk) for c in range(0, ff, chunk)]
                ahead_of = dot_nt(g_low, w_red[i, l, jobs[0], :])
                held = None
                for n, cols in enumerate(jobs):
                    after = dot_nt(g_low, w_red[i, l, jobs[n + 1], :]) if n + 1 < len(jobs) else None
                    if held is not None:
                        total = total + dot_nt(*held)
                    gb = ahead_of * slope[l, i, at, cols].astype(F32)
                    d_bexp[i, 0:1, cols] += jnp.sum(gb, axis=0, keepdims=True)
                    low = gb.astype(BF16)
                    gb_low[i, at, cols] = low
                    held = (low, w_exp[i, l, :, cols])
                    ahead_of = after
                return total + dot_nt(*held)

            gs[at, :] = lax.fori_loop(0, shards, one, jnp.zeros((ROWS_BLOCK, width), F32))

        over_blocks(feed_back, (l, "feed_back"))
        span = min(width, ff)
        for n in range(shards * (ff // span)):
            i, c = n // (ff // span), n % (ff // span) * span
            row = n
            if fused:
                row = lax.rem(links.m + i, shards) * (ff // span) + n % (ff // span)
            small[l, pl.ds(SMALL_EXPAND + row, 1), :span] = d_bexp[i, 0:1, c : c + span]

        def expand_weights(i, carry, l=l):
            if blocked:
                for c in range(0, ff, width):
                    d_feed[l, i, c : c + width, :] = dot_tn(second[l], gb_low[i, :, c : c + width]).astype(BF16)
            else:
                d_feed[l, i, :ff, :] = dot_tn(gb_low[i], second[l]).astype(BF16)
            return carry

        lax.fori_loop(0, shards, expand_weights, 0)
        advance(f"E{l}")
        ticks(l, "expand_weights")

        def middle_back(at, l=l):
            dmid, dgain, doffset = norm_back(mid[l, at, :], gain[l, 1:2, :], gs[at, :])
            add_small("gain2", dgain)
            add_small("bias2", doffset)
            gm = g[at, :] + dmid
            g[at, :] = gm
            add_small("output", jnp.sum(gm, axis=0, keepdims=True))
            low = gm.astype(BF16)
            gz[at, :] = low
            go[at, :] = dot_nt(low, w_out[l]).astype(BF16)

        over_blocks(middle_back, (l, "middle_back"))
        d_mixed = dot_tn(mixed[l], gz[...]).astype(BF16)
        for part in range(PART):
            at = part * part_rows + width
            d_attn[l, at : at + width // PART, :] = d_mixed[part * (width // PART) : (part + 1) * (width // PART)]
        bias_sum[...] = jnp.zeros(bias_sum.shape, F32)

        def attend_back(i, carry, l=l, grp=0):
            count = windows // 2
            at = pl.ds(pl.multiple_of(i * count * SLOTS, count * SLOTS), count * SLOTS)
            parts = [slice(p * width + grp * GLANES, p * width + (grp + 1) * GLANES) for p in range(3)]
            heres = [slice(w * SLOTS, (w + 1) * SLOTS) for w in range(count)]
            q, k, v = (qkv[l, at, part].astype(F32) for part in parts)
            go_now = go[at, parts[0]].astype(F32)
            go_all = [expand_heads(go_now[here]) for here in heres]
            dps = [dot_nt(v[here].astype(BF16), one) for one, here in zip(go_all, heres)]
            lows = [probs[l, count * i + w, grp] for w in range(count)]
            dvs = [dot(p, one) for p, one in zip(lows, go_all)]
            ps = [p.astype(F32) for p in lows]
            pds = [p * dp for p, dp in zip(ps, dps)]
            totals = [jnp.sum(pd, axis=0, keepdims=True) for pd in pds]
            dss = [(pd - p * total).astype(BF16) for pd, p, total in zip(pds, ps, totals)]
            dqs = [
                fold_heads(dot_tn(ds, k[here].astype(BF16))) * HEAD_DIM**-0.5 for ds, here in zip(dss, heres)
            ]
            dks = [dot(ds, expand_heads(q[here])) * HEAD_DIM**-0.5 for ds, here in zip(dss, heres)]
            total = bias_sum[grp]
            for ds in dss:
                total = total + ds.astype(F32)
            bias_sum[grp] = total
            for name, part, made in zip(("query", None, "value"), parts, (dqs, dks, dvs)):
                whole = jnp.concatenate(made, axis=0)
                if name:
                    row = SMALL[name]
                    small[l, row : row + 1, parts[0]] += jnp.sum(whole, axis=0, keepdims=True)
                dqkv[at, part] = whole.astype(BF16)
            ticks(l, f"attend_back{grp}", i)
            return carry

        for grp in range(GROUPS):
            lax.fori_loop(0, 2, functools.partial(attend_back, grp=grp), 0)
            for p in range(3):
                lanes = slice(p * width + grp * GLANES, p * width + (grp + 1) * GLANES)
                d_attn[l, grp * part_rows : grp * part_rows + width, p * GLANES : (p + 1) * GLANES] = dot_tn(
                    normed[l], dqkv[:, lanes]
                ).astype(BF16)
            if f"A{grp}{l}" in flows:
                advance(f"A{grp}{l}")
            ticks(l, f"group{grp}")

        krow = iota((SLOTS, 128), 0)
        qlane = iota((SLOTS, 128), 1)
        ahead = (qlane & (PITCH - 1)) >= (krow & (PITCH - 1))
        for grp in range(GROUPS):
            low = bias_sum[grp, :, :128]
            high = jnp.concatenate([bias_sum[grp, :, 128:], jnp.zeros((SLOTS, 256 - GQ), F32)], axis=1)
            for j in range(GROUP):
                h = grp * GROUP + j
                at = j * SLOTS
                if at + SLOTS <= 128:
                    one = pltpu.roll(low, 128 - at, 1) if at else low
                elif at < 128:
                    one = jnp.where(qlane < 128 - at, pltpu.roll(low, 128 - at, 1), pltpu.roll(high, 128 - at, 1))
                else:
                    one = pltpu.roll(high, (256 - at) % 128, 1)
                one = jnp.where(qlane < SLOTS, one, 0.0)
                for s in range(2):
                    picked = jnp.where(ahead if s == 0 else jnp.logical_not(ahead), one, 0.0)
                    tile = picked[:PITCH]
                    for r in range(1, WIN):
                        tile = tile + pltpu.roll(picked[r * PITCH : (r + 1) * PITCH], 128 - r * PITCH, 1)
                    for step in (1, 2, 4):
                        tile = jnp.where((iota(tile.shape, 0) & step) > 0, pltpu.roll(tile, 128 - step, 1), tile)
                    n = s * HEADS + h
                    small[l, SMALL_TABLE + n // 3 : SMALL_TABLE + n // 3 + 1, n % 3 * 128 : (n % 3 + 1) * 128] = jnp.sum(
                        tile, axis=0, keepdims=True
                    )

        def input_back(at, l=l):
            ga = dot_nt(dqkv[at, :], w_in[l])
            dx, dgain, doffset = norm_back(x[l, at, :], gain[l, 0:1, :], ga)
            add_small("gain1", dgain)
            add_small("bias1", doffset)
            gs[at, :] = g[at, :] + dx

        over_blocks(input_back, (l, "input_back"))
        advance(f"S{l}")
        ticks(l, "input_done")
        if l == 1:
            shifted_to_regular(gs, g, side)
        else:
            windows_to_grid(gs, grad_tokens, side, False)
        ticks(l, "placed")

    advance(*LAST)
    while not all(flow.done for flow in flows.values()):
        advance(*(name for name, flow in flows.items() if not flow.done))


def lanes_table(lanes):
    layers, heads = lanes.shape[0], lanes.shape[1] // 2
    both = lanes.reshape(layers, 2, heads, 128)
    span = SPAN_SIDE * PITCH

    def square(part, back):
        return jnp.roll(part, back, axis=-1)[..., :span].reshape(layers, heads, SPAN_SIDE, PITCH)

    right = square(both[:, 0], (WIN - 1) * PITCH)[..., :WIN]
    left = square(both[:, 1], WIN * PITCH)[..., PITCH - WIN + 1 :]
    whole = jnp.concatenate([left, right], axis=-1)
    return whole.reshape(layers, heads, SPAN_SIDE * SPAN_SIDE).transpose(0, 2, 1)


def on_device(
    mesh_shape,
    tokens,
    crop_ids,
    norm_gain,
    norm_bias,
    input_proj,
    input_bias,
    position_table,
    output_proj,
    output_bias,
    expand_weight,
    expand_bias,
    reduce_weight,
    reduce_bias,
    cotangent,
):
    _, side, _, width = tokens.shape
    layers, _, ff = expand_weight.shape
    win, shards = mesh_shape
    ids = jnp.broadcast_to(crop_ids[0, :, :, None], (side, side, 128))
    windows = (side // WIN) ** 2
    rows = windows * SLOTS
    attn_rows, feed_rows = 4 * width, 2 * ff
    fused = win % 4 == 0 and attn_rows % (16 * PART * win * shards) == 0 and ff % (16 * win) == 0
    vmem = pl.BlockSpec(memory_space=pltpu.VMEM)
    hbm = pl.BlockSpec(memory_space=pl.ANY)
    if fused:
        w_exp, w_red = expand_weight, reduce_weight
        b_exp = expand_bias
    else:
        w_exp = lax.all_gather(expand_weight, "mlp", axis=0)
        w_red = lax.all_gather(reduce_weight, "mlp", axis=0)
        b_exp = lax.all_gather(expand_bias, "mlp", axis=0).astype(F32)
    scratch = [
        pltpu.VMEM((layers, rows, width), F32),
        pltpu.VMEM((layers, rows, width), BF16),
        pltpu.VMEM((layers, rows, 3 * width), BF16),
        pltpu.VMEM((layers, windows, GROUPS, SLOTS, GQ), BF16),
        pltpu.VMEM((layers, rows, width), BF16),
        pltpu.VMEM((layers, rows, width), F32),
        pltpu.VMEM((layers, rows, width), BF16),
        pltpu.VMEM((layers, shards, rows, ff), BF16),
        pltpu.VMEM((layers, shards, rows, ff), BF16),
        pltpu.VMEM((rows, 128), F32),
        pltpu.VMEM((GROUPS, SLOTS, GQ), F32),
        pltpu.VMEM((GROUPS, SLOTS, GQ), F32),
        pltpu.VMEM((rows, width), F32),
        pltpu.VMEM((rows, width), F32),
        pltpu.VMEM((rows, width), BF16),
        pltpu.VMEM((shards, rows, ff), BF16),
        pltpu.VMEM((rows, 3 * width), BF16),
        pltpu.VMEM((rows, width), BF16),
        pltpu.VMEM((shards, 8, ff), F32),
    ]
    small_shape = (layers, SMALL_ROWS, width)
    scratch += [pltpu.VMEM((2, 128, 128), F32), pltpu.VMEM((2, 16, 128), F32)]
    if fused:
        plane, depth = 2 * shards, win // 4
        _, shapes = flow_table(mesh_shape, width, ff)
        scratch += [
            pltpu.VMEM((layers, attn_rows, width), BF16),
            pltpu.VMEM((layers, shards, feed_rows, width), BF16),
            pltpu.VMEM(small_shape, F32),
            pltpu.VMEM((shards, layers, width, ff), BF16),
            pltpu.VMEM((shards, 8, ff), F32),
            pltpu.VMEM((shards, layers, ff, width), BF16),
            pltpu.VMEM((layers, 2) + small_shape[1:], F32),
            pltpu.VMEM((layers, plane) + small_shape[1:], F32),
            pltpu.VMEM((layers, depth) + small_shape[1:], F32),
        ]
        scratch += [pltpu.VMEM(shape, BF16) for group in shapes.values() for shape in group]
        scratch += [
            pltpu.SemaphoreType.DMA((3 + len(shapes),)),
            pltpu.SemaphoreType.DMA((160,)),
            pltpu.SemaphoreType.DMA((160,)),
        ]
    outs = pl.pallas_call(
        functools.partial(kernel, side, mesh_shape if fused else None),
        out_shape=(
            jax.ShapeDtypeStruct(tokens.shape[1:], BF16),
            jax.ShapeDtypeStruct(tokens.shape[1:], BF16),
            jax.ShapeDtypeStruct((layers, attn_rows, width), BF16),
            jax.ShapeDtypeStruct((layers, feed_rows, width) if fused else (layers, shards, feed_rows, width), BF16),
            jax.ShapeDtypeStruct(small_shape, F32),
        ),
        in_specs=[vmem] * 9 + ([hbm, vmem, hbm] if fused else [vmem] * 3) + [vmem] * 2,
        out_specs=[vmem] * 2 + ([hbm] * 2 if fused else [vmem] * 2) + [vmem],
        scratch_shapes=scratch,
        compiler_params=pltpu.CompilerParams(
            vmem_limit_bytes=64 * 1024 * 1024,
            **(dict(collective_id=0, has_side_effects=True) if fused else {}),
        ),
    )(
        tokens[0],
        ids,
        norm_gain,
        norm_bias,
        input_proj,
        input_bias,
        position_table,
        output_proj,
        output_bias,
        w_exp,
        b_exp,
        w_red,
        reduce_bias,
        cotangent[0],
    )
    out, grad_tokens, d_attn, d_feed, small = outs
    if not fused:
        d_attn, small = lax.psum((d_attn, small), ("win", "mlp"))
        d_feed = lax.psum(lax.psum_scatter(d_feed, "mlp", scatter_dimension=1, tiled=False), "win")
    parts = d_attn.reshape(layers, PART, attn_rows // PART, width)
    d_in = jnp.concatenate(
        [parts[:, grp, :width, p * GLANES : (p + 1) * GLANES] for p in range(3) for grp in range(GROUPS)], axis=2
    )
    d_out = parts[:, :, width:].reshape(layers, width, width)
    if ff % width == 0:
        d_exp = jnp.concatenate([d_feed[:, c : c + width] for c in range(0, ff, width)], axis=2)
    else:
        d_exp = d_feed[:, :ff].swapaxes(1, 2)
    span = min(width, ff)
    d_bexp = small[:, SMALL_EXPAND : SMALL_EXPAND + shards * (ff // span), :span].reshape(layers, shards, ff)
    d_bexp = lax.dynamic_index_in_dim(d_bexp, lax.axis_index("mlp"), 1, keepdims=False)
    d_table = small[:, SMALL_TABLE : SMALL_TABLE + 8].reshape(layers, 2 * HEADS, 128)
    return (
        out[None],
        grad_tokens[None],
        small[:, 0:2],
        small[:, 2:4],
        d_in.astype(F32),
        small[:, 4:6],
        lanes_table(d_table),
        d_out.astype(F32),
        small[:, 6],
        d_exp.astype(F32),
        d_bexp,
        d_feed[:, ff:].astype(F32),
        small[:, 7],
    )


def solution(mesh):
    tokens = P(("win", "mlp"), None, None, None)
    placed = (
        tokens,
        P(("win", "mlp"), None, None),
        P(),
        P(),
        P(),
        P(),
        P(),
        P(),
        P(),
        P(None, None, "mlp"),
        P(None, "mlp"),
        P(None, "mlp", None),
        P(),
        tokens,
    )
    return jax.shard_map(
        functools.partial(on_device, (mesh.shape["win"], mesh.shape["mlp"])),
        mesh=mesh,
        in_specs=placed,
        out_specs=(
            tokens,
            tokens,
            P(),
            P(),
            P(),
            P(),
            P(),
            P(),
            P(),
            P(None, None, "mlp"),
            P(None, "mlp"),
            P(None, "mlp", None),
            P(),
        ),
        check_vma=False,
    )
```

time: 542 us -> 161 us (0.30)
  waiting for transfers between devices: 298 us -> 0 us
  blocking collectives: 85 us -> 0 us
  between operations: 14.4 us -> 0.79 us
  Pallas kernels: 127 us -> 139 us
  local copies, waits for them, and re-layouts: 6.95 us -> 14.1 us
    psum x2 -> x0, waiting for transfers between devices: 155 us -> none  [the longest x1 97.4 us: on_device(): lax.psum(lax.psum_scatter(d_exp, 'mlp', scatter_dimension=0, tiled=False)...]
    reduce_scatter x2 -> x0, waiting for transfers between devices: 71.1 us -> none  [the longest x1 37.5 us: on_device(): lax.psum_scatter(d_red, 'mlp', scatter_dimension=0, tiled=False)]
    psum x2 -> x0, blocking collectives: 70.9 us -> none  [the longest x1 40.2 us: on_device(): small, d_table = lax.psum((small, d_table), ('win', 'mlp'))]
    all_gather x2 -> x0, waiting for transfers between devices: 69.4 us -> none  [the longest x1 37.6 us: on_device(): w_red = lax.all_gather(reduce_weight, 'mlp', axis=0)]
    pallas_call x1, Pallas kernels: 127 us -> 139 us  [on_device(): pl.pallas_call(functools.partial(kernel, side, mesh_shape if fused else N...]
    unnamed x1 -> x0, blocking collectives: 8.84 us -> none
  transfers between devices with their start and end apart: 6 -> 0, of which waited for: 6 -> 0; matrix products, arithmetic and copies ran while one was open for 2% -> 0% of each run, Pallas kernels for 0% -> 0%
where the time goes in v3:
time: 161 us
  Pallas kernels  139 us (86%)
  local copies, waits for them, and re-layouts  14.1 us (9%)
  other arithmetic  6.5 us (4%)
    pallas_call x1, Pallas kernels, on_device(): pl.pallas_call(functools.partial(kernel, side, mesh_shape if fused else N...  139 us
    unnamed x22, local copies, waits for them, and re-layouts  6.96 us

profile of v3, /device:TPU:0, one launch (start us, length us, event | category | flops | bytes accessed | tf_op | source)
XLA Modules:
  0.0 160.9 jit_solution(2760428238325606457)
XLA Ops:
  0.6 0.7 copy.70
  1.4 1.5 copy.39.refs_6_
  2.9 1.0 broadcast_in_dim.14.refs_1_
  3.9 139.4 %shard_map.237 = (bf16[28,28,384]{2,1,0:T(8,128)(2,1)}, bf16[28,28,384]{2,1,0:T(8,128)(2,1)}, bf16[2,1536,384]{2,1,0:T(8,128)(2,1)}, bf16[2,1536,384]{2,1,0:T(8,128)(2,1)}, f32[2,24,384]{2,1,0:T(8,128)}) custom-call(bf16[28,28,384]{2,1,0:T(8,128)(2,1)} %bitcast.96, s32[28,28,128]{2,1,0:T(8,128)} %broadcast_in_dim.14.refs_1_, f32[2,2,384]{2,1,0:T(2,128)} %refs_2_.1, ...), custom_call_target="tpu_custom_call" | custom-call | tf_op jit(solution)/shard_map/pallas_call | solution.py:1016
  143.3 0.8 fusion.10
  144.1 0.6 copy_bitcast_fusion.2
  144.7 0.7 slice.121
  145.5 0.6 copy.71
  146.1 1.5 fusion.11
  147.5 0.7 slice.106
  148.3 0.1 slice.134
  148.4 0.1 pad_maximum_fusion.2
  148.5 0.1 slice.138
  148.5 0.1 pad_maximum_fusion.1
  148.6 0.1 copy.50
  148.7 0.1 copy.49
  148.9 0.0 copy-start.1
  148.9 0.7 copy.52
  149.7 1.1 slice.141
  150.8 1.1 bitcast_convert_fusion
  151.9 0.0 copy-done.1
  151.9 0.1 fusion.9
  152.1 1.6 slice_convert_fusion
  153.6 0.0 copy-start
  153.6 1.6 maximum_convert_fusion
  155.2 0.9 copy-done
  156.6 0.0 copy-start.3
  156.6 2.0 %convert_element_type.15 = f32[2,384,1152]{2,1,0:T(8,128)} convert(bf16[2,384,1152]{2,1,0:T(8,128)(2,1)S(1)} %fusion) | non-fusion elementwise | flops 884736 | bytes 5308416 | tf_op jit(solution)/shard_map/convert_element_type | solution.py:1070
  158.7 0.0 copy-done.3
  158.7 0.0 copy-start.2
  158.7 0.8 copy.82
  159.5 0.5 copy-done.2
  160.0 0.8 copy.83
  (16 shorter events, 0.5 us)
Async XLA Ops:
  148.9 3.0 %copy-start.1 = (bf16[2,1536,384]{2,1,0:T(8,128)(2,1)S(1)}, bf16[2,1536,384]{2,1,0:T(8,128)(2,1)}, u32[]{:S(2)}) copy-start(bf16[2,1536,384]{2,1,0:T(8,128)(2,1)} %get-tuple-element.22) | copy-start | bytes 7077892
  153.6 2.5 %copy-start = (bf16[2,1536,384]{2,1,0:T(8,128)(2,1)S(1)}, bf16[2,1536,384]{2,1,0:T(8,128)(2,1)}, u32[]{:S(2)}) copy-start(bf16[2,1536,384]{2,1,0:T(8,128)(2,1)} %get-tuple-element.21) | copy-start | bytes 7077892
  156.6 2.0 %copy-start.3 = (bf16[28,28,384]{2,1,0:T(8,128)(2,1)S(1)}, bf16[28,28,384]{2,1,0:T(8,128)(2,1)}, u32[]{:S(2)}) copy-start(bf16[28,28,384]{2,1,0:T(8,128)(2,1)} %get-tuple-element.18) | copy-start | bytes 1806340
  158.7 1.3 copy-start.2

commit v4 on v3

--- a/solution.py
+++ b/solution.py
@@ -26,17 +26,15 @@
 F32 = jnp.float32
 BF16 = jnp.bfloat16
 
-ERF_P = 0.39
+ERF_P = 0.4
 ERF_C = (
-    0.22003399505358215,
-    0.22002241291251284,
-    0.20367769093249805,
-    0.16514655576456758,
-    0.15214218925854978,
-    -0.024768996902218943,
-    0.20836931643666226,
-    -0.19248882577712367,
-    0.04786540601145673,
+    0.22567691835428957,
+    0.22565742813591003,
+    0.2069437219941218,
+    0.18213740047970625,
+    0.06806251607656177,
+    0.1868261013466735,
+    -0.09530889147438172,
 )
 
 
@@ -120,7 +118,8 @@
             row = lax.rem(wr * WIN + r + (SHIFT if shifted else 0), side)
             line = src[row].astype(F32)
             width = line.shape[1]
-            line = jnp.concatenate([line, jnp.zeros((32 - side, width), F32)], axis=0)
+            if line.shape[0] < 32:
+                line = jnp.concatenate([line, jnp.zeros((32 - line.shape[0], width), F32)], axis=0)
             if shifted:
                 i = iota(line.shape, 0)
                 line = jnp.where(i < side - SHIFT, pltpu.roll(line, 32 - SHIFT, 0), pltpu.roll(line, side - SHIFT, 0))
@@ -204,17 +203,15 @@
 BLOCK_WINDOWS = 4
 ROWS_BLOCK = BLOCK_WINDOWS * SLOTS
 JOBS = [
-    (w, grp, slice(w * SLOTS, (w + 1) * SLOTS), slice(grp * GLANES, (grp + 1) * GLANES))
-    for w in range(BLOCK_WINDOWS)
-    for grp in range(GROUPS)
+    (w, grp, slice(w * SLOTS, (w + 1) * SLOTS)) for w in range(BLOCK_WINDOWS) for grp in range(GROUPS)
 ]
 SMALL = {"gain1": 0, "gain2": 1, "bias1": 2, "bias2": 3, "query": 4, "value": 5, "output": 6, "reduce": 7}
-SMALL_TABLE = 8
-SMALL_EXPAND = 16
-SMALL_ROWS = 24
+SMALL_EXPAND = 8
+SMALL_EARLY = 16
+SMALL_TABLE = {0: 16, 1: 24}
+SMALL_ROWS = 32
 ADD_ROWS = 96
 PART = 3
-ATTN_PARTS = (((0, 2), (2, 1)), ((0, 3),))
 
 
 def table_spans():
@@ -238,6 +235,7 @@
             "x": (2, self.x, lambda q: self.at(x=q)),
             "z": (self.depth, self.z, lambda q: self.at(z=q)),
             "mlp": (self.mlp, m, lambda q: self.at(m=q)),
+            "y": (self.mlp, m, lambda q: self.at(m=q)),
             "plane": (
                 2 * self.mlp,
                 self.x * self.mlp + m,
@@ -290,91 +288,122 @@
         )
 
 
-def add_rows(dst, sources, start, count):
+def add_rows(dst, sources, count):
     step = next(n for n in (ADD_ROWS, 64, 48, 32, 16) if count % n == 0)
 
     def one(i, carry):
-        at = pl.multiple_of(start + i * step, 16)
-        total = dst[pl.ds(at, step), :].astype(F32)
+        at = pl.ds(pl.multiple_of(i * step, 16), step)
+        total = dst[at, :].astype(F32)
         for source in sources:
-            total = total + source[pl.ds(pl.multiple_of(i * step, 16), step), :].astype(F32)
-        dst[pl.ds(at, step), :] = total.astype(dst.dtype)
+            total = total + source[at, :].astype(F32)
+        dst[at, :] = total.astype(dst.dtype)
         return carry
 
     lax.fori_loop(0, count // step, one, 0)
+
+
+FLOWS = {
+    "R1": ("R1", 1, 0, ("core", "plane", "z")),
+    "E1": ("E1", 1, 0, ("core", "plane", "z")),
+    "A01": ("A011", 1, 0, ("core", "y", "x", "z")),
+    "A21": ("A121", 1, 0, ("core", "y", "x", "z")),
+    "R0a": ("R0", 3, 0, ("core", "mlp", "x", "z")),
+    "R0b": ("R0", 3, 1, ("core", "mlp", "x", "z")),
+    "R0c": ("R0", 3, 2, ("core", "mlp", "x", "z")),
+    "E0a": ("E0", 3, 0, ("core", "mlp", "x", "z")),
+    "E0b": ("E0", 3, 1, ("core", "mlp", "x", "z")),
+    "E0c": ("E0", 3, 2, ("core", "mlp", "x", "z")),
+    "A00": ("A010", 1, 0, ("core", "plane", "z")),
+    "A20a": ("A120", 3, 0, ("core", "plane", "z")),
+    "A20b": ("A120", 3, 1, ("core", "plane", "z")),
+    "A20c": ("A120", 3, 2, ("core", "plane", "z")),
+}
 
 
 def flow_table(mesh_shape, width, ff):
     part = 4 * width // PART
-    flows = {}
-    for l in (1, 0):
-        flows[f"R{l}"] = (l, ff, ff, ("core", "mlp", "x", "z"))
-        flows[f"E{l}"] = (l, 0, ff, ("core", "mlp", "x", "z"))
-        for first, count in ATTN_PARTS[l]:
-            flows[f"A{first + count - 1}{l}"] = (l, first * part, count * part, ("core", "plane", "z"))
     win, mlp = mesh_shape
-    sizes = {"core": 2, "x": 2, "z": win // 4, "mlp": mlp, "plane": 2 * mlp}
-    shapes = {}
-    for name, (_, _, rows, stages) in flows.items():
-        slots = mlp if "mlp" in stages else 1
+    sizes = {"core": 2, "x": 2, "z": win // 4, "mlp": mlp, "y": mlp, "plane": 2 * mlp}
+    flows, shapes = {}, {}
+    for name, (what, splits, split, stages) in FLOWS.items():
+        kind, l = what[0], int(what[-1])
+        if kind == "A":
+            first, rows = int(what[1]) * part, int(what[2]) * part
+        else:
+            first, rows = (ff if kind == "R" else 0), ff
+        lanes = (split * (width // splits), width // splits)
+        slots = mlp if kind in "RE" else 1
+        flows[name] = (l, kind in "RE", (first, rows), lanes, stages)
         shapes[name] = []
         for stage in stages:
             if stage == "mlp":
                 slots = 1
+            elif stage == "plane" and slots > 1:
+                slots, rows = 1, rows // 2
             else:
                 rows //= sizes[stage]
-            shapes[name].append((sizes[stage] - 1, slots, rows, width))
+            shapes[name].append((sizes[stage] - 1, slots, rows, lanes[1]))
     return flows, shapes
 
 
+def flow_after(what):
+    return what if what[0] in "RE" else f"A{int(what[1]) + int(what[2]) - 1}{what[-1]}"
+
+
 class Flow:
-    def __init__(self, links, staged, out, first, rows, stages, buffers, local_sem):
+    def __init__(self, links, staged, out, slots, span, lanes, stages, buffers, local_sem):
         self.links, self.staged, self.out, self.local_sem = links, staged, out, local_sem
-        self.stages, self.buffers = stages, buffers
-        self.spans = [(first, rows)]
-        for stage in stages:
+        self.stages, self.buffers, self.lanes = stages, buffers, pl.ds(*lanes)
+        self.spans, self.slots, self.down = [span], [slots], []
+        for n, stage in enumerate(stages):
             first, rows = self.spans[-1]
-            if stage != "mlp":
+            if stage == "mlp":
+                slots = 1
+            elif stage == "plane" and slots > 1:
+                slots, rows = 1, rows // 2
+                first = first + links.x * rows
+                self.down.insert(0, (n, "x"))
+            else:
                 rows = rows // links.size(stage)
                 first = first + links.me(stage) * rows
+                self.down.insert(0, (n, stage))
             self.spans.append((first, rows))
-        self.down = [n for n in reversed(range(len(stages))) if stages[n] != "mlp"]
+            self.slots.append(slots)
         self.steps = len(stages) + len(self.down)
-        self.sems = [
-            links.reserve(links.size(stages[n]) - 1) for n in list(range(len(stages))) + self.down
-        ]
+        self.sems = [links.reserve(links.size(group) - 1) for group in stages + tuple(group for _, group in self.down)]
         self.at = 0
         self.done = False
-
-    def slots(self, n):
-        return self.staged.shape[0] if "mlp" in self.stages[n:] else 1
 
     def copies(self, k):
         links = self.links
         made = []
         if k < len(self.stages):
-            stage = self.stages[k]
+            stage, slots = self.stages[k], self.slots[k]
+            (first, _), (_, rows) = self.spans[k], self.spans[k + 1]
             for d, q in links.peers(stage):
-                first, rows = self.spans[k]
                 if stage == "mlp":
-                    src = self.staged.at[pl.ds(d, 1), pl.ds(pl.multiple_of(first, 16), rows)]
+                    slot, at = pl.ds(d, 1), first
+                elif stage == "plane" and slots > 1:
+                    slot, at = pl.ds(d % links.mlp, 1), first + lax.div(q, links.mlp) * rows
                 else:
-                    rows = self.spans[k + 1][1]
-                    src = self.staged.at[pl.ds(0, self.slots(k)), pl.ds(pl.multiple_of(first + q * rows, 16), rows)]
+                    slot, at = pl.ds(0, slots), first + q * rows
+                src = self.staged.at[slot, pl.ds(pl.multiple_of(at, 16), rows), self.lanes]
                 made.append(links.copy(stage, q, src, self.buffers[k].at[d - 1], self.sems[k] + d - 1))
             return made
-        n = self.down[k - len(self.stages)]
-        first, rows = self.spans[n + 1]
-        mine = pl.ds(pl.multiple_of(first, 16), rows)
-        src = self.staged.at[0, mine] if k == len(self.stages) else self.out.at[mine]
-        for d, q in links.peers(self.stages[n]):
-            made.append(links.copy(self.stages[n], q, src, self.out.at[mine], self.sems[k] + d - 1))
+        n, group = self.down[k - len(self.stages)]
+        src = self.mine(n + 1, self.staged.at[0] if k == len(self.stages) else self.out)
+        for d, q in links.peers(group):
+            made.append(links.copy(group, q, src, self.mine(n + 1, self.out), self.sems[k] + d - 1))
         return made
 
+    def mine(self, n, ref):
+        first, rows = self.spans[n]
+        return ref.at[pl.ds(pl.multiple_of(first, 16), rows), self.lanes]
+
     def local(self):
-        first, rows = self.spans[-1]
-        mine = pl.ds(pl.multiple_of(first, 16), rows)
-        return pltpu.make_async_copy(self.staged.at[0, mine], self.out.at[mine], self.local_sem)
+        return pltpu.make_async_copy(
+            self.mine(len(self.stages), self.staged.at[0]), self.mine(len(self.stages), self.out), self.local_sem
+        )
 
     def advance(self):
         k = self.at
@@ -382,13 +411,11 @@
             for copy in self.copies(k - 1):
                 copy.wait()
             if k - 1 < len(self.stages):
-                first, rows = self.spans[k]
-                for slot in range(self.slots(k)):
+                for slot in range(self.slots[k]):
                     add_rows(
-                        self.staged.at[slot],
+                        self.mine(k, self.staged.at[slot]),
                         [self.buffers[k - 1].at[d - 1, slot] for d, _ in self.links.peers(self.stages[k - 1])],
-                        first,
-                        rows,
+                        self.spans[k][1],
                     )
             elif k - 1 == len(self.stages):
                 self.local().wait()
@@ -440,21 +467,25 @@
 
 PLAN = {
     (1, "feed_back"): {1: ("R1",)},
-    (1, "middle_back"): {3: ("E1",)},
-    (1, "attend_back0"): {0: ("R1",)},
-    (1, "attend_back2"): {1: ("R1", "E1")},
-    (1, "input_back"): {2: ("A21",)},
-    (1, "placed"): {None: ("E1", "R1", "S1")},
-    (0, "feed_back"): {2: ("R0", "E1", "A21"), 3: ("S1", "R1")},
-    (0, "middle_back"): {3: ("E0", "E1", "R1", "R0")},
-    (0, "attend_back0"): {0: ("A21", "R1")},
-    (0, "group0"): {None: ("S1",)},
-    (0, "attend_back1"): {1: ("E1",)},
-    (0, "attend_back2"): {1: ("E0", "R0", "E1", "A10", "A21")},
-    (0, "input_back"): {0: ("A20",), 3: ("E0",)},
-    (0, "placed"): {None: ("R0",)},
+    (1, "attend_back0"): {0: ("E1",)},
+    (1, "attend_back1"): {0: ("R1",), 1: ("A01",)},
+    (1, "input_done"): {None: ("A21",)},
+    (1, "placed"): {None: ("E1", "S1", "R1")},
+    (0, "reduce_weights"): {None: ("A01",)},
+    (0, "feed_back"): {1: ("R0b", "R0c", "R0a"), 2: ("A21", "A01"), 3: ("E1", "S1")},
+    (0, "expand_weights"): {None: ("R0b", "R1")},
+    (0, "middle_back"): {2: ("E0a", "A21", "R0c", "A01", "E0b", "E0c")},
+    (0, "attend_back0"): {0: ("R0b", "R0a", "E1")},
+    (0, "group0"): {None: ("E0a",)},
+    (0, "attend_back1"): {0: ("S1", "R1", "A00", "R0c"), 1: ("R0a", "A21", "E0b", "R1")},
+    (0, "group1"): {None: ("A01",)},
+    (0, "attend_back2"): {0: ("R0b", "E0c"), 1: ("E1",)},
+    (0, "group2"): {None: ("E0a", "R0c")},
+    (0, "input_back"): {1: ("R0a", "E1", "A20a"), 2: ("A20b", "A20c", "A00"), 3: ("E0b", "A21")},
+    (0, "table1"): {None: ("R0b", "A01")},
+    (0, "placed"): {None: ("E0a", "E0c")},
 }
-LAST = ("S0", "A10", "E0", "A21", "R0", "A20", "A21", "A10", "S0", "E0", "R0", "A20", "R0", "A10", "E0", "S0", "A20", "E0", "A10", "A20", "A10", "A20")
+LAST = ("R0c", "S0", "A20a", "R0a", "A20b", "A00", "A20c", "E0a", "A01", "E0b", "A21", "R0b", "A01", "A20a", "A20b", "R0c", "R0b", "A00", "R0c", "A20c", "E0c", "S0", "R0a", "E0b", "E0a", "A20a", "A20b", "R0a", "E0a", "A21", "A20c", "A00", "A21", "E0b", "E0c", "A20a", "A00", "E0b", "A20b", "A20a", "A20c", "A20b", "S0", "E0c", "A20c", "E0c")
 
 
 def kernel(side, mesh_shape, *refs):
@@ -465,41 +496,45 @@
         del refs[:n]
         return got
 
-    tokens, ids, gain, offset, w_in, b_in, table, w_out, b_out, w_exp, b_exp, w_red, b_red, cot = take(14)
+    tokens, ids, gain, offset, global_in, b_in, table, w_out, b_out, w_exp, b_exp, w_red, b_red, cot = take(14)
     fused = mesh_shape is not None
     out, grad_tokens, d_attn, d_feed, small = take(5)
     (x, normed, qkv, probs, mixed, mid, second, hidden, slope) = take(9)
-    (keys, bias, bias_sum, g, gs, gz, gb_low, dqkv, go, d_bexp, turn, spread) = take(12)
+    (keys, bias, bias_sum, g, gs, gz, gb_low, dqkv, go, d_bexp, turn, spread, w_in, turned, wide, tall, hot_grid, in_sems) = take(18)
     flows = {}
     if fused:
         out_attn, out_feed, out_small = d_attn, d_feed, small
         d_attn, d_feed, small = take(3)
         local_exp, local_bexp, local_red = w_exp, b_exp, w_red
         w_exp, b_exp, w_red = take(3)
-        small_buffers = take(3)
+        small_buffers = [take(3) for _ in range(2)]
         flow_rows, shapes = flow_table(mesh_shape, x.shape[2], local_exp.shape[2])
         landing = {name: take(len(shapes[name])) for name in flow_rows}
         local_sems, send_sem, recv_sem = take(3)
         links = Links(mesh_shape, send_sem, recv_sem)
-        for n, (name, (l, first, count, stages)) in enumerate(flow_rows.items()):
-            feed_flow = "mlp" in stages
+        for n, (name, (l, feed_flow, span, lanes, stages)) in enumerate(flow_rows.items()):
             flows[name] = Flow(
                 links,
                 d_feed.at[l] if feed_flow else d_attn.at[pl.ds(l, 1)],
                 out_feed.at[l] if feed_flow else out_attn.at[l],
-                first,
-                count,
+                mesh_shape[1] if feed_flow else 1,
+                span,
+                lanes,
                 stages,
                 landing[name],
                 local_sems.at[3 + n],
             )
         for l in (1, 0):
-            flows[f"S{l}"] = SmallFlow(links, small.at[l], [b.at[l] for b in small_buffers], out_small.at[l])
+            part = pl.ds(0, SMALL_EARLY if l else SMALL_ROWS)
+            flows[f"S{l}"] = SmallFlow(links, small.at[l, part], small_buffers[l], out_small.at[l, part])
 
     def advance(*names):
         if fused:
             for name in names:
                 flows[name].advance()
+
+    def begin(point):
+        advance(*(name for name in flows if name in FLOWS and flow_after(FLOWS[name][0]) == point))
 
     def ticks(l, phase, i=None):
         for iteration, names in PLAN.get((l, phase), {}).items():
@@ -517,6 +552,18 @@
     blocked = ff % width == 0
     part_rows = 4 * width // PART
 
+    gathers = [
+        pltpu.make_async_copy(
+            global_in.at[l, :, pl.ds(p * width + grp * GLANES, GLANES)],
+            w_in.at[l, :, pl.ds(grp * width + p * GLANES, GLANES)],
+            in_sems.at[(l * GROUPS + grp) * 3 + p],
+        )
+        for l in range(2)
+        for grp in range(GROUPS)
+        for p in range(3)
+    ]
+    for copy in gathers:
+        copy.start()
     if fused:
         links.greet()
         own = [
@@ -571,14 +618,24 @@
             for copy in passes(l, n):
                 copy.wait()
 
-    def over_blocks(body, tick=None):
+    def over_blocks(body, tick=None, after=None):
         def step(i, carry):
             body(pl.ds(pl.multiple_of(i * ROWS_BLOCK, ROWS_BLOCK), ROWS_BLOCK))
             if tick:
                 ticks(*tick, i)
+            if after:
+                after(i)
             return carry
 
         lax.fori_loop(0, blocks, step, 0)
+
+    wide[...] = jnp.zeros(wide.shape, F32)
+    for row in range(side):
+        wide[row : row + 1, :side] = ids[row].astype(F32)
+    by_column = wide[:, :128].T[:32]
+    for row in range(side):
+        hot_grid[row] = jnp.broadcast_to(by_column[:, row : row + 1], (32, 128))
+    wide[...] = jnp.zeros(wide.shape, F32)
 
     def put_tokens(wr, wc, r, tile):
         x[0, pl.ds(window_row(per_side, wr, wc, r), PITCH), :] = tile
@@ -604,14 +661,17 @@
             hot = jnp.where((lane == label) & (slot < WIN), 1.0, 0.0)
             keys[pl.ds(window_row(per_side, wr, wc, r), PITCH), :] = hot
 
-        grid_to_windows(ids, side, shifted, put_keys)
+        grid_to_windows(hot_grid, side, shifted, put_keys)
 
         krow = iota((SLOTS, 128), 0)
         qlane = iota((SLOTS, 128), 1)
         ahead = (qlane & (PITCH - 1)) >= (krow & (PITCH - 1))
         turn[...] = jnp.zeros(turn.shape, F32)
+        for h in range(HEADS):
+            wide[h : h + 1, : table.shape[2]] = table[h, l : l + 1, :]
+        tall[...] = wide[...].T
         for lane, entry, count, s in table_spans():
-            turn[s, lane : lane + count, :HEADS] = table[l, entry : entry + count, :]
+            turn[s, lane : lane + count, :] = tall[entry : entry + count, :]
         for s in range(2):
             spread[s] = turn[s].T[: spread.shape[1]]
         for grp in range(GROUPS):
@@ -641,8 +701,16 @@
             bias[grp, :, 128:] = high[:, : GQ - 128]
 
         bias_row = jnp.concatenate(
-            [b_in[l, 0:1, :], jnp.zeros((1, width), F32), b_in[l, 1:2, :]], axis=1
+            [
+                one[:, grp * GLANES : (grp + 1) * GLANES]
+                for grp in range(GROUPS)
+                for one in (b_in[l, 0:1, :], jnp.zeros((1, width), F32), b_in[l, 1:2, :])
+            ],
+            axis=1,
         )
+        if l == 0:
+            for copy in gathers:
+                copy.wait()
 
         def project(at, l=l, bias_row=bias_row):
             xhat, _ = norm_stats(x[l, at, :])
@@ -659,9 +727,13 @@
 
         def attend(i, carry, l=l):
             at = pl.ds(pl.multiple_of(i * ROWS_BLOCK, ROWS_BLOCK), ROWS_BLOCK)
-            q = qkv[l, at, :width].astype(F32)
-            k = qkv[l, at, width : 2 * width].astype(F32)
-            v = qkv[l, at, 2 * width :].astype(F32)
+            q, k, v = (
+                [
+                    qkv[l, at, grp * width + p * GLANES : grp * width + (p + 1) * GLANES].astype(F32)
+                    for grp in range(GROUPS)
+                ]
+                for p in range(3)
+            )
             hot = keys[at, :]
             allowed = []
             for w in range(BLOCK_WINDOWS):
@@ -669,21 +741,20 @@
                 same = dot_nt(hot_w.astype(BF16), jnp.concatenate([hot_w] * GROUP, axis=0).astype(BF16))
                 allowed.append(same > 0.5)
             scores = [
-                dot_nt(k[here, lanes].astype(BF16), expand_heads(q[here, lanes])) for _, _, here, lanes in JOBS
+                dot_nt(k[grp][here].astype(BF16), expand_heads(q[grp][here])) for _, grp, here in JOBS
             ]
             scores = [
                 jnp.where(allowed[w], s * HEAD_DIM**-0.5 + bias[grp], MASKED)
-                for s, (w, grp, _, _) in zip(scores, JOBS)
+                for s, (w, grp, _) in zip(scores, JOBS)
             ]
             tops = [jnp.max(s, axis=0, keepdims=True) for s in scores]
             raised = [jnp.exp(s - top) for s, top in zip(scores, tops)]
             shares = [1.0 / jnp.sum(e, axis=0, keepdims=True) for e in raised]
             ps = [(e * share).astype(BF16) for e, share in zip(raised, shares)]
-            for p, (w, grp, _, _) in zip(ps, JOBS):
+            for p, (w, grp, _) in zip(ps, JOBS):
                 probs[l, BLOCK_WINDOWS * i + w, grp] = p
             outs = [
-                fold_heads(dot_tn(p, v[here, lanes].astype(BF16)))
-                for p, (_, _, here, lanes) in zip(ps, JOBS)
+                fold_heads(dot_tn(p, v[grp][here].astype(BF16))) for p, (_, grp, here) in zip(ps, JOBS)
             ]
             mixed[l, at, :] = by_window(outs).astype(BF16)
             return carry
@@ -724,17 +795,38 @@
         over_blocks(functools.partial(feed, i=0))
         if fused:
             if l == 0:
-                pass_on(0, 1)
                 for copy in bias_fetches():
                     copy.wait()
             passed(l, 0)
+
+        def feed_up(at, i, l=l):
+            s = second[l, at, :]
+            jobs = [slice(c, c + chunk) for c in range(0, ff, chunk)]
+            befores = [dot(s, w_exp[i, l, :, cols]) for cols in jobs]
+            for before, cols in zip(befores, jobs):
+                value, slope_now = gelu_pair(before + b_exp[i, l : l + 1, cols])
+                hidden[l, i, at, cols] = value.astype(BF16)
+                slope[l, i, at, cols] = slope_now.astype(BF16)
+
+        def feed_down(at, i, l=l):
+            gs[at, :] += dot(hidden[l, i, at, :], w_red[i, l])
+
+        def second_fetch(block, shard, l=l):
+            if fused and l == 0:
+                pl.when((block == blocks // 2) & (shard == 1))(functools.partial(pass_on, 0, 1))
+
+        def up(i, carry, feed_up=feed_up):
+            over_blocks(functools.partial(feed_up, i=i), after=functools.partial(second_fetch, shard=i))
+            return carry
+
+        def down(i, carry, feed_down=feed_down):
+            over_blocks(functools.partial(feed_down, i=i))
+            return carry
+
+        lax.fori_loop(1, shards, up, 0)
+        if fused:
             passed(l, 1)
-
-        def feed_rest(i, carry, feed=feed):
-            over_blocks(functools.partial(feed, i=i))
-            return carry
-
-        lax.fori_loop(1, shards, feed_rest, 0)
+        lax.fori_loop(1, shards, down, 0)
 
         if l == 0:
             regular_to_shifted(gs, x.at[1], side)
@@ -744,6 +836,37 @@
 
     grid_to_windows(cot, side, True, put_cot)
     small[...] = jnp.zeros(small.shape, F32)
+
+    def table_back(l):
+        krow = iota((SLOTS, 128), 0)
+        qlane = iota((SLOTS, 128), 1)
+        ahead = (qlane & (PITCH - 1)) >= (krow & (PITCH - 1))
+        kept = (ahead & (qlane < SLOTS), jnp.logical_not(ahead) & (qlane < SLOTS))
+        lined = []
+        for grp in range(GROUPS):
+            low = bias_sum[l, grp, :, :128]
+            high = jnp.concatenate([bias_sum[l, grp, :, 128:], jnp.zeros((SLOTS, 256 - GQ), F32)], axis=1)
+            for j in range(GROUP):
+                at = j * SLOTS
+                if at + SLOTS <= 128:
+                    one = pltpu.roll(low, 128 - at, 1) if at else low
+                elif at < 128:
+                    one = jnp.where(qlane < 128 - at, pltpu.roll(low, 128 - at, 1), pltpu.roll(high, 128 - at, 1))
+                else:
+                    one = pltpu.roll(high, (256 - at) % 128, 1)
+                lined.append(one)
+        picked = [jnp.where(keep, one, 0.0) for keep in kept for one in lined]
+        tiles = [one[:PITCH] for one in picked]
+        for r in range(1, WIN):
+            turned_rows = [pltpu.roll(one[r * PITCH : (r + 1) * PITCH], 128 - r * PITCH, 1) for one in picked]
+            tiles = [tile + one for tile, one in zip(tiles, turned_rows)]
+        odd = iota((PITCH, 128), 0)
+        for step in (1, 2, 4):
+            tiles = [jnp.where((odd & step) > 0, pltpu.roll(tile, 128 - step, 1), tile) for tile in tiles]
+        for n, tile in enumerate(tiles):
+            row = SMALL_TABLE[l] + n // 3
+            small[0, row : row + 1, n % 3 * 128 : (n % 3 + 1) * 128] = jnp.sum(tile, axis=0, keepdims=True)
+
 
     for l in (1, 0):
 
@@ -758,13 +881,19 @@
 
         over_blocks(lower)
 
+        if blocked:
+            turned[...] = gz[...].T
+
         def reduce_weights(i, carry, l=l):
-            for c in range(0, ff, chunk):
-                d_feed[l, i, ff + c : ff + c + chunk, :] = dot_tn(hidden[l, i, :, c : c + chunk], gz[...]).astype(BF16)
+            if blocked:
+                for c in range(0, ff, width):
+                    d_feed[l, i, ff + c : ff + c + width, :] = dot(turned[...], hidden[l, i, :, c : c + width]).astype(BF16)
+            else:
+                d_feed[l, i, ff:, :] = dot_tn(hidden[l, i], gz[...]).astype(BF16)
             return carry
 
         lax.fori_loop(0, shards, reduce_weights, 0)
-        advance(f"R{l}")
+        begin(f"R{l}")
         ticks(l, "reduce_weights")
         if l == 1:
             windows_to_grid(gs, out, side, True)
@@ -773,23 +902,26 @@
         def feed_back(at, l=l):
             g_low = gz[at, :]
 
-            def one(i, total):
+            def one(i, first):
                 jobs = [slice(c, c + chunk) for c in range(0, ff, chunk)]
-                ahead_of = dot_nt(g_low, w_red[i, l, jobs[0], :])
-                held = None
-                for n, cols in enumerate(jobs):
-                    after = dot_nt(g_low, w_red[i, l, jobs[n + 1], :]) if n + 1 < len(jobs) else None
-                    if held is not None:
-                        total = total + dot_nt(*held)
-                    gb = ahead_of * slope[l, i, at, cols].astype(F32)
+                ghs = [dot_nt(g_low, w_red[i, l, cols, :]) for cols in jobs]
+                for gh, cols in zip(ghs, jobs):
+                    gb = gh * slope[l, i, at, cols].astype(F32)
                     d_bexp[i, 0:1, cols] += jnp.sum(gb, axis=0, keepdims=True)
-                    low = gb.astype(BF16)
-                    gb_low[i, at, cols] = low
-                    held = (low, w_exp[i, l, :, cols])
-                    ahead_of = after
-                return total + dot_nt(*held)
-
-            gs[at, :] = lax.fori_loop(0, shards, one, jnp.zeros((ROWS_BLOCK, width), F32))
+                    gb_low[i, at, cols] = gb.astype(BF16)
+                part = dot_nt(gb_low[i, at, :], w_exp[i, l])
+                if first:
+                    gs[at, :] = part
+                else:
+                    gs[at, :] += part
+
+            one(0, True)
+
+            def rest(i, carry):
+                one(i, False)
+                return carry
+
+            lax.fori_loop(1, shards, rest, 0)
 
         over_blocks(feed_back, (l, "feed_back"))
         span = min(width, ff)
@@ -800,16 +932,19 @@
                 row = lax.rem(links.m + i, shards) * (ff // span) + n % (ff // span)
             small[l, pl.ds(SMALL_EXPAND + row, 1), :span] = d_bexp[i, 0:1, c : c + span]
 
+        if blocked:
+            turned[...] = second[l].T
+
         def expand_weights(i, carry, l=l):
             if blocked:
                 for c in range(0, ff, width):
-                    d_feed[l, i, c : c + width, :] = dot_tn(second[l], gb_low[i, :, c : c + width]).astype(BF16)
+                    d_feed[l, i, c : c + width, :] = dot(turned[...], gb_low[i, :, c : c + width]).astype(BF16)
             else:
                 d_feed[l, i, :ff, :] = dot_tn(gb_low[i], second[l]).astype(BF16)
             return carry
 
         lax.fori_loop(0, shards, expand_weights, 0)
-        advance(f"E{l}")
+        begin(f"E{l}")
         ticks(l, "expand_weights")
 
         def middle_back(at, l=l):
@@ -828,15 +963,17 @@
         for part in range(PART):
             at = part * part_rows + width
             d_attn[l, at : at + width // PART, :] = d_mixed[part * (width // PART) : (part + 1) * (width // PART)]
-        bias_sum[...] = jnp.zeros(bias_sum.shape, F32)
+        bias_sum[l] = jnp.zeros(bias_sum.shape[1:], F32)
+        turned[...] = normed[l].T
 
         def attend_back(i, carry, l=l, grp=0):
             count = windows // 2
             at = pl.ds(pl.multiple_of(i * count * SLOTS, count * SLOTS), count * SLOTS)
-            parts = [slice(p * width + grp * GLANES, p * width + (grp + 1) * GLANES) for p in range(3)]
+            parts = [slice(grp * width + p * GLANES, grp * width + (p + 1) * GLANES) for p in range(3)]
+            lanes = slice(grp * GLANES, (grp + 1) * GLANES)
             heres = [slice(w * SLOTS, (w + 1) * SLOTS) for w in range(count)]
             q, k, v = (qkv[l, at, part].astype(F32) for part in parts)
-            go_now = go[at, parts[0]].astype(F32)
+            go_now = go[at, lanes].astype(F32)
             go_all = [expand_heads(go_now[here]) for here in heres]
             dps = [dot_nt(v[here].astype(BF16), one) for one, here in zip(go_all, heres)]
             lows = [probs[l, count * i + w, grp] for w in range(count)]
@@ -849,57 +986,26 @@
                 fold_heads(dot_tn(ds, k[here].astype(BF16))) * HEAD_DIM**-0.5 for ds, here in zip(dss, heres)
             ]
             dks = [dot(ds, expand_heads(q[here])) * HEAD_DIM**-0.5 for ds, here in zip(dss, heres)]
-            total = bias_sum[grp]
+            total = bias_sum[l, grp]
             for ds in dss:
                 total = total + ds.astype(F32)
-            bias_sum[grp] = total
+            bias_sum[l, grp] = total
             for name, part, made in zip(("query", None, "value"), parts, (dqs, dks, dvs)):
                 whole = jnp.concatenate(made, axis=0)
                 if name:
                     row = SMALL[name]
-                    small[l, row : row + 1, parts[0]] += jnp.sum(whole, axis=0, keepdims=True)
+                    small[l, row : row + 1, lanes] += jnp.sum(whole, axis=0, keepdims=True)
                 dqkv[at, part] = whole.astype(BF16)
             ticks(l, f"attend_back{grp}", i)
             return carry
 
         for grp in range(GROUPS):
             lax.fori_loop(0, 2, functools.partial(attend_back, grp=grp), 0)
-            for p in range(3):
-                lanes = slice(p * width + grp * GLANES, p * width + (grp + 1) * GLANES)
-                d_attn[l, grp * part_rows : grp * part_rows + width, p * GLANES : (p + 1) * GLANES] = dot_tn(
-                    normed[l], dqkv[:, lanes]
-                ).astype(BF16)
-            if f"A{grp}{l}" in flows:
-                advance(f"A{grp}{l}")
+            at = grp * part_rows
+            cols = slice(grp * width, (grp + 1) * width)
+            d_attn[l, at : at + width, :] = dot(turned[...], dqkv[:, cols]).astype(BF16)
+            begin(f"A{grp}{l}")
             ticks(l, f"group{grp}")
-
-        krow = iota((SLOTS, 128), 0)
-        qlane = iota((SLOTS, 128), 1)
-        ahead = (qlane & (PITCH - 1)) >= (krow & (PITCH - 1))
-        for grp in range(GROUPS):
-            low = bias_sum[grp, :, :128]
-            high = jnp.concatenate([bias_sum[grp, :, 128:], jnp.zeros((SLOTS, 256 - GQ), F32)], axis=1)
-            for j in range(GROUP):
-                h = grp * GROUP + j
-                at = j * SLOTS
-                if at + SLOTS <= 128:
-                    one = pltpu.roll(low, 128 - at, 1) if at else low
-                elif at < 128:
-                    one = jnp.where(qlane < 128 - at, pltpu.roll(low, 128 - at, 1), pltpu.roll(high, 128 - at, 1))
-                else:
-                    one = pltpu.roll(high, (256 - at) % 128, 1)
-                one = jnp.where(qlane < SLOTS, one, 0.0)
-                for s in range(2):
-                    picked = jnp.where(ahead if s == 0 else jnp.logical_not(ahead), one, 0.0)
-                    tile = picked[:PITCH]
-                    for r in range(1, WIN):
-                        tile = tile + pltpu.roll(picked[r * PITCH : (r + 1) * PITCH], 128 - r * PITCH, 1)
-                    for step in (1, 2, 4):
-                        tile = jnp.where((iota(tile.shape, 0) & step) > 0, pltpu.roll(tile, 128 - step, 1), tile)
-                    n = s * HEADS + h
-                    small[l, SMALL_TABLE + n // 3 : SMALL_TABLE + n // 3 + 1, n % 3 * 128 : (n % 3 + 1) * 128] = jnp.sum(
-                        tile, axis=0, keepdims=True
-                    )
 
         def input_back(at, l=l):
             ga = dot_nt(dqkv[at, :], w_in[l])
@@ -909,13 +1015,19 @@
             gs[at, :] = g[at, :] + dx
 
         over_blocks(input_back, (l, "input_back"))
-        advance(f"S{l}")
-        ticks(l, "input_done")
         if l == 1:
+            advance("S1")
+            ticks(l, "input_done")
             shifted_to_regular(gs, g, side)
+            ticks(l, "placed")
         else:
+            ticks(l, "input_done")
+            for one in range(2):
+                table_back(one)
+                ticks(l, f"table{one}")
+            advance("S0")
             windows_to_grid(gs, grad_tokens, side, False)
-        ticks(l, "placed")
+            ticks(l, "placed")
 
     advance(*LAST)
     while not all(flow.done for flow in flows.values()):
@@ -956,7 +1068,7 @@
     _, side, _, width = tokens.shape
     layers, _, ff = expand_weight.shape
     win, shards = mesh_shape
-    ids = jnp.broadcast_to(crop_ids[0, :, :, None], (side, side, 128))
+    ids = crop_ids.transpose(1, 0, 2)
     windows = (side // WIN) ** 2
     rows = windows * SLOTS
     attn_rows, feed_rows = 4 * width, 2 * ff
@@ -982,7 +1094,7 @@
         pltpu.VMEM((layers, shards, rows, ff), BF16),
         pltpu.VMEM((rows, 128), F32),
         pltpu.VMEM((GROUPS, SLOTS, GQ), F32),
-        pltpu.VMEM((GROUPS, SLOTS, GQ), F32),
+        pltpu.VMEM((layers, GROUPS, SLOTS, GQ), F32),
         pltpu.VMEM((rows, width), F32),
         pltpu.VMEM((rows, width), F32),
         pltpu.VMEM((rows, width), BF16),
@@ -992,7 +1104,16 @@
         pltpu.VMEM((shards, 8, ff), F32),
     ]
     small_shape = (layers, SMALL_ROWS, width)
-    scratch += [pltpu.VMEM((2, 128, 128), F32), pltpu.VMEM((2, 16, 128), F32)]
+    scratch += [
+        pltpu.VMEM((2, 128, 128), F32),
+        pltpu.VMEM((2, 16, 128), F32),
+        pltpu.VMEM(input_proj.shape, BF16),
+        pltpu.VMEM((width, rows), BF16),
+        pltpu.VMEM((128, 256), F32),
+        pltpu.VMEM((256, 128), F32),
+        pltpu.VMEM((side, 32, 128), F32),
+        pltpu.SemaphoreType.DMA((layers * GROUPS * 3,)),
+    ]
     if fused:
         plane, depth = 2 * shards, win // 4
         _, shapes = flow_table(mesh_shape, width, ff)
@@ -1003,15 +1124,17 @@
             pltpu.VMEM((shards, layers, width, ff), BF16),
             pltpu.VMEM((shards, 8, ff), F32),
             pltpu.VMEM((shards, layers, ff, width), BF16),
-            pltpu.VMEM((layers, 2) + small_shape[1:], F32),
-            pltpu.VMEM((layers, plane) + small_shape[1:], F32),
-            pltpu.VMEM((layers, depth) + small_shape[1:], F32),
+        ]
+        scratch += [
+            pltpu.VMEM((members, count, width), F32)
+            for count in (SMALL_ROWS, SMALL_EARLY)
+            for members in (2, plane, depth)
         ]
         scratch += [pltpu.VMEM(shape, BF16) for group in shapes.values() for shape in group]
         scratch += [
             pltpu.SemaphoreType.DMA((3 + len(shapes),)),
-            pltpu.SemaphoreType.DMA((160,)),
-            pltpu.SemaphoreType.DMA((160,)),
+            pltpu.SemaphoreType.DMA((256,)),
+            pltpu.SemaphoreType.DMA((256,)),
         ]
     outs = pl.pallas_call(
         functools.partial(kernel, side, mesh_shape if fused else None),
@@ -1022,7 +1145,7 @@
             jax.ShapeDtypeStruct((layers, feed_rows, width) if fused else (layers, shards, feed_rows, width), BF16),
             jax.ShapeDtypeStruct(small_shape, F32),
         ),
-        in_specs=[vmem] * 9 + ([hbm, vmem, hbm] if fused else [vmem] * 3) + [vmem] * 2,
+        in_specs=[vmem] * 4 + [hbm] + [vmem] * 4 + ([hbm, vmem, hbm] if fused else [vmem] * 3) + [vmem] * 2,
         out_specs=[vmem] * 2 + ([hbm] * 2 if fused else [vmem] * 2) + [vmem],
         scratch_shapes=scratch,
         compiler_params=pltpu.CompilerParams(
@@ -1036,7 +1159,7 @@
         norm_bias,
         input_proj,
         input_bias,
-        position_table,
+        position_table.transpose(2, 0, 1),
         output_proj,
         output_bias,
         w_exp,
@@ -1049,19 +1172,25 @@
     if not fused:
         d_attn, small = lax.psum((d_attn, small), ("win", "mlp"))
         d_feed = lax.psum(lax.psum_scatter(d_feed, "mlp", scatter_dimension=1, tiled=False), "win")
+    if fused and ff % width == 0 and width % 128 == 0 and side % 2 == 0:
+        return finish(out, grad_tokens, d_attn, d_feed, small, side, ff)
     parts = d_attn.reshape(layers, PART, attn_rows // PART, width)
     d_in = jnp.concatenate(
         [parts[:, grp, :width, p * GLANES : (p + 1) * GLANES] for p in range(3) for grp in range(GROUPS)], axis=2
     )
     d_out = parts[:, :, width:].reshape(layers, width, width)
     if ff % width == 0:
-        d_exp = jnp.concatenate([d_feed[:, c : c + width] for c in range(0, ff, width)], axis=2)
+        d_exp, d_red = (
+            jnp.concatenate([d_feed[:, c : c + width] for c in range(first, first + ff, width)], axis=2)
+            for first in (0, ff)
+        )
+        d_red = d_red.swapaxes(1, 2)
     else:
-        d_exp = d_feed[:, :ff].swapaxes(1, 2)
+        d_exp, d_red = d_feed[:, :ff].swapaxes(1, 2), d_feed[:, ff:]
     span = min(width, ff)
     d_bexp = small[:, SMALL_EXPAND : SMALL_EXPAND + shards * (ff // span), :span].reshape(layers, shards, ff)
     d_bexp = lax.dynamic_index_in_dim(d_bexp, lax.axis_index("mlp"), 1, keepdims=False)
-    d_table = small[:, SMALL_TABLE : SMALL_TABLE + 8].reshape(layers, 2 * HEADS, 128)
+    d_table = jnp.stack([small[0, SMALL_TABLE[l] : SMALL_TABLE[l] + 8] for l in range(layers)])
     return (
         out[None],
         grad_tokens[None],
@@ -1069,14 +1198,119 @@
         small[:, 2:4],
         d_in.astype(F32),
         small[:, 4:6],
-        lanes_table(d_table),
+        lanes_table(d_table.reshape(layers, 2 * HEADS, 128)),
         d_out.astype(F32),
         small[:, 6],
         d_exp.astype(F32),
         d_bexp,
-        d_feed[:, ff:].astype(F32),
+        d_red.astype(F32),
         small[:, 7],
     )
+
+
+def finish_kernel(blocks, *refs):
+    (a_in, a_out, f_exp, f_red, small, out, grad_tokens) = refs[:7]
+    (out_to, grad_to, gain, offset, d_in, b_in, table, d_out, b_out, d_exp, b_exp, d_red, b_red, tall) = refs[7:]
+    width = a_in.shape[3]
+    out_to[0] = out[...]
+    grad_to[0] = grad_tokens[...]
+    for grp in range(GROUPS):
+        for p in range(3):
+            at = p * width + grp * GLANES
+            d_in[0, :, at : at + GLANES] = a_in[0, grp, :, p * GLANES : (p + 1) * GLANES].astype(F32)
+    d_out[0] = a_out[0, 0].astype(F32)
+    for b in range(blocks):
+        cols = slice(b * width, (b + 1) * width)
+        d_exp[0, :, cols] = f_exp[0, b].astype(F32)
+        d_red[0, cols, :] = f_red[0, b].astype(F32).T
+
+    @pl.when((pl.program_id(0) == 0) & (pl.program_id(1) == 0))
+    def _():
+        for l in range(2):
+            gain[l] = small[l, 0:2, :]
+            offset[l] = small[l, 2:4, :]
+            b_in[l] = small[l, 4:6, :]
+            b_out[l : l + 1, :] = small[l, 6:7, :]
+            b_red[l : l + 1, :] = small[l, 7:8, :]
+            for b in range(blocks):
+                row = SMALL_EXPAND + lax.axis_index("mlp") * blocks + b
+                b_exp[l : l + 1, b * width : (b + 1) * width] = small[l, pl.ds(row, 1), :]
+            turned = []
+            for s in range(2):
+                heads = []
+                for h in range(HEADS):
+                    n = s * HEADS + h
+                    row = SMALL_TABLE[l] + n // 3
+                    heads.append(small[0, row : row + 1, n % 3 * 128 : (n % 3 + 1) * 128])
+                heads.append(jnp.zeros((128 - HEADS, 128), F32))
+                turned.append(jnp.concatenate(heads, axis=0).T)
+            tall[...] = jnp.zeros(tall.shape, F32)
+            for lane, entry, count, s in table_spans():
+                tall[entry : entry + count, :] = turned[s][lane : lane + count]
+            wide = tall[...].T
+            for h in range(HEADS):
+                table[h, l : l + 1, :] = wide[h : h + 1, : table.shape[2]]
+
+
+def finish(out, grad_tokens, d_attn, d_feed, small, side, ff):
+    layers, attn_rows, width = d_attn.shape
+    blocks, steps, half = ff // width, width // 128, side // 2
+    part = attn_rows // PART
+    attn = d_attn.reshape(layers, PART, part, width)
+    feed = d_feed.reshape(layers, 2 * blocks, width, width)
+    fixed = lambda *shape: pl.BlockSpec(shape, lambda l, i: (0,) * len(shape))
+    grid_in = pl.BlockSpec((half, side, width), lambda l, i: (l, 0, 0))
+    grid_out = pl.BlockSpec((1, half, side, width), lambda l, i: (0, l, 0, 0))
+    pair, row = fixed(layers, 2, width), fixed(layers, width)
+    span = SPAN_SIDE * SPAN_SIDE
+    shape = lambda *dims: jax.ShapeDtypeStruct(dims, F32)
+    grid_shape = jax.ShapeDtypeStruct((1, side, side, width), BF16)
+    made = pl.pallas_call(
+        functools.partial(finish_kernel, blocks),
+        grid=(layers, steps),
+        in_specs=[
+            pl.BlockSpec((1, PART, 128, width), lambda l, i: (l, 0, i, 0)),
+            pl.BlockSpec((1, 1, 128, width), lambda l, i: (l, i, steps, 0)),
+            pl.BlockSpec((1, blocks, 128, width), lambda l, i: (l, 0, i, 0)),
+            pl.BlockSpec((1, blocks, 128, width), lambda l, i: (l, 1, i, 0)),
+            fixed(*small.shape),
+            grid_in,
+            grid_in,
+        ],
+        out_specs=[
+            grid_out,
+            grid_out,
+            pair,
+            pair,
+            pl.BlockSpec((1, 128, 3 * width), lambda l, i: (l, i, 0)),
+            pair,
+            fixed(HEADS, layers, span),
+            pl.BlockSpec((1, 128, width), lambda l, i: (l, i, 0)),
+            row,
+            pl.BlockSpec((1, 128, ff), lambda l, i: (l, i, 0)),
+            fixed(layers, ff),
+            pl.BlockSpec((1, ff, 128), lambda l, i: (l, 0, i)),
+            row,
+        ],
+        out_shape=[
+            grid_shape,
+            grid_shape,
+            shape(layers, 2, width),
+            shape(layers, 2, width),
+            shape(layers, width, 3 * width),
+            shape(layers, 2, width),
+            shape(HEADS, layers, span),
+            shape(layers, width, width),
+            shape(layers, width),
+            shape(layers, width, ff),
+            shape(layers, ff),
+            shape(layers, ff, width),
+            shape(layers, width),
+        ],
+        scratch_shapes=[pltpu.VMEM((256, 128), F32)],
+        compiler_params=pltpu.CompilerParams(vmem_limit_bytes=64 * 1024 * 1024),
+    )(attn, attn, feed, feed, small, out, grad_tokens)
+    return (*made[:6], made[6].transpose(1, 2, 0), *made[7:])
 
 
 def solution(mesh):

time: 161 us -> 140 us (0.87)
  local copies, waits for them, and re-layouts: 14.1 us -> 0 us
  other arithmetic: 6.5 us -> 0 us
    pallas_call x1, Pallas kernels: 139 us -> 130 us  [on_device(): pl.pallas_call(functools.partial(kernel, side, mesh_shape if fused else N...]
    pallas_call x0 -> x1, Pallas kernels: none -> 8.46 us  [finish(): pl.pallas_call(functools.partial(finish_kernel, blocks), grid=(layers, st...]
    unnamed x22 -> x0, local copies, waits for them, and re-layouts: 6.96 us -> none
    convert_element_type x4 -> x0, other arithmetic: 6.3 us -> none  [the longest x1 2.02 us: on_device(): d_in.astype(F32)]
    slice x11 -> x0, local copies, waits for them, and re-layouts: 5.38 us -> none  [the longest x1 1.46 us: on_device(): small[:, 4:6]]
where the time goes in v4:
time: 140 us; the launch traced here: 139 us
  Pallas kernels  138 us (99%)
    pallas_call x1, Pallas kernels, on_device(): pl.pallas_call(functools.partial(kernel, side, mesh_shape if fused else N...  130 us
    pallas_call x1, Pallas kernels, finish(): pl.pallas_call(functools.partial(finish_kernel, blocks), grid=(layers, st...  8.46 us

profile of v4, /device:TPU:0, one launch (start us, length us, event | category | flops | bytes accessed | tf_op | source)
XLA Modules:
  0.0 139.3 jit_solution(4554742336226048980)
XLA Ops:
  0.7 130.0 %shard_map.237 = (bf16[28,28,384]{2,1,0:T(8,128)(2,1)}, bf16[28,28,384]{2,1,0:T(8,128)(2,1)}, bf16[2,1536,384]{2,1,0:T(8,128)(2,1)}, bf16[2,1536,384]{2,1,0:T(8,128)(2,1)}, f32[2,32,384]{2,1,0:T(8,128)}) custom-call(bf16[28,28,384]{2,1,0:T(8,128)(2,1)} %bitcast.11, s32[28,1,28]{2,1,0:T(1,128)} %bitcast.14, f32[2,2,384]{2,1,0:T(2,128)} %refs_2_.1, ...), custom_call_target="tpu_custom_call" | custom-call | tf_op jit(solution)/shard_map/pallas_call | solution.py:1139
  130.6 8.5 %shard_map.238 = (bf16[1,28,28,384]{3,2,1,0:T(8,128)(2,1)}, bf16[1,28,28,384]{3,2,1,0:T(8,128)(2,1)}, f32[2,2,384]{2,1,0:T(2,128)}, f32[2,2,384]{2,1,0:T(2,128)}...) custom-call(bf16[2,3,512,384]{3,2,1,0:T(8,128)(2,1)} %bitcast.7, ...), custom_call_target="tpu_custom_call" | custom-call | tf_op jit(solution)/shard_map/pallas_call | solution.py:1268
